TPU v7x, 128 devices: a whole 4x4x4 slice. The times are simulated.
128 devices in a mesh: pool: 16 (over x, y), grp: 8 (over z, core).
Axes of the slice: x: 4, y: 4, z: 4, core: 2. Of those that a mesh axis runs over, the one named last changes fastest.
Arguments:
- queries: bfloat16 [256, 4096], P(('pool', 'grp')), may hold values from -6 to 6
- key_cache: bfloat16 [256, 1024, 256], P(('pool', 'grp')), may hold values from -8 to 8
- value_cache: bfloat16 [256, 1024, 256], P(('pool', 'grp')), may hold values from -24 to 24
- lengths: int32 [256], P(('pool', 'grp')), may hold values from 128 to 1024, as said below
- residual: bfloat16 [256, 4096], P('pool', 'grp'), may hold values from -6 to 6
- out_proj: bfloat16 [4096, 4096], P(None, 'grp'), may hold values from -0.09375 to 0.09375
- norm_gain: float32 [4096], P('grp'), may hold values from 0.1 to 1.9
- expert_ids: int32 [256, 8], P('pool'), may hold values from 0 to 63, all different within a row; in each aligned block of 16 rows (0 to 15, 16 to 31, ...) at most 4 rows name the same one
- route_weights: float32 [256, 8], P('pool'), may hold values from 0.05 to 1
- w_gate: bfloat16 [64, 4096, 1536], P('pool', None, 'grp'), may hold values from -0.09375 to 0.09375
- w_up: bfloat16 [64, 4096, 1536], P('pool', None, 'grp'), may hold values from -0.09375 to 0.09375
- w_down: bfloat16 [64, 1536, 4096], P('pool', 'grp'), may hold values from -0.15625 to 0.15625
Outputs:
- layer_out: bfloat16 [256, 4096], P('pool', 'grp')
Inputs may be any that keep to these rules, and one draw needn't show every extreme that they name: `expert_ids`: among the 16 rows of one index of pool (aligned blocks of rows) no expert is named by more than 4 routes; a row names 8 different experts. `lengths`: some row has exactly 1024 and some row exactly 128.
All inputs are finite; a program needn't handle non-finite values.
Results may differ from a plain program's by a relative error of at most 0.018.
Values may be sent and summed in bfloat16 or wider, within the bound.
No kernel may reach another device: no remote copies, remote signals or barrier semaphores. Data moves between devices by JAX's collectives and lax.ppermute only.
A program may use at most 128 MiB of HBM per device.

v0:
```python
import math

import jax
import jax.numpy as jnp
from jax import lax
from jax.sharding import PartitionSpec as P

D = 4096
KV_HEADS = 2
HEAD = 128
CAP = 4


def route_targets(ids, n_experts):
    flat_ids = ids.reshape(-1)
    onehot = (flat_ids[:, None] == jnp.arange(n_experts, dtype=jnp.int32)[None, :]).astype(
        jnp.int32
    )
    earlier = jnp.cumsum(onehot, axis=0) - onehot
    slot_index = jnp.sum(earlier * onehot, axis=1)
    return flat_ids * CAP + slot_index


def on_device(
    queries,
    key_cache,
    value_cache,
    lengths,
    residual,
    out_proj,
    norm_gain,
    expert_ids,
    route_weights,
    w_gate,
    w_up,
    w_down,
):
    local_rows = queries.shape[0]
    per_group = queries.shape[1] // (KV_HEADS * HEAD)
    positions = key_cache.shape[1]
    query_heads = queries.reshape(local_rows, KV_HEADS, per_group, HEAD)
    key_heads = key_cache.reshape(local_rows, positions, KV_HEADS, HEAD)
    value_heads = value_cache.reshape(local_rows, positions, KV_HEADS, HEAD).astype(jnp.float32)
    scores = jnp.einsum(
        "rkhd,rpkd->rkhp", query_heads, key_heads, preferred_element_type=jnp.float32
    ) / math.sqrt(HEAD)
    live_mask = (jnp.arange(positions, dtype=jnp.int32)[None, :] < lengths[:, None])[
        :, None, None, :
    ]
    peak = jnp.max(jnp.where(live_mask, scores, -1e30), axis=3)
    probs = jnp.where(live_mask, jnp.exp(scores - peak[..., None]), 0.0)
    weight_sum = jnp.sum(probs, axis=3)
    summed = jnp.einsum("rkhp,rpkd->rkhd", probs, value_heads, precision=lax.Precision.HIGHEST)
    attended = (summed / weight_sum[..., None]).reshape(local_rows, -1).astype(jnp.bfloat16)
    attended_all = lax.all_gather(attended, "grp", axis=0, tiled=True)
    stream = (
        residual.astype(jnp.float32)
        + jnp.dot(attended_all, out_proj, preferred_element_type=jnp.float32)
    ).astype(jnp.bfloat16)
    widened = stream.astype(jnp.float32)
    squares = lax.psum(jnp.sum(widened * widened, axis=1), "grp")
    moe_in = (widened * lax.rsqrt(squares / D + 1e-06)[:, None] * norm_gain[None, :]).astype(
        jnp.bfloat16
    )
    pool_count = lax.axis_size("pool")
    local_experts = w_gate.shape[0]
    n_experts = local_experts * pool_count
    block_rows = expert_ids.shape[0]
    top_count = expert_ids.shape[1]
    targets = route_targets(expert_ids, n_experts)
    slot_numbers = jnp.arange(n_experts * CAP, dtype=jnp.int32)
    picks = (
        (targets[:, None] == slot_numbers[None, :])
        .astype(jnp.float32)
        .reshape(block_rows, top_count, -1)
    )
    placing = jnp.sum(picks, axis=1).astype(jnp.bfloat16)
    mixing = jnp.sum(picks * route_weights[:, :, None], axis=1)
    full_rows = lax.all_gather(moe_in, "grp", axis=1, tiled=True)
    outgoing = jnp.einsum(
        "rj,rd->jd", placing, full_rows, preferred_element_type=jnp.float32
    ).astype(jnp.bfloat16)
    outgoing = outgoing.reshape(pool_count, local_experts, CAP, -1)
    received = lax.all_to_all(outgoing, "pool", split_axis=0, concat_axis=0, tiled=True)
    gate_act = jnp.einsum("secd,edf->secf", received, w_gate, preferred_element_type=jnp.float32)
    up_act = jnp.einsum("secd,edf->secf", received, w_up, preferred_element_type=jnp.float32)
    hidden = (jax.nn.silu(gate_act) * up_act).astype(jnp.bfloat16)
    partial_out = jnp.einsum("secf,efd->secd", hidden, w_down, preferred_element_type=jnp.float32)
    returned = lax.all_to_all(
        partial_out.astype(jnp.bfloat16), "pool", split_axis=0, concat_axis=0, tiled=True
    ).astype(partial_out.dtype)
    weighted = jnp.dot(
        mixing, returned.reshape(n_experts * CAP, -1), precision=lax.Precision.HIGHEST
    )
    combined = lax.psum_scatter(
        weighted.astype(jnp.bfloat16), "grp", scatter_dimension=1, tiled=True
    ).astype(jnp.float32)
    return (widened + combined).astype(jnp.bfloat16)


def solution(mesh):
    in_specs = (
        P(("pool", "grp"), None),
        P(("pool", "grp"), None, None),
        P(("pool", "grp"), None, None),
        P(("pool", "grp")),
        P("pool", "grp"),
        P(None, "grp"),
        P("grp"),
        P("pool", None),
        P("pool", None),
        P("pool", None, "grp"),
        P("pool", None, "grp"),
        P("pool", "grp", None),
    )
    out_specs = P("pool", "grp")
    return jax.shard_map(
        on_device, mesh=mesh, in_specs=in_specs, out_specs=out_specs, check_vma=False
    )
```

profile of v0, /device:TPU:0, one launch (start us, length us, event | category | flops | bytes accessed | tf_op | source)
XLA Modules:
  0.0 185.1 jit_solution(7415568069888519756)
XLA Ops:
  6.5 0.0 copy-start
  6.5 0.0 copy-start.1
  6.5 0.0 reduce-scatter.2.cloned.1.call-start
  6.5 0.8 iota_compare_fusion.2
  7.4 0.8 copy.36
  8.1 0.1 eq.29
  8.2 0.8 copy.38
  9.0 0.7 copy.47
  9.7 0.1 fusion.55
  9.8 0.2 reduce_window_sum.11
  9.9 0.2 select_reduce_fusion.2
  10.1 0.1 reduce_sum.49
  10.2 0.0 copy-done
  10.2 0.5 select_reduce_fusion
  10.7 0.2 fusion.50
  10.9 1.8 fusion.34
  12.8 14.0 %all-gather = bf16[8,2,4096]{2,1,0:T(2,128)(2,1)S(1)} all-gather(bf16[1,2,4096]{2,1,0:T(2,128)(2,1)S(1)} %reshape.63), channel_id=1, replica_groups=mesh['pool'=16,'grp'=8] {'grp'}, dimensions={0}, use_global_device_ids=true | all-gather | bytes 147456 | tf_op jit(solution)/shard_map/all_gather | solution.py:55
  26.8 0.1 reshape.64
  26.9 0.0 copy-done.1
  26.9 0.0 copy-start.2
  26.9 3.0 %multiply_reduce_fusion = (f32[16]{0:T(128)S(1)}, f32[16,512]{1,0:T(8,128)S(1)}) fusion(bf16[16,4096]{1,0:T(8,128)(2,1)S(1)} %reshape.64, bf16[4096,512]{1,0:T(8,128)(2,1)} %param.17, bf16[16,512]{1,0:T(8,128)(2,1)S(1)} %copy-done.1), kind=kOutput, calls=%fused_computation.46 | convolution fusion | flops 67158000 | bytes 4374592 | tf_op jit(solution)/shard_map/dot_general | solution.py:58
  29.8 15.2 %psum.7 = f32[16]{0:T(128)S(1)} all-reduce(f32[16]{0:T(128)S(1)} %get-tuple-element.9), channel_id=1, replica_groups=mesh['pool'=16,'grp'=8] {'grp'}, use_global_device_ids=true, to_apply=%region_7.8 | all-reduce | flops 16 | bytes 128 | tf_op jit(solution)/shard_map/psum | solution.py:61
  45.0 0.0 copy-done.2
  45.0 0.1 multiply_convert_fusion
  45.1 12.8 %all_gather.7 = bf16[16,4096]{1,0:T(8,128)(2,1)S(1)} all-gather(bf16[16,512]{1,0:T(8,128)(2,1)S(1)} %multiply_convert_fusion), channel_id=1, replica_groups=mesh['pool'=16,'grp'=8] {'grp'}, dimensions={1}, use_global_device_ids=true | all-gather | bytes 147456 | tf_op jit(solution)/shard_map/all_gather | solution.py:79
  57.9 0.1 convert_reduce_fusion
  58.0 0.7 convolution_convert_fusion
  58.8 2.2 %reshape.61 = bf16[16,4,4,4096]{3,2,1,0:T(4,128)(2,1)} reshape(bf16[256,4096]{1,0:T(8,128)(2,1)S(1)} %convolution_convert_fusion) | data formatting | bytes 4194304 | tf_op jit(solution)/shard_map/reshape | solution.py:83
  61.0 35.9 %all_to_all.10 = bf16[16,4,4,4096]{3,2,1,0:T(4,128)(2,1)S(1)} all-to-all(bf16[16,4,4,4096]{3,2,1,0:T(4,128)(2,1)} %reshape.61), channel_id=1, replica_groups=mesh['pool'=16,'grp'=8] {'pool'}, dimensions={0} | all-to-all | bytes 4194304 | tf_op jit(solution)/shard_map/all_to_all | solution.py:84
  96.9 5.2 %fusion.14 = f32[16,4,4,192]{3,0,2,1:T(8,128)S(1)} fusion(bf16[4,4096,192]{1,2,0:T(8,128)(2,1)} %param.21, bf16[16,4,4,4096]{3,2,1,0:T(4,128)(2,1)S(1)} %all_to_all.10), kind=kOutput, calls=%fused_computation.13 | convolution fusion | flops 402653184 | bytes 8585216 | tf_op jit(solution)/shard_map/secd,edf->secf/dot_general | solution.py:85
  102.1 9.6 %fusion.9 = bf16[16,4,4,4096]{3,0,2,1:T(8,128)(2,1)} fusion(bf16[4,192,4096]{2,1,0:T(8,128)(2,1)} %param.23, bf16[4,4096,192]{1,2,0:T(8,128)(2,1)} %param.22, bf16[16,4,4,4096]{3,2,1,0:T(4,128)(2,1)S(1)} %all_to_all.10, f32[16,4,4,192]{3,0,2,1:T(8,128)S(1)} %fusion.14), kind=kOutput, calls=%fused_computation.8 | convolution fusion | flops 806649856 | bytes 16973824 | tf_op jit(solution)/shard_map/secf,efd->secd/dot_general | solution.py:88
  111.7 3.2 %copy.41 = bf16[16,4,4,4096]{3,2,1,0:T(4,128)(2,1)S(1)} copy(bf16[16,4,4,4096]{3,0,2,1:T(8,128)(2,1)} %fusion.9) | data formatting | bytes 4194304 | tf_op jit(solution)/shard_map/convert_element_type | solution.py:90
  114.9 31.1 %all_to_all.11 = bf16[16,4,4,4096]{3,2,1,0:T(4,128)(2,1)} all-to-all(bf16[16,4,4,4096]{3,2,1,0:T(4,128)(2,1)S(1)} %copy.41), channel_id=1, replica_groups=mesh['pool'=16,'grp'=8] {'pool'}, dimensions={0} | all-to-all | bytes 4194304 | tf_op jit(solution)/shard_map/all_to_all | solution.py:89
  146.0 2.5 %reshape.62 = bf16[256,4096]{1,0:T(8,128)(2,1)S(1)} reshape(bf16[16,4,4,4096]{3,2,1,0:T(4,128)(2,1)} %all_to_all.11) | data formatting | bytes 4194304 | tf_op jit(solution)/shard_map/reshape | solution.py:93
  148.5 1.6 convolution_convert_fusion.1
  150.1 0.0 reduce-scatter.2.cloned.1.call-update
  150.1 26.8 %reduce-scatter.2.cloned.1.call-done = bf16[16,512]{1,0:T(8,128)(2,1)} async-done(((bf16[16,4096]{1,0:T(8,128)(2,1)}), bf16[16,512]{1,0:T(8,128)(2,1)}) %reduce-scatter.2.cloned.1.call-update) | async-done | bytes 16400 | tf_op jit(solution)/shard_map/reduce_scatter | solution.py:95
  176.9 1.3 add_convert_fusion
  (3 shorter events, 0.0 us)
Async XLA Ops:
  6.5 3.7 %copy-start = (bf16[2,1024,256]{2,1,0:T(8,128)(2,1)S(1)}, bf16[2,1024,256]{2,1,0:T(8,128)(2,1)}, u32[]{:S(2)}) copy-start(bf16[2,1024,256]{2,1,0:T(8,128)(2,1)} %param.13) | copy-start | bytes 3145732
  6.5 20.3 %copy-start.1 = (bf16[16,512]{1,0:T(8,128)(2,1)S(1)}, bf16[16,512]{1,0:T(8,128)(2,1)}, u32[]{:S(2)}) copy-start(bf16[16,512]{1,0:T(8,128)(2,1)} %param.16) | copy-start | bytes 49156
  6.5 170.4 %reduce-scatter.2.cloned.1.call-start = ((), (), s32[]{:S(2)}) async-start(), calls=%async_computation.3 | async-start | bytes 147456 | tf_op jit(solution)/shard_map/reduce_scatter | solution.py:95
  26.9 18.2 %copy-start.2 = (f32[512]{0:T(512)S(1)}, f32[512]{0:T(512)}, u32[]{:S(2)}) copy-start(f32[512]{0:T(512)} %param.18) | copy-start | bytes 6148
Sparse Core Ops, SparseCore 0:
  150.2 26.6 reduce-scatter.1
where the time goes:
time: 186 us; the launch traced here: 185 us
  blocking collectives  109 us (59%)
  waiting for transfers between devices  26.8 us (14%)
  matrix products  22.3 us (12%)
  between operations  13.5 us (7%)
  local copies, waits for them, and re-layouts  10.5 us (6%)
  other arithmetic  3.02 us (2%)
    all_to_all x1, blocking collectives, on_device(): lax.all_to_all(outgoing, 'pool', split_axis=0, concat_axis=0, tiled=True)  35.9 us
    all_to_all x1, blocking collectives, on_device(): lax.all_to_all(partial_out.astype(jnp.bfloat16), 'pool', split_axis=0, co...  31.1 us
    reduce_scatter x1, waiting for transfers between devices, on_device(): lax.psum_scatter(weighted.astype(jnp.bfloat16), 'grp', scatter_dimension=...  26.8 us
    psum x1, blocking collectives, on_device(): squares = lax.psum(jnp.sum(widened * widened, axis=1), 'grp')  15.2 us
    all_gather x1, blocking collectives, on_device(): attended_all = lax.all_gather(attended, 'grp', axis=0, tiled=True)  14 us
    all_gather x1, blocking collectives, on_device(): full_rows = lax.all_gather(moe_in, 'grp', axis=1, tiled=True)  12.8 us
    dot_general x1, matrix products, on_device(): jnp.einsum('secf,efd->secd', hidden, w_down, preferred_element_type=jnp.f...  9.59 us
    dot_general x1, matrix products, on_device(): jnp.einsum('secd,edf->secf', received, w_gate, preferred_element_type=jnp...  5.22 us
  transfers between devices with their start and end apart: 1, of which 1 were waited for; matrix products, arithmetic and copies ran while one was open for 0% of the time, Pallas kernels for 0%

commit v1 on v0

v1 whole, which is shorter than its diff:
```python
import functools
import math

import jax
import jax.numpy as jnp
from jax import lax
from jax.experimental import pallas as pl
from jax.experimental.pallas import tpu as pltpu
from jax.sharding import PartitionSpec as P

D = 4096
KV_HEADS = 2
HEAD = 128
SIDE = 4
CORES = 2
COLS = D // (SIDE * CORES)
EXTRA = 128
IDS, HI, MID, LO, SQ = 0, 8, 16, 24, 32
F32 = jnp.float32
BF16 = jnp.bfloat16
NT = (((1,), (1,)), ((), ()))
VMEM = pl.BlockSpec(memory_space=pltpu.VMEM)
SMEM = pl.BlockSpec(memory_space=pltpu.SMEM)


def params(mib):
    return pltpu.CompilerParams(vmem_limit_bytes=mib * 1024 * 1024)


def split3(value):
    hi = value.astype(BF16).astype(F32)
    mid = (value - hi).astype(BF16).astype(F32)
    lo = value - hi - mid
    return hi, mid, lo


def shift_x(k):
    return [(x * SIDE + y, (x + k) % SIDE * SIDE + y) for x in range(SIDE) for y in range(SIDE)]


def shift_y(k):
    return [(x * SIDE + y, x * SIDE + (y + k) % SIDE) for x in range(SIDE) for y in range(SIDE)]


def shift_z(k):
    return [(z * CORES + c, (z + k) % SIDE * CORES + c) for z in range(SIDE) for c in range(CORES)]


OTHER_CORE = [(z * CORES + c, z * CORES + 1 - c) for z in range(SIDE) for c in range(CORES)]


def spread(block, axis, shift):
    return [block] + [lax.ppermute(block, axis, shift(k)) for k in range(1, SIDE)]


def give_back(blocks, axis, shift):
    return [blocks[0]] + [lax.ppermute(blocks[k], axis, shift(-k)) for k in range(1, SIDE)]


def attention_kernel(len_ref, q_ref, k_ref, v_ref, out_ref, q_rows, out_rows):
    rows = q_ref.shape[0]
    positions = k_ref.shape[1]
    heads = q_ref.shape[1] // HEAD
    per_group = heads // KV_HEADS
    queries = q_ref[...].astype(F32)
    for r in range(rows):
        for h in range(heads):
            q_rows[r * heads + h : r * heads + h + 1, :] = queries[
                r : r + 1, h * HEAD : (h + 1) * HEAD
            ]
    spots = lax.broadcasted_iota(jnp.int32, (per_group, positions), 1)
    for r in range(rows):
        live = spots < len_ref[r]
        for g in range(KV_HEADS):
            first = r * heads + g * per_group
            q = q_rows[first : first + per_group, :].astype(BF16)
            keys = k_ref[r, :, g * HEAD : (g + 1) * HEAD]
            scores = lax.dot_general(q, keys, NT, preferred_element_type=F32) / math.sqrt(HEAD)
            scores = jnp.where(live, scores, -1e30)
            peak = jnp.max(scores, axis=1, keepdims=True)
            probs = jnp.where(live, jnp.exp(scores - peak), 0.0)
            weight_sum = jnp.sum(probs, axis=1, keepdims=True)
            values = v_ref[r, :, g * HEAD : (g + 1) * HEAD]
            summed = jnp.dot(probs.astype(BF16), values, preferred_element_type=F32)
            summed = summed / weight_sum
            for j in range(per_group):
                h = g * per_group + j
                out_rows[r : r + 1, h * HEAD : (h + 1) * HEAD] = summed[j : j + 1, :]
    out_ref[...] = out_rows[...].astype(BF16)


def attention(lengths, queries, keys, values):
    rows, width = queries.shape
    return pl.pallas_call(
        attention_kernel,
        out_shape=jax.ShapeDtypeStruct((rows, width), BF16),
        in_specs=[SMEM, VMEM, VMEM, VMEM],
        out_specs=VMEM,
        scratch_shapes=[
            pltpu.VMEM((rows * width // HEAD, HEAD), F32),
            pltpu.VMEM((rows, width), F32),
        ],
        compiler_params=params(16),
        name="attention",
    )(lengths, queries, keys, values)


def routes_kernel(ids_ref, weights_ref, out_ref):
    top = ids_ref.shape[0]
    lane = lax.broadcasted_iota(jnp.int32, (top, EXTRA), 1)
    slot = lax.broadcasted_iota(jnp.int32, (top, EXTRA), 0)
    hi, mid, lo = split3(weights_ref[...])
    total = None
    for piece, start in ((ids_ref[...].astype(F32), IDS), (hi, HI), (mid, MID), (lo, LO)):
        place = (lane == slot + start).astype(BF16)
        part = lax.dot_general(
            piece.astype(BF16), place, (((0,), (0,)), ((), ())), preferred_element_type=F32
        )
        total = part if total is None else total + part
    out_ref[...] = total.astype(BF16)


def routes(ids, weights):
    return pl.pallas_call(
        routes_kernel,
        out_shape=jax.ShapeDtypeStruct((ids.shape[1], EXTRA), BF16),
        in_specs=[VMEM, VMEM],
        out_specs=VMEM,
        name="routes",
    )(ids, weights)


def with_squares(extra, squares):
    lane = lax.broadcasted_iota(jnp.int32, extra.shape, 1)
    for i, piece in enumerate(split3(squares)):
        extra = jnp.where(lane == SQ + i, piece, extra)
    return extra


def squares_of(extra):
    lane = lax.broadcasted_iota(jnp.int32, extra.shape, 1)
    return jnp.sum(
        jnp.where((lane >= SQ) & (lane < SQ + 3), extra, 0.0), axis=1, keepdims=True
    )


def stream_kernel(
    a0, a1, a2, a3, w_ref, residual_ref, gain_ref, extra_ref, stream_ref, unit_ref, rows_ref
):
    part = a0.shape[0]
    for k, a in enumerate((a0, a1, a2, a3)):
        rows_ref[k * part : (k + 1) * part, :] = a[...].astype(F32)
    mixed = jnp.dot(rows_ref[...].astype(BF16), w_ref[...], preferred_element_type=F32)
    rows = SIDE * part
    half = part // CORES
    me = lax.axis_index("grp")
    z, c = me // CORES, me % CORES
    here = lax.broadcasted_iota(jnp.int32, (rows, rows), 1)
    wanted = lax.broadcasted_iota(jnp.int32, (rows, rows), 0)
    slot, within = here // part, here % part
    owner = (z - slot + SIDE) % SIDE * CORES + (c + within // half) % CORES
    order = (wanted == owner * half + within % half).astype(F32)
    mixed = jnp.dot(order, mixed, precision=lax.Precision.HIGHEST, preferred_element_type=F32)
    stream = (residual_ref[...].astype(F32) + mixed).astype(BF16)
    stream_ref[...] = stream
    widened = stream.astype(F32)
    unit_ref[:, :COLS] = (widened * gain_ref[...]).astype(BF16)
    squares = jnp.sum(widened * widened, axis=1, keepdims=True)
    unit_ref[:, COLS:] = with_squares(extra_ref[...].astype(F32), squares).astype(BF16)


def make_stream(parts, out_proj, residual, gain, extra):
    rows = residual.shape[0]
    return pl.pallas_call(
        stream_kernel,
        out_shape=[
            jax.ShapeDtypeStruct((rows, COLS), BF16),
            jax.ShapeDtypeStruct((rows, COLS + EXTRA), BF16),
        ],
        in_specs=[VMEM] * 8,
        out_specs=[VMEM, VMEM],
        scratch_shapes=[pltpu.VMEM((rows, D), F32)],
        compiler_params=params(16),
        name="stream",
    )(*parts, out_proj, residual, gain, extra)


def pack_kernel(u0, u1, u2, u3, out_ref):
    squares = None
    for k, unit in enumerate((u0, u1, u2, u3)):
        out_ref[:, k * COLS : (k + 1) * COLS] = unit[:, :COLS]
        part = squares_of(unit[:, COLS:].astype(F32))
        squares = part if squares is None else squares + part
    out_ref[:, SIDE * COLS :] = with_squares(u0[:, COLS:].astype(F32), squares).astype(BF16)


def pack(units):
    return pl.pallas_call(
        pack_kernel,
        out_shape=jax.ShapeDtypeStruct((units[0].shape[0], SIDE * COLS + EXTRA), BF16),
        in_specs=[VMEM] * SIDE,
        out_specs=VMEM,
        name="pack",
    )(*units)


def column_block(z, k, c):
    return pl.ds(pl.multiple_of(((z - k + SIDE) % SIDE * CORES + c) * COLS, COLS), COLS)


def experts_kernel(
    o0, o1, o2, o3, t0, t1, t2, t3, gate_ref, up_ref, down_ref, hidden_ref, out_ref, x_ref
):
    me = lax.axis_index("grp")
    z, c = me // CORES, me % CORES
    first = lax.axis_index("pool") * (gate_ref.shape[0] // EXPERT_COLS)
    rows = o0.shape[0]
    scales = []
    mixes = []
    for kx, (own, other) in enumerate(((o0, t0), (o1, t1), (o2, t2), (o3, t3))):
        for k in range(SIDE):
            for half, parity in ((own, c), (other, 1 - c)):
                x_ref[kx * rows : (kx + 1) * rows, column_block(z, k, parity)] = half[
                    :, k * COLS : (k + 1) * COLS
                ]
        extra = own[:, SIDE * COLS :].astype(F32)
        squares = squares_of(extra) + squares_of(other[:, SIDE * COLS :].astype(F32))
        scales.append(lax.rsqrt(squares / D + 1e-06))
        lane = lax.broadcasted_iota(jnp.int32, extra.shape, 1)
        weights = (
            pltpu.roll(extra, EXTRA - HI, 1)
            + pltpu.roll(extra, EXTRA - MID, 1)
            + pltpu.roll(extra, EXTRA - LO, 1)
        )
        picked = []
        for e in range(gate_ref.shape[0] // EXPERT_COLS):
            mine = (lane < HI) & (extra == (first + e).astype(F32))
            picked.append(jnp.sum(jnp.where(mine, weights, 0.0), axis=1, keepdims=True))
        mixes.append(picked)
    scale = jnp.concatenate(scales, axis=0)
    x = x_ref[...]
    gate = lax.dot_general(x, gate_ref[...], NT, preferred_element_type=F32) * scale
    up = lax.dot_general(x, up_ref[...], NT, preferred_element_type=F32) * scale
    column = lax.broadcasted_iota(jnp.int32, gate.shape, 1)
    mix = None
    for e in range(len(mixes[0])):
        one = jnp.concatenate([m[e] for m in mixes], axis=0)
        mix = one if mix is None else jnp.where(column < e * EXPERT_COLS, mix, one)
    hidden = (gate / (1.0 + jnp.exp(-gate)) * up * mix).astype(BF16)
    hidden_ref[...] = hidden
    for k in range(SIDE):
        out_ref[:, k * COLS : (k + 1) * COLS] = jnp.dot(
            hidden, down_ref[:, column_block(z, k, 1 - c)], preferred_element_type=F32
        ).astype(BF16)


EXPERT_COLS = 192


def experts(own, other, gate, up, down):
    rows = SIDE * own[0].shape[0]
    width = gate.shape[0]
    return pl.pallas_call(
        experts_kernel,
        out_shape=[
            jax.ShapeDtypeStruct((rows, width), BF16),
            jax.ShapeDtypeStruct((rows, SIDE * COLS), BF16),
        ],
        in_specs=[VMEM] * 11,
        out_specs=[VMEM, VMEM],
        scratch_shapes=[pltpu.VMEM((rows, D), BF16)],
        compiler_params=params(20),
        cost_estimate=pl.CostEstimate(
            flops=5 * rows * width * D, bytes_accessed=6 * width * D, transcendentals=rows * width
        ),
        name="experts",
    )(*own, *other, gate, up, down)


def down_kernel(hidden_ref, down_ref, out_ref):
    me = lax.axis_index("grp")
    z, c = me // CORES, me % CORES
    for k in range(SIDE):
        out_ref[:, k * COLS : (k + 1) * COLS] = jnp.dot(
            hidden_ref[...], down_ref[:, column_block(z, k, c)], preferred_element_type=F32
        ).astype(BF16)


def down_own(hidden, down):
    rows, width = hidden.shape
    return pl.pallas_call(
        down_kernel,
        out_shape=jax.ShapeDtypeStruct((rows, SIDE * COLS), BF16),
        in_specs=[VMEM, VMEM],
        out_specs=VMEM,
        compiler_params=params(20),
        cost_estimate=pl.CostEstimate(
            flops=rows * width * D, bytes_accessed=2 * width * D, transcendentals=0
        ),
        name="down_own",
    )(hidden, down)


def on_device(
    queries,
    key_cache,
    value_cache,
    lengths,
    residual,
    out_proj,
    norm_gain,
    expert_ids,
    route_weights,
    w_gate,
    w_up,
    w_down,
):
    gate = jnp.swapaxes(w_gate, 1, 2).reshape(-1, D)
    up = jnp.swapaxes(w_up, 1, 2).reshape(-1, D)
    down = w_down.reshape(-1, D)
    gate, up, down, out_proj = (
        pltpu.with_memory_space_constraint(w, pltpu.VMEM) for w in (gate, up, down, out_proj)
    )
    extra = routes(expert_ids.T, route_weights.T)
    attended = attention(lengths, queries, key_cache, value_cache)
    pair = jnp.concatenate([attended, lax.ppermute(attended, "grp", OTHER_CORE)], axis=0)
    parts = spread(pair, "grp", shift_z)
    stream, unit = make_stream(parts, out_proj, residual, norm_gain[None, :], extra)
    column = pack(spread(unit, "grp", shift_z))
    plane = jnp.concatenate(spread(column, "pool", shift_y), axis=0)
    own = spread(plane, "pool", shift_x)
    other = [lax.ppermute(block, "grp", OTHER_CORE) for block in own]
    hidden, theirs = experts(own, other, gate, up, down)
    came = lax.ppermute(theirs, "grp", OTHER_CORE)
    mine = down_own(hidden, down)
    total = (mine.astype(F32) + came.astype(F32)).astype(BF16)
    for axis, shift in (("pool", shift_x), ("pool", shift_y)):
        slots = give_back(jnp.split(total, SIDE, axis=0), axis, shift)
        total = sum(s.astype(F32) for s in slots).astype(BF16)
    slots = give_back(jnp.split(total, SIDE, axis=1), "grp", shift_z)
    combined = sum(s.astype(F32) for s in slots)
    return (stream.astype(F32) + combined).astype(BF16)


def solution(mesh):
    in_specs = (
        P(("pool", "grp"), None),
        P(("pool", "grp"), None, None),
        P(("pool", "grp"), None, None),
        P(("pool", "grp")),
        P("pool", "grp"),
        P(None, "grp"),
        P("grp"),
        P("pool", None),
        P("pool", None),
        P("pool", None, "grp"),
        P("pool", None, "grp"),
        P("pool", "grp", None),
    )
    return jax.shard_map(
        on_device, mesh=mesh, in_specs=in_specs, out_specs=P("pool", "grp"), check_vma=False
    )
```

time: 186 us -> 106 us (0.57)
  blocking collectives: 109 us -> 0 us
  starting transfers between devices: 0.01 us -> 28.1 us
  matrix products: 22.3 us -> 0 us
  waiting for transfers between devices: 26.8 us -> 47.1 us
  between operations: 13.5 us -> 0.14 us
  Pallas kernels: 0 us -> 11.3 us
  local copies, waits for them, and re-layouts: 10.5 us -> 17.1 us
    all_to_all x2 -> x0, blocking collectives: 67 us -> none  [the longest x1 35.9 us: on_device(): lax.all_to_all(outgoing, 'pool', split_axis=0, concat_axis=0, tiled=True)]
    ppermute x0 -> x27, waiting for transfers between devices: none -> 47.1 us  [the longest x12 21.5 us: spread(): lax.ppermute(block, axis, shift(k))]
    ppermute x0 -> x27, starting transfers between devices: none -> 28.1 us  [the longest x12 18 us: spread(): lax.ppermute(block, axis, shift(k))]
    reduce_scatter x1 -> x0, waiting for transfers between devices: 26.8 us -> none  [on_device(): lax.psum_scatter(weighted.astype(jnp.bfloat16), 'grp', scatter_dimension=...]
    all_gather x2 -> x0, blocking collectives: 26.8 us -> none  [the longest x1 14 us: on_device(): attended_all = lax.all_gather(attended, 'grp', axis=0, tiled=True)]
    dot_general x7 -> x0, matrix products: 22.3 us -> none  [the longest x1 9.59 us: on_device(): jnp.einsum('secf,efd->secd', hidden, w_down, preferred_element_type=jnp.f...]
    psum x1 -> x0, blocking collectives: 15.2 us -> none  [on_device(): squares = lax.psum(jnp.sum(widened * widened, axis=1), 'grp')]
    unnamed x11 -> x30, local copies, waits for them, and re-layouts: 2.32 us -> 17 us
  transfers between devices with their start and end apart: 1 -> 27, of which waited for: 1 -> 21; matrix products, arithmetic and copies ran while one was open for 0% -> 0% of each run, Pallas kernels for 0% -> 2%
where the time goes in v1:
time: 106 us
  waiting for transfers between devices  47.1 us (44%)
  starting transfers between devices  28.1 us (27%)
  local copies, waits for them, and re-layouts  17.1 us (16%)
  Pallas kernels  11.3 us (11%)
  other arithmetic  2.12 us (2%)
    ppermute x12, waiting for transfers between devices, spread(): lax.ppermute(block, axis, shift(k))  21.5 us
    ppermute x9, waiting for transfers between devices, give_back(): lax.ppermute(blocks[k], axis, shift(-k))  21.3 us
    ppermute x12, starting transfers between devices, spread(): lax.ppermute(block, axis, shift(k))  18 us
    unnamed x30, local copies, waits for them, and re-layouts  17 us
    ppermute x9, starting transfers between devices, give_back(): lax.ppermute(blocks[k], axis, shift(-k))  9.79 us
    pallas_call x1, Pallas kernels, experts(): pl.pallas_call(experts_kernel, out_shape=[jax.ShapeDtypeStruct((rows, wid...  4.56 us
  transfers between devices with their start and end apart: 27, of which 21 were waited for; matrix products, arithmetic and copies ran while one was open for 0% of the time, Pallas kernels for 2%

profile of v1, /device:TPU:0, one launch (start us, length us, event | category | flops | bytes accessed | tf_op | source)
XLA Modules:
  0.0 105.8 jit_solution(1571051780808121989)
XLA Ops:
  0.0 1.2 %copy-done.4 = bf16[2,1024,256]{2,1,0:T(8,128)(2,1)S(1)} copy-done((bf16[2,1024,256]{2,1,0:T(8,128)(2,1)S(1)}, bf16[2,1024,256]{2,1,0:T(8,128)(2,1)}, u32[]{:S(2)}) %copy-start.4) | copy-done | bytes 1048600
  1.2 1.2 %copy-done.5 = bf16[2,1024,256]{2,1,0:T(8,128)(2,1)S(1)} copy-done((bf16[2,1024,256]{2,1,0:T(8,128)(2,1)S(1)}, bf16[2,1024,256]{2,1,0:T(8,128)(2,1)}, u32[]{:S(2)}) %copy-start.5) | copy-done | bytes 1048600
  2.5 0.7 copy-done.7
  3.2 0.7 copy-done.11
  3.8 1.9 %attention.1 = bf16[2,4096]{1,0:T(2,128)(2,1)S(1)} custom-call(s32[2]{0:T(128)S(1)} %copy-done.11, bf16[2,4096]{1,0:T(2,128)(2,1)S(1)} %copy-done.7, bf16[2,1024,256]{2,1,0:T(8,128)(2,1)S(1)} %copy-done.4, bf16[2,1024,256]{2,1,0:T(8,128)(2,1)S(1)} %copy-done.5), custom_call_target="tpu_custom_call" | custom-call | tf_op jit(solution)/shard_map/attention/pallas_call | solution.py:94
  5.8 1.2 %collective-permute-done = bf16[2,4096]{1,0:T(2,128)(2,1)S(1)} collective-permute-done((bf16[2,4096]{1,0:T(2,128)(2,1)S(1)}, bf16[2,4096]{1,0:T(2,128)(2,1)S(1)}, u32[]{:S(2)}, u32[]{:S(2)}) %collective-permute-start) | collective-permute-done | bytes 16416 | tf_op jit(solution)/shard_map/ppermute | solution.py:326
  7.0 4.2 %collective-permute-start.3 = (bf16[4,4096]{1,0:T(4,128)(2,1)S(1)}, bf16[4,4096]{1,0:T(4,128)(2,1)S(1)}, u32[]{:S(2)}, u32[]{:S(2)}) collective-permute-start(bf16[4,4096]{1,0:T(4,128)(2,1)S(1)} %pad_maximum_fusion.1.a0), channel_id=1, source_target_pairs={{0,6},{1,7},{2,0},{3,1},{4,2},{5,3},{6,4},{7,5},{8,14},{9,15},{10,... | collective-permute-start | bytes 98312 | tf_op jit(solution)/shard_map/ppermute | solution.py:53
  11.2 1.3 %collective-permute-start.1 = (bf16[4,4096]{1,0:T(4,128)(2,1)S(1)}, bf16[4,4096]{1,0:T(4,128)(2,1)S(1)}, u32[]{:S(2)}, u32[]{:S(2)}) collective-permute-start(bf16[4,4096]{1,0:T(4,128)(2,1)S(1)} %pad_maximum_fusion.1.a0), channel_id=1, source_target_pairs={{0,2},{1,3},{2,4},{3,5},{4,6},{5,7},{6,0},{7,1},{8,10},{9,11},{10,... | collective-permute-start | bytes 98312 | tf_op jit(solution)/shard_map/ppermute | solution.py:53
  12.5 1.5 %routes.1.extra_ref = bf16[16,128]{1,0:T(8,128)(2,1)} custom-call(s32[8,16]{1,0:T(8,128)} %bitcast.15, f32[8,16]{1,0:T(8,128)} %bitcast.16), custom_call_target="tpu_custom_call" | custom-call | tf_op jit(solution)/shard_map/routes/pallas_call | solution.py:124
  13.9 2.7 %collective-permute-done.2.a2 = bf16[4,4096]{1,0:T(4,128)(2,1)S(1)} collective-permute-done((bf16[4,4096]{1,0:T(4,128)(2,1)S(1)}, bf16[4,4096]{1,0:T(4,128)(2,1)S(1)}, u32[]{:S(2)}, u32[]{:S(2)}) %collective-permute-start.2) | collective-permute-done | bytes 32800 | tf_op jit(solution)/shard_map/ppermute | solution.py:53
  16.7 2.2 %copy-done.3 = bf16[4096,512]{1,0:T(8,128)(2,1)S(1)} copy-done((bf16[4096,512]{1,0:T(8,128)(2,1)S(1)}, bf16[4096,512]{1,0:T(8,128)(2,1)}, u32[]{:S(2)}) %copy-start.3) | copy-done | bytes 4194328
  18.9 0.7 copy-done.8
  19.6 0.7 copy-done.9
  20.3 0.7 copy-done.10
  20.9 0.9 stream.1
  21.9 0.9 collective-permute-start.6
  22.7 1.2 %collective-permute-start.5 = (bf16[16,640]{1,0:T(8,128)(2,1)S(1)}, bf16[16,640]{1,0:T(8,128)(2,1)S(1)}, u32[]{:S(2)}, u32[]{:S(2)}) collective-permute-start(bf16[16,640]{1,0:T(8,128)(2,1)S(1)} %get-tuple-element.10.u0), channel_id=1, source_target_pairs={{0,4},{1,5},{2,6},{3,7},{4,0},{5,1},{6,2},{7,3},{8,12},{9,13},{10,... | collective-permute-start | bytes 61448 | tf_op jit(solution)/shard_map/ppermute | solution.py:53
  23.9 1.3 %collective-permute-start.4 = (bf16[16,640]{1,0:T(8,128)(2,1)S(1)}, bf16[16,640]{1,0:T(8,128)(2,1)S(1)}, u32[]{:S(2)}, u32[]{:S(2)}) collective-permute-start(bf16[16,640]{1,0:T(8,128)(2,1)S(1)} %get-tuple-element.10.u0), channel_id=1, source_target_pairs={{0,2},{1,3},{2,4},{3,5},{4,6},{5,7},{6,0},{7,1},{8,10},{9,11},{10,... | collective-permute-start | bytes 61448 | tf_op jit(solution)/shard_map/ppermute | solution.py:53
  25.3 0.4 collective-permute-done.6.u3
  25.7 2.4 %collective-permute-done.5.u2 = bf16[16,640]{1,0:T(8,128)(2,1)S(1)} collective-permute-done((bf16[16,640]{1,0:T(8,128)(2,1)S(1)}, bf16[16,640]{1,0:T(8,128)(2,1)S(1)}, u32[]{:S(2)}, u32[]{:S(2)}) %collective-permute-start.5) | collective-permute-done | bytes 20512 | tf_op jit(solution)/shard_map/ppermute | solution.py:53
  28.0 0.9 collective-permute-done.4.u1
  29.0 0.6 copy-done.14
  29.5 1.5 %pack.1 = bf16[16,2176]{1,0:T(8,128)(2,1)} custom-call(bf16[16,640]{1,0:T(8,128)(2,1)} %copy-done.6, bf16[16,640]{1,0:T(8,128)(2,1)} %copy-done.14, bf16[16,640]{1,0:T(8,128)(2,1)} %copy-done.13, bf16[16,640]{1,0:T(8,128)(2,1)} %copy-done.12), custom_call_target="tpu_custom_call" | custom-call | tf_op jit(solution)/shard_map/pack/pallas_call | solution.py:198
  31.0 3.0 %collective-permute-start.9 = (bf16[16,2176]{1,0:T(8,128)(2,1)}, bf16[16,2176]{1,0:T(8,128)(2,1)S(1)}, u32[]{:S(2)}, u32[]{:S(2)}) collective-permute-start(bf16[16,2176]{1,0:T(8,128)(2,1)} %pack.1), channel_id=1, source_target_pairs={{0,24},{8,0},{16,8},{24,16},{32,56},{40,32},{48,40},{56,48},{64,88... | collective-permute-start | bytes 208904 | tf_op jit(solution)/shard_map/ppermute | solution.py:53
  34.1 0.6 collective-permute-start.8
  34.7 1.0 collective-permute-start.7
  35.7 0.7 collective-permute-done.9
  36.3 3.8 %collective-permute-done.8 = bf16[16,2176]{1,0:T(8,128)(2,1)S(1)} collective-permute-done((bf16[16,2176]{1,0:T(8,128)(2,1)}, bf16[16,2176]{1,0:T(8,128)(2,1)S(1)}, u32[]{:S(2)}, u32[]{:S(2)}) %collective-permute-start.8) | collective-permute-done | bytes 69664 | tf_op jit(solution)/shard_map/ppermute | solution.py:53
  40.1 0.7 collective-permute-done.7
  40.8 0.9 pad_maximum_fusion.o0
  41.7 2.8 %collective-permute-start.12 = (bf16[64,2176]{1,0:T(8,128)(2,1)S(1)}, bf16[64,2176]{1,0:T(8,128)(2,1)S(1)}, u32[]{:S(2)}, u32[]{:S(2)}) collective-permute-start(bf16[64,2176]{1,0:T(8,128)(2,1)S(1)} %pad_maximum_fusion.o0), channel_id=1, source_target_pairs={{0,96},{8,104},{16,112},{24,120},{32,0},{40,8},{48,16},{56,24},{64... | collective-permute-start | bytes 835592 | tf_op jit(solution)/shard_map/ppermute | solution.py:53
  44.6 0.8 collective-permute-start.11
  45.4 0.9 collective-permute-start.10
  46.2 6.2 %collective-permute-done.12.o3 = bf16[64,2176]{1,0:T(8,128)(2,1)S(1)} collective-permute-done((bf16[64,2176]{1,0:T(8,128)(2,1)S(1)}, bf16[64,2176]{1,0:T(8,128)(2,1)S(1)}, u32[]{:S(2)}, u32[]{:S(2)}) %collective-permute-start.12) | collective-permute-done | bytes 278560 | tf_op jit(solution)/shard_map/ppermute | solution.py:53
  52.5 0.8 collective-permute-done.11.o2
  53.3 2.8 %collective-permute-done.10.o1 = bf16[64,2176]{1,0:T(8,128)(2,1)S(1)} collective-permute-done((bf16[64,2176]{1,0:T(8,128)(2,1)S(1)}, bf16[64,2176]{1,0:T(8,128)(2,1)S(1)}, u32[]{:S(2)}, u32[]{:S(2)}) %collective-permute-start.10) | collective-permute-done | bytes 278560 | tf_op jit(solution)/shard_map/ppermute | solution.py:53
  56.2 1.5 %collective-permute-done.14.t1 = bf16[64,2176]{1,0:T(8,128)(2,1)S(1)} collective-permute-done((bf16[64,2176]{1,0:T(8,128)(2,1)S(1)}, bf16[64,2176]{1,0:T(8,128)(2,1)S(1)}, u32[]{:S(2)}, u32[]{:S(2)}) %collective-permute-start.14) | collective-permute-done | bytes 278560 | tf_op jit(solution)/shard_map/ppermute | solution.py:332
  57.7 2.8 %copy-done = bf16[4,192,4096]{2,1,0:T(8,128)(2,1)S(1)} copy-done((bf16[4,192,4096]{2,1,0:T(8,128)(2,1)S(1)}, bf16[4,192,4096]{2,1,0:T(8,128)(2,1)}, u32[]{:S(2)}) %copy-start) | copy-done | bytes 6291480
  60.5 2.8 %copy-done.1 = bf16[4,4096,192]{1,2,0:T(8,128)(2,1)S(1)} copy-done((bf16[4,4096,192]{1,2,0:T(8,128)(2,1)S(1)}, bf16[4,4096,192]{1,2,0:T(8,128)(2,1)}, u32[]{:S(2)}) %copy-start.1) | copy-done | bytes 6291480
  63.3 2.8 %copy-done.2 = bf16[4,4096,192]{1,2,0:T(8,128)(2,1)S(1)} copy-done((bf16[4,4096,192]{1,2,0:T(8,128)(2,1)S(1)}, bf16[4,4096,192]{1,2,0:T(8,128)(2,1)}, u32[]{:S(2)}) %copy-start.2) | copy-done | bytes 6291480
  66.1 4.6 %experts.1 = (bf16[256,768]{1,0:T(8,128)(2,1)S(1)}, bf16[256,2048]{1,0:T(8,128)(2,1)S(1)}) custom-call(bf16[64,2176]{1,0:T(8,128)(2,1)S(1)} %pad_maximum_fusion.o0, bf16[64,2176]{1,0:T(8,128)(2,1)S(1)} %collective-permute-done.10.o1, bf16[64,2176]{1,0:T(8,128)(2,1)S(1)} %collective-permute-done.11.o2, bf16[64,2176]{1,0:T(8,128)(2,1)S(1)} %collective-permute-done.12.o3, ...), custom_call_target="tpu_custom_call" | custom-call | flops 4026531840 | bytes 18874368 | tf_op jit(solution)/shard_map/experts/pallas_call | solution.py:263
  70.6 0.2 collective-permute-start.17
  70.8 1.0 down_own.1
  71.8 1.6 %collective-permute-done.17 = bf16[256,2048]{1,0:T(8,128)(2,1)S(1)} collective-permute-done((bf16[256,2048]{1,0:T(8,128)(2,1)S(1)}, bf16[256,2048]{1,0:T(8,128)(2,1)S(1)}, u32[]{:S(2)}, u32[]{:S(2)}) %collective-permute-start.17) | collective-permute-done | bytes 1048608 | tf_op jit(solution)/shard_map/ppermute | solution.py:334
  73.4 0.4 add_convert_fusion
  73.8 1.0 collective-permute-start.18
  74.9 1.2 %collective-permute-start.20 = (bf16[64,2048]{1,0:T(8,128)(2,1)S(1)}, bf16[64,2048]{1,0:T(8,128)(2,1)S(1)}, u32[]{:S(2)}, u32[]{:S(2)}) collective-permute-start(bf16[64,2048]{1,0:T(8,128)(2,1)S(1)} %get-tuple-element.14), channel_id=1, source_target_pairs={{0,32},{8,40},{16,48},{24,56},{32,64},{40,72},{48,80},{56,88},{64,... | collective-permute-start | bytes 786440 | tf_op jit(solution)/shard_map/ppermute | solution.py:57
  76.1 0.8 collective-permute-start.19
  77.0 6.3 %collective-permute-done.18 = bf16[64,2048]{1,0:T(8,128)(2,1)S(1)} collective-permute-done((bf16[64,2048]{1,0:T(8,128)(2,1)S(1)}, bf16[64,2048]{1,0:T(8,128)(2,1)S(1)}, u32[]{:S(2)}, u32[]{:S(2)}) %collective-permute-start.18) | collective-permute-done | bytes 262176 | tf_op jit(solution)/shard_map/ppermute | solution.py:57
  83.2 6.5 %collective-permute-done.20 = bf16[64,2048]{1,0:T(8,128)(2,1)S(1)} collective-permute-done((bf16[64,2048]{1,0:T(8,128)(2,1)S(1)}, bf16[64,2048]{1,0:T(8,128)(2,1)S(1)}, u32[]{:S(2)}, u32[]{:S(2)}) %collective-permute-start.20) | collective-permute-done | bytes 262176 | tf_op jit(solution)/shard_map/ppermute | solution.py:57
  89.8 0.1 add_convert_fusion.1
  89.9 0.6 collective-permute-start.21
  90.6 1.5 %collective-permute-start.23 = (bf16[16,2048]{1,0:T(8,128)(2,1)S(1)}, bf16[16,2048]{1,0:T(8,128)(2,1)S(1)}, u32[]{:S(2)}, u32[]{:S(2)}) collective-permute-start(bf16[16,2048]{1,0:T(8,128)(2,1)S(1)} %get-tuple-element.17), channel_id=1, source_target_pairs={{0,8},{8,16},{16,24},{24,0},{32,40},{40,48},{48,56},{56,32},{64,72... | collective-permute-start | bytes 196616 | tf_op jit(solution)/shard_map/ppermute | solution.py:57
  92.0 1.0 collective-permute-start.22
  93.0 1.2 %collective-permute-done.21 = bf16[16,2048]{1,0:T(8,128)(2,1)S(1)} collective-permute-done((bf16[16,2048]{1,0:T(8,128)(2,1)S(1)}, bf16[16,2048]{1,0:T(8,128)(2,1)S(1)}, u32[]{:S(2)}, u32[]{:S(2)}) %collective-permute-start.21) | collective-permute-done | bytes 65568 | tf_op jit(solution)/shard_map/ppermute | solution.py:57
  94.3 1.8 %collective-permute-done.23 = bf16[16,2048]{1,0:T(8,128)(2,1)S(1)} collective-permute-done((bf16[16,2048]{1,0:T(8,128)(2,1)S(1)}, bf16[16,2048]{1,0:T(8,128)(2,1)S(1)}, u32[]{:S(2)}, u32[]{:S(2)}) %collective-permute-start.23) | collective-permute-done | bytes 65568 | tf_op jit(solution)/shard_map/ppermute | solution.py:57
  96.0 1.8 %collective-permute-done.22 = bf16[16,2048]{1,0:T(8,128)(2,1)S(1)} collective-permute-done((bf16[16,2048]{1,0:T(8,128)(2,1)S(1)}, bf16[16,2048]{1,0:T(8,128)(2,1)S(1)}, u32[]{:S(2)}, u32[]{:S(2)}) %collective-permute-start.22) | collective-permute-done | bytes 65568 | tf_op jit(solution)/shard_map/ppermute | solution.py:57
  97.8 1.6 %collective-permute-start.24 = (bf16[16,512]{1,0:T(8,128)(2,1)S(1)}, bf16[16,512]{1,0:T(8,128)(2,1)S(1)}, u32[]{:S(2)}, u32[]{:S(2)}) collective-permute-start(bf16[16,512]{1,0:T(8,128)(2,1)S(1)} %get-tuple-element.19), channel_id=1, source_target_pairs={{0,6},{1,7},{2,0},{3,1},{4,2},{5,3},{6,4},{7,5},{8,14},{9,15},{10,... | collective-permute-start | bytes 49160 | tf_op jit(solution)/shard_map/ppermute | solution.py:57
  99.4 0.5 collective-permute-start.26
  99.9 1.5 %collective-permute-start.25 = (bf16[16,512]{1,0:T(8,128)(2,1)S(1)}, bf16[16,512]{1,0:T(8,128)(2,1)S(1)}, u32[]{:S(2)}, u32[]{:S(2)}) collective-permute-start(bf16[16,512]{1,0:T(8,128)(2,1)S(1)} %get-tuple-element.21), channel_id=1, source_target_pairs={{0,4},{1,5},{2,6},{3,7},{4,0},{5,1},{6,2},{7,3},{8,12},{9,13},{10,... | collective-permute-start | bytes 49160 | tf_op jit(solution)/shard_map/ppermute | solution.py:57
  101.4 0.2 collective-permute-done.24
  101.6 2.7 %collective-permute-done.26 = bf16[16,512]{1,0:T(8,128)(2,1)S(1)} collective-permute-done((bf16[16,512]{1,0:T(8,128)(2,1)S(1)}, bf16[16,512]{1,0:T(8,128)(2,1)S(1)}, u32[]{:S(2)}, u32[]{:S(2)}) %collective-permute-start.26) | collective-permute-done | bytes 16416 | tf_op jit(solution)/shard_map/ppermute | solution.py:57
  104.3 0.8 collective-permute-done.25
  105.2 0.6 add_convert_fusion.3
  (35 shorter events, 0.3 us)
Async XLA Ops:
  0.0 1.2 %copy-start.4 = (bf16[2,1024,256]{2,1,0:T(8,128)(2,1)S(1)}, bf16[2,1024,256]{2,1,0:T(8,128)(2,1)}, u32[]{:S(2)}) copy-start(bf16[2,1024,256]{2,1,0:T(8,128)(2,1)} %k_ref.1) | copy-start | bytes 3145732
  1.2 1.2 %copy-start.5 = (bf16[2,1024,256]{2,1,0:T(8,128)(2,1)S(1)}, bf16[2,1024,256]{2,1,0:T(8,128)(2,1)}, u32[]{:S(2)}) copy-start(bf16[2,1024,256]{2,1,0:T(8,128)(2,1)} %v_ref.1) | copy-start | bytes 3145732
  2.5 0.7 copy-start.7
  3.2 0.7 copy-start.11
  5.7 1.3 %collective-permute-start = (bf16[2,4096]{1,0:T(2,128)(2,1)S(1)}, bf16[2,4096]{1,0:T(2,128)(2,1)S(1)}, u32[]{:S(2)}, u32[]{:S(2)}) collective-permute-start(bf16[2,4096]{1,0:T(2,128)(2,1)S(1)} %attention.1), channel_id=1, source_target_pairs={{0,1},{1,0},{2,3},{3,2},{4,5},{5,4},{6,7},{7,6},{8,9},{9,8},{10,11... | collective-permute-start | bytes 49160 | tf_op jit(solution)/shard_map/ppermute | solution.py:326
  7.0 6.9 %collective-permute-start.3 = (bf16[4,4096]{1,0:T(4,128)(2,1)S(1)}, bf16[4,4096]{1,0:T(4,128)(2,1)S(1)}, u32[]{:S(2)}, u32[]{:S(2)}) collective-permute-start(bf16[4,4096]{1,0:T(4,128)(2,1)S(1)} %pad_maximum_fusion.1.a0), channel_id=1, source_target_pairs={{0,6},{1,7},{2,0},{3,1},{4,2},{5,3},{6,4},{7,5},{8,14},{9,15},{10,... | collective-permute-start | bytes 98312 | tf_op jit(solution)/shard_map/ppermute | solution.py:53
  11.2 5.5 %collective-permute-start.2 = (bf16[4,4096]{1,0:T(4,128)(2,1)S(1)}, bf16[4,4096]{1,0:T(4,128)(2,1)S(1)}, u32[]{:S(2)}, u32[]{:S(2)}) collective-permute-start(bf16[4,4096]{1,0:T(4,128)(2,1)S(1)} %pad_maximum_fusion.1.a0), channel_id=1, source_target_pairs={{0,4},{1,5},{2,6},{3,7},{4,0},{5,1},{6,2},{7,3},{8,12},{9,13},{10,... | collective-permute-start | bytes 98312 | tf_op jit(solution)/shard_map/ppermute | solution.py:53
  11.2 5.5 %collective-permute-start.1 = (bf16[4,4096]{1,0:T(4,128)(2,1)S(1)}, bf16[4,4096]{1,0:T(4,128)(2,1)S(1)}, u32[]{:S(2)}, u32[]{:S(2)}) collective-permute-start(bf16[4,4096]{1,0:T(4,128)(2,1)S(1)} %pad_maximum_fusion.1.a0), channel_id=1, source_target_pairs={{0,2},{1,3},{2,4},{3,5},{4,6},{5,7},{6,0},{7,1},{8,10},{9,11},{10,... | collective-permute-start | bytes 98312 | tf_op jit(solution)/shard_map/ppermute | solution.py:53
  16.7 2.2 %copy-start.3 = (bf16[4096,512]{1,0:T(8,128)(2,1)S(1)}, bf16[4096,512]{1,0:T(8,128)(2,1)}, u32[]{:S(2)}) copy-start(bf16[4096,512]{1,0:T(8,128)(2,1)} %w_ref.1) | copy-start | bytes 12582916
  18.9 0.7 copy-start.8
  19.6 0.7 copy-start.9
  20.3 0.7 copy-start.10
  21.9 7.1 %copy-start.6 = (bf16[16,640]{1,0:T(8,128)(2,1)}, bf16[16,640]{1,0:T(8,128)(2,1)S(1)}, u32[]{:S(2)}) copy-start(bf16[16,640]{1,0:T(8,128)(2,1)S(1)} %get-tuple-element.10.u0) | copy-start | bytes 61444
  21.9 3.8 %collective-permute-start.6 = (bf16[16,640]{1,0:T(8,128)(2,1)S(1)}, bf16[16,640]{1,0:T(8,128)(2,1)S(1)}, u32[]{:S(2)}, u32[]{:S(2)}) collective-permute-start(bf16[16,640]{1,0:T(8,128)(2,1)S(1)} %get-tuple-element.10.u0), channel_id=1, source_target_pairs={{0,6},{1,7},{2,0},{3,1},{4,2},{5,3},{6,4},{7,5},{8,14},{9,15},{10,... | collective-permute-start | bytes 61448 | tf_op jit(solution)/shard_map/ppermute | solution.py:53
  22.7 5.3 %collective-permute-start.5 = (bf16[16,640]{1,0:T(8,128)(2,1)S(1)}, bf16[16,640]{1,0:T(8,128)(2,1)S(1)}, u32[]{:S(2)}, u32[]{:S(2)}) collective-permute-start(bf16[16,640]{1,0:T(8,128)(2,1)S(1)} %get-tuple-element.10.u0), channel_id=1, source_target_pairs={{0,4},{1,5},{2,6},{3,7},{4,0},{5,1},{6,2},{7,3},{8,12},{9,13},{10,... | collective-permute-start | bytes 61448 | tf_op jit(solution)/shard_map/ppermute | solution.py:53
  23.9 5.0 %collective-permute-start.4 = (bf16[16,640]{1,0:T(8,128)(2,1)S(1)}, bf16[16,640]{1,0:T(8,128)(2,1)S(1)}, u32[]{:S(2)}, u32[]{:S(2)}) collective-permute-start(bf16[16,640]{1,0:T(8,128)(2,1)S(1)} %get-tuple-element.10.u0), channel_id=1, source_target_pairs={{0,2},{1,3},{2,4},{3,5},{4,6},{5,7},{6,0},{7,1},{8,10},{9,11},{10,... | collective-permute-start | bytes 61448 | tf_op jit(solution)/shard_map/ppermute | solution.py:53
  25.7 3.3 %copy-start.12 = (bf16[16,640]{1,0:T(8,128)(2,1)}, bf16[16,640]{1,0:T(8,128)(2,1)S(1)}, u32[]{:S(2)}) copy-start(bf16[16,640]{1,0:T(8,128)(2,1)S(1)} %collective-permute-done.6.u3) | copy-start | bytes 61444
  28.0 0.9 copy-start.13
  28.9 0.6 copy-start.14
  31.0 5.3 %collective-permute-start.9 = (bf16[16,2176]{1,0:T(8,128)(2,1)}, bf16[16,2176]{1,0:T(8,128)(2,1)S(1)}, u32[]{:S(2)}, u32[]{:S(2)}) collective-permute-start(bf16[16,2176]{1,0:T(8,128)(2,1)} %pack.1), channel_id=1, source_target_pairs={{0,24},{8,0},{16,8},{24,16},{32,56},{40,32},{48,40},{56,48},{64,88... | collective-permute-start | bytes 208904 | tf_op jit(solution)/shard_map/ppermute | solution.py:53
  34.1 6.1 %collective-permute-start.8 = (bf16[16,2176]{1,0:T(8,128)(2,1)}, bf16[16,2176]{1,0:T(8,128)(2,1)S(1)}, u32[]{:S(2)}, u32[]{:S(2)}) collective-permute-start(bf16[16,2176]{1,0:T(8,128)(2,1)} %pack.1), channel_id=1, source_target_pairs={{0,16},{8,24},{16,0},{24,8},{32,48},{40,56},{48,32},{56,40},{64,80... | collective-permute-start | bytes 208904 | tf_op jit(solution)/shard_map/ppermute | solution.py:53
  34.7 6.1 %collective-permute-start.7 = (bf16[16,2176]{1,0:T(8,128)(2,1)}, bf16[16,2176]{1,0:T(8,128)(2,1)S(1)}, u32[]{:S(2)}, u32[]{:S(2)}) collective-permute-start(bf16[16,2176]{1,0:T(8,128)(2,1)} %pack.1), channel_id=1, source_target_pairs={{0,8},{8,16},{16,24},{24,0},{32,40},{40,48},{48,56},{56,32},{64,72... | collective-permute-start | bytes 208904 | tf_op jit(solution)/shard_map/ppermute | solution.py:53
  41.7 10.8 %collective-permute-start.12 = (bf16[64,2176]{1,0:T(8,128)(2,1)S(1)}, bf16[64,2176]{1,0:T(8,128)(2,1)S(1)}, u32[]{:S(2)}, u32[]{:S(2)}) collective-permute-start(bf16[64,2176]{1,0:T(8,128)(2,1)S(1)} %pad_maximum_fusion.o0), channel_id=1, source_target_pairs={{0,96},{8,104},{16,112},{24,120},{32,0},{40,8},{48,16},{56,24},{64... | collective-permute-start | bytes 835592 | tf_op jit(solution)/shard_map/ppermute | solution.py:53
  44.6 8.8 %collective-permute-start.11 = (bf16[64,2176]{1,0:T(8,128)(2,1)S(1)}, bf16[64,2176]{1,0:T(8,128)(2,1)S(1)}, u32[]{:S(2)}, u32[]{:S(2)}) collective-permute-start(bf16[64,2176]{1,0:T(8,128)(2,1)S(1)} %pad_maximum_fusion.o0), channel_id=1, source_target_pairs={{0,64},{8,72},{16,80},{24,88},{32,96},{40,104},{48,112},{56,120},{... | collective-permute-start | bytes 835592 | tf_op jit(solution)/shard_map/ppermute | solution.py:53
  45.4 10.8 %collective-permute-start.10 = (bf16[64,2176]{1,0:T(8,128)(2,1)S(1)}, bf16[64,2176]{1,0:T(8,128)(2,1)S(1)}, u32[]{:S(2)}, u32[]{:S(2)}) collective-permute-start(bf16[64,2176]{1,0:T(8,128)(2,1)S(1)} %pad_maximum_fusion.o0), channel_id=1, source_target_pairs={{0,32},{8,40},{16,48},{24,56},{32,64},{40,72},{48,80},{56,88},{64,... | collective-permute-start | bytes 835592 | tf_op jit(solution)/shard_map/ppermute | solution.py:53
  46.2 9.9 %collective-permute-start.13 = (bf16[64,2176]{1,0:T(8,128)(2,1)S(1)}, bf16[64,2176]{1,0:T(8,128)(2,1)S(1)}, u32[]{:S(2)}, u32[]{:S(2)}) collective-permute-start(bf16[64,2176]{1,0:T(8,128)(2,1)S(1)} %pad_maximum_fusion.o0), channel_id=1, source_target_pairs={{0,1},{1,0},{2,3},{3,2},{4,5},{5,4},{6,7},{7,6},{8,9},{9,8},{10,11... | collective-permute-start | bytes 835592 | tf_op jit(solution)/shard_map/ppermute | solution.py:332
  52.5 3.7 %collective-permute-start.16 = (bf16[64,2176]{1,0:T(8,128)(2,1)S(1)}, bf16[64,2176]{1,0:T(8,128)(2,1)S(1)}, u32[]{:S(2)}, u32[]{:S(2)}) collective-permute-start(bf16[64,2176]{1,0:T(8,128)(2,1)S(1)} %collective-permute-done.12.o3), channel_id=1, source_target_pairs={{0,1},{1,0},{2,3},{3,2},{4,5},{5,4},{6,7},{7,6},{8,9},{9,8},{10,11... | collective-permute-start | bytes 835592 | tf_op jit(solution)/shard_map/ppermute | solution.py:332
  53.3 2.9 %collective-permute-start.15 = (bf16[64,2176]{1,0:T(8,128)(2,1)S(1)}, bf16[64,2176]{1,0:T(8,128)(2,1)S(1)}, u32[]{:S(2)}, u32[]{:S(2)}) collective-permute-start(bf16[64,2176]{1,0:T(8,128)(2,1)S(1)} %collective-permute-done.11.o2), channel_id=1, source_target_pairs={{0,1},{1,0},{2,3},{3,2},{4,5},{5,4},{6,7},{7,6},{8,9},{9,8},{10,11... | collective-permute-start | bytes 835592 | tf_op jit(solution)/shard_map/ppermute | solution.py:332
  56.2 1.6 %collective-permute-start.14 = (bf16[64,2176]{1,0:T(8,128)(2,1)S(1)}, bf16[64,2176]{1,0:T(8,128)(2,1)S(1)}, u32[]{:S(2)}, u32[]{:S(2)}) collective-permute-start(bf16[64,2176]{1,0:T(8,128)(2,1)S(1)} %collective-permute-done.10.o1), channel_id=1, source_target_pairs={{0,1},{1,0},{2,3},{3,2},{4,5},{5,4},{6,7},{7,6},{8,9},{9,8},{10,11... | collective-permute-start | bytes 835592 | tf_op jit(solution)/shard_map/ppermute | solution.py:332
  57.7 2.8 %copy-start = (bf16[4,192,4096]{2,1,0:T(8,128)(2,1)S(1)}, bf16[4,192,4096]{2,1,0:T(8,128)(2,1)}, u32[]{:S(2)}) copy-start(bf16[4,192,4096]{2,1,0:T(8,128)(2,1)} %param.23) | copy-start | bytes 18874372
  60.5 2.8 %copy-start.1 = (bf16[4,4096,192]{1,2,0:T(8,128)(2,1)S(1)}, bf16[4,4096,192]{1,2,0:T(8,128)(2,1)}, u32[]{:S(2)}) copy-start(bf16[4,4096,192]{1,2,0:T(8,128)(2,1)} %param.21) | copy-start | bytes 18874372
  63.3 2.8 %copy-start.2 = (bf16[4,4096,192]{1,2,0:T(8,128)(2,1)S(1)}, bf16[4,4096,192]{1,2,0:T(8,128)(2,1)}, u32[]{:S(2)}) copy-start(bf16[4,4096,192]{1,2,0:T(8,128)(2,1)} %param.22) | copy-start | bytes 18874372
  70.6 2.7 %collective-permute-start.17 = (bf16[256,2048]{1,0:T(8,128)(2,1)S(1)}, bf16[256,2048]{1,0:T(8,128)(2,1)S(1)}, u32[]{:S(2)}, u32[]{:S(2)}) collective-permute-start(bf16[256,2048]{1,0:T(8,128)(2,1)S(1)} %get-tuple-element.12), channel_id=1, source_target_pairs={{0,1},{1,0},{2,3},{3,2},{4,5},{5,4},{6,7},{7,6},{8,9},{9,8},{10,11... | collective-permute-start | bytes 3145736 | tf_op jit(solution)/shard_map/ppermute | solution.py:334
  73.8 9.4 %collective-permute-start.18 = (bf16[64,2048]{1,0:T(8,128)(2,1)S(1)}, bf16[64,2048]{1,0:T(8,128)(2,1)S(1)}, u32[]{:S(2)}, u32[]{:S(2)}) collective-permute-start(bf16[64,2048]{1,0:T(8,128)(2,1)S(1)} %get-tuple-element.13), channel_id=1, source_target_pairs={{0,96},{8,104},{16,112},{24,120},{32,0},{40,8},{48,16},{56,24},{64... | collective-permute-start | bytes 786440 | tf_op jit(solution)/shard_map/ppermute | solution.py:57
  74.9 14.9 %collective-permute-start.20 = (bf16[64,2048]{1,0:T(8,128)(2,1)S(1)}, bf16[64,2048]{1,0:T(8,128)(2,1)S(1)}, u32[]{:S(2)}, u32[]{:S(2)}) collective-permute-start(bf16[64,2048]{1,0:T(8,128)(2,1)S(1)} %get-tuple-element.14), channel_id=1, source_target_pairs={{0,32},{8,40},{16,48},{24,56},{32,64},{40,72},{48,80},{56,88},{64,... | collective-permute-start | bytes 786440 | tf_op jit(solution)/shard_map/ppermute | solution.py:57
  76.1 13.7 %collective-permute-start.19 = (bf16[64,2048]{1,0:T(8,128)(2,1)S(1)}, bf16[64,2048]{1,0:T(8,128)(2,1)S(1)}, u32[]{:S(2)}, u32[]{:S(2)}) collective-permute-start(bf16[64,2048]{1,0:T(8,128)(2,1)S(1)} %get-tuple-element.15), channel_id=1, source_target_pairs={{0,64},{8,72},{16,80},{24,88},{32,96},{40,104},{48,112},{56,120},{... | collective-permute-start | bytes 786440 | tf_op jit(solution)/shard_map/ppermute | solution.py:57
  89.9 4.3 %collective-permute-start.21 = (bf16[16,2048]{1,0:T(8,128)(2,1)S(1)}, bf16[16,2048]{1,0:T(8,128)(2,1)S(1)}, u32[]{:S(2)}, u32[]{:S(2)}) collective-permute-start(bf16[16,2048]{1,0:T(8,128)(2,1)S(1)} %get-tuple-element.16), channel_id=1, source_target_pairs={{0,24},{8,0},{16,8},{24,16},{32,56},{40,32},{48,40},{56,48},{64,88... | collective-permute-start | bytes 196616 | tf_op jit(solution)/shard_map/ppermute | solution.py:57
  90.6 5.5 %collective-permute-start.23 = (bf16[16,2048]{1,0:T(8,128)(2,1)S(1)}, bf16[16,2048]{1,0:T(8,128)(2,1)S(1)}, u32[]{:S(2)}, u32[]{:S(2)}) collective-permute-start(bf16[16,2048]{1,0:T(8,128)(2,1)S(1)} %get-tuple-element.17), channel_id=1, source_target_pairs={{0,8},{8,16},{16,24},{24,0},{32,40},{40,48},{48,56},{56,32},{64,72... | collective-permute-start | bytes 196616 | tf_op jit(solution)/shard_map/ppermute | solution.py:57
  92.0 5.8 %collective-permute-start.22 = (bf16[16,2048]{1,0:T(8,128)(2,1)S(1)}, bf16[16,2048]{1,0:T(8,128)(2,1)S(1)}, u32[]{:S(2)}, u32[]{:S(2)}) collective-permute-start(bf16[16,2048]{1,0:T(8,128)(2,1)S(1)} %get-tuple-element.18), channel_id=1, source_target_pairs={{0,16},{8,24},{16,0},{24,8},{32,48},{40,56},{48,32},{56,40},{64,80... | collective-permute-start | bytes 196616 | tf_op jit(solution)/shard_map/ppermute | solution.py:57
  97.8 3.8 %collective-permute-start.24 = (bf16[16,512]{1,0:T(8,128)(2,1)S(1)}, bf16[16,512]{1,0:T(8,128)(2,1)S(1)}, u32[]{:S(2)}, u32[]{:S(2)}) collective-permute-start(bf16[16,512]{1,0:T(8,128)(2,1)S(1)} %get-tuple-element.19), channel_id=1, source_target_pairs={{0,6},{1,7},{2,0},{3,1},{4,2},{5,3},{6,4},{7,5},{8,14},{9,15},{10,... | collective-permute-start | bytes 49160 | tf_op jit(solution)/shard_map/ppermute | solution.py:57
  99.4 4.9 %collective-permute-start.26 = (bf16[16,512]{1,0:T(8,128)(2,1)S(1)}, bf16[16,512]{1,0:T(8,128)(2,1)S(1)}, u32[]{:S(2)}, u32[]{:S(2)}) collective-permute-start(bf16[16,512]{1,0:T(8,128)(2,1)S(1)} %get-tuple-element.20), channel_id=1, source_target_pairs={{0,2},{1,3},{2,4},{3,5},{4,6},{5,7},{6,0},{7,1},{8,10},{9,11},{10,... | collective-permute-start | bytes 49160 | tf_op jit(solution)/shard_map/ppermute | solution.py:57
  99.9 5.2 %collective-permute-start.25 = (bf16[16,512]{1,0:T(8,128)(2,1)S(1)}, bf16[16,512]{1,0:T(8,128)(2,1)S(1)}, u32[]{:S(2)}, u32[]{:S(2)}) collective-permute-start(bf16[16,512]{1,0:T(8,128)(2,1)S(1)} %get-tuple-element.21), channel_id=1, source_target_pairs={{0,4},{1,5},{2,6},{3,7},{4,0},{5,1},{6,2},{7,3},{8,12},{9,13},{10,... | collective-permute-start | bytes 49160 | tf_op jit(solution)/shard_map/ppermute | solution.py:57

commit v2 on v1

v2 whole, which is shorter than its diff:
```python
import math

import jax
import jax.numpy as jnp
from jax import lax
from jax.experimental import pallas as pl
from jax.experimental.pallas import tpu as pltpu
from jax.sharding import Mesh
from jax.sharding import PartitionSpec as P

D = 4096
KV_HEADS = 2
HEAD = 128
LANES = 128
SIDE = 4
CORES = 2
PLACES = SIDE * SIDE
COLS = D // (SIDE * CORES)
CHUNKS = COLS // LANES
ROWS = 16
UNIT = CHUNKS * ROWS
EXTRA = 8
IDS, HI, MID, LO, SQ = 0, ROWS, 2 * ROWS, 3 * ROWS, 4 * ROWS
EXPERT_COLS = 192
F32 = jnp.float32
BF16 = jnp.bfloat16
NT = (((1,), (1,)), ((), ()))
VMEM = pl.BlockSpec(memory_space=pltpu.VMEM)
ANY = pl.BlockSpec(memory_space=pl.ANY)


def params(mib):
    return pltpu.CompilerParams(vmem_limit_bytes=mib * 1024 * 1024)


def split3(value):
    hi = value.astype(BF16).astype(F32)
    mid = (value - hi).astype(BF16).astype(F32)
    lo = value - hi - mid
    return hi, mid, lo


SWAP = [(0, 1), (1, 0)]


def swap(block):
    return lax.ppermute(block, "c", SWAP)


def spread_z(block):
    return [block] + [
        lax.ppermute(block, "z", [(i, (i + k) % SIDE) for i in range(SIDE)])
        for k in range(1, SIDE)
    ]


def attention_kernel(
    len_hbm, q_hbm, k_hbm, v_hbm, out_ref, lens, q_ref, k_ref, v_ref, q_rows, out_rows, sems
):
    rows, width = q_ref.shape
    positions = k_ref.shape[1]
    heads = width // HEAD
    per_group = heads // KV_HEADS
    len_copy = pltpu.make_async_copy(len_hbm, lens, sems.at[0])
    q_copy = pltpu.make_async_copy(q_hbm, q_ref, sems.at[1])
    k_copies = [
        pltpu.make_async_copy(k_hbm.at[r], k_ref.at[r], sems.at[2 + r]) for r in range(rows)
    ]
    v_copies = [
        pltpu.make_async_copy(v_hbm.at[r], v_ref.at[r], sems.at[2 + rows + r])
        for r in range(rows)
    ]
    q_copy.start()
    len_copy.start()
    for r in range(rows):
        k_copies[r].start()
        v_copies[r].start()
    q_copy.wait()
    queries = q_ref[...].astype(F32)
    for r in range(rows):
        for h in range(heads):
            q_rows[r * heads + h : r * heads + h + 1, :] = queries[
                r : r + 1, h * HEAD : (h + 1) * HEAD
            ]
    len_copy.wait()
    spots = lax.broadcasted_iota(jnp.int32, (per_group, positions), 1)
    for r in range(rows):
        live = spots < lens[r]
        k_copies[r].wait()
        v_copies[r].wait()
        for g in range(KV_HEADS):
            first = r * heads + g * per_group
            q = q_rows[first : first + per_group, :].astype(BF16)
            keys = k_ref[r, :, g * HEAD : (g + 1) * HEAD]
            scores = lax.dot_general(q, keys, NT, preferred_element_type=F32) / math.sqrt(HEAD)
            scores = jnp.where(live, scores, -1e30)
            peak = jnp.max(scores, axis=1, keepdims=True)
            probs = jnp.where(live, jnp.exp(scores - peak), 0.0)
            weight_sum = jnp.sum(probs, axis=1, keepdims=True)
            values = v_ref[r, :, g * HEAD : (g + 1) * HEAD]
            summed = jnp.dot(probs.astype(BF16), values, preferred_element_type=F32)
            summed = summed / weight_sum
            for j in range(per_group):
                h = g * per_group + j
                out_rows[r : r + 1, h * HEAD : (h + 1) * HEAD] = summed[j : j + 1, :]
    out_ref[...] = out_rows[...].astype(BF16)


def attention(lengths, queries, keys, values):
    rows, width = queries.shape
    return pl.pallas_call(
        attention_kernel,
        out_shape=jax.ShapeDtypeStruct((rows, width), BF16),
        in_specs=[ANY] * 4,
        out_specs=VMEM,
        scratch_shapes=[
            pltpu.SMEM(lengths.shape, jnp.int32),
            pltpu.VMEM((rows, width), BF16),
            pltpu.VMEM(keys.shape, BF16),
            pltpu.VMEM(values.shape, BF16),
            pltpu.VMEM((rows * width // HEAD, HEAD), F32),
            pltpu.VMEM((rows, width), F32),
            pltpu.SemaphoreType.DMA((2 + 2 * rows,)),
        ],
        compiler_params=params(16),
        name="attention",
    )(*map(in_hbm, (lengths, queries, keys, values)))


def in_hbm(value):
    return pltpu.with_memory_space_constraint(value, pltpu.HBM)


def fetch_kernel(*refs):
    count = (len(refs) - 2) // 2
    sources, targets, sems = refs[1 : 1 + count], refs[1 + count : -1], refs[-1]
    copies = [
        pltpu.make_async_copy(s, t, sems.at[i]) for i, (s, t) in enumerate(zip(sources, targets))
    ]
    for copy in copies:
        copy.start()
    for copy in copies:
        copy.wait()


def fetch(after, *arrays):
    size = sum(a.size * a.dtype.itemsize for a in arrays)
    return pl.pallas_call(
        fetch_kernel,
        out_shape=[pltpu.VMEM(a.shape, a.dtype) for a in arrays],
        in_specs=[ANY] * (1 + len(arrays)),
        out_specs=[VMEM] * len(arrays),
        scratch_shapes=[pltpu.SemaphoreType.DMA((len(arrays),))],
        compiler_params=params(1),
        cost_estimate=pl.CostEstimate(flops=0, bytes_accessed=size, transcendentals=0),
        name="fetch",
    )(after, *map(in_hbm, arrays))


def routes_of(ids, weights):
    top = ids.shape[0]
    lane = lax.broadcasted_iota(jnp.int32, (ROWS, LANES), 1)
    row = lax.broadcasted_iota(jnp.int32, (ROWS, LANES), 0)
    hi, mid, lo = split3(weights)
    total = jnp.zeros((top, LANES), F32)
    for piece, start in ((ids.astype(F32), IDS), (hi, HI), (mid, MID), (lo, LO)):
        place = (lane == row + start).astype(BF16)
        total += jnp.dot(piece.astype(BF16), place, preferred_element_type=F32)
    return total


def stream_kernel(
    a0, a1, a2, a3, w_ref, residual_ref, gain_ref, ids_ref, weights_ref, stream_ref, unit_ref, rows_ref
):
    part = a0.shape[0]
    for k, a in enumerate((a0, a1, a2, a3)):
        rows_ref[k * part : (k + 1) * part, :] = a[...].astype(F32)
    mixed = jnp.dot(rows_ref[...].astype(BF16), w_ref[...], preferred_element_type=F32)
    half = part // CORES
    z, c = lax.axis_index("z"), lax.axis_index("c")
    here = lax.broadcasted_iota(jnp.int32, (ROWS, ROWS), 1)
    wanted = lax.broadcasted_iota(jnp.int32, (ROWS, ROWS), 0)
    slot, within = here // part, here % part
    owner = (z - slot + SIDE) % SIDE * CORES + (c + within // half) % CORES
    order = (wanted == owner * half + within % half).astype(F32)
    mixed = jnp.dot(order, mixed, precision=lax.Precision.HIGHEST, preferred_element_type=F32)
    stream = (residual_ref[...].astype(F32) + mixed).astype(BF16)
    stream_ref[...] = stream
    widened = stream.astype(F32)
    scaled = (widened * gain_ref[...]).astype(BF16)
    squares = jnp.sum(widened * widened, axis=1, keepdims=True)
    lane = lax.broadcasted_iota(jnp.int32, (ROWS, LANES), 1)
    row = lax.broadcasted_iota(jnp.int32, (ROWS, LANES), 0)
    squares = jnp.sum(jnp.where(lane == row + SQ, squares, 0.0), axis=0, keepdims=True)
    extra = routes_of(ids_ref[...], weights_ref[...])
    line = lax.broadcasted_iota(jnp.int32, extra.shape, 0)
    held = lax.broadcasted_iota(jnp.int32, extra.shape, 1) >= SQ
    for i, piece in enumerate(split3(squares)):
        extra = jnp.where(held & (line == i), piece, extra)
    unit = jnp.concatenate(
        [scaled[:, j * LANES : (j + 1) * LANES] for j in range(CHUNKS)] + [extra.astype(BF16)],
        axis=0,
    )
    for i in range(unit_ref.shape[0]):
        unit_ref[i] = unit


def make_stream(parts, out_proj, residual, gain, ids, weights):
    return pl.pallas_call(
        stream_kernel,
        out_shape=[
            jax.ShapeDtypeStruct((ROWS, COLS), BF16),
            jax.ShapeDtypeStruct((PLACES * SIDE, UNIT + EXTRA, LANES), BF16),
        ],
        in_specs=[VMEM] * 9,
        out_specs=[VMEM, VMEM],
        scratch_shapes=[pltpu.VMEM((ROWS, D), F32)],
        compiler_params=params(4),
        name="stream",
    )(*parts, out_proj, residual, gain, ids, weights)


def column_block(z, c):
    return pl.ds(pl.multiple_of((z * CORES + c) * COLS, COLS), COLS)


def to_columns(lines, start):
    shape = (PLACES, ROWS, LANES)
    lane = lax.broadcasted_iota(jnp.int32, shape, 2)
    row = lax.broadcasted_iota(jnp.int32, shape, 1)
    kept = jnp.where(lane == row + start, jnp.broadcast_to(lines, shape), 0.0)
    return jnp.sum(kept, axis=2, keepdims=True).reshape(PLACES * ROWS, 1)


def down_half(hidden, down_ref, out_ref, c):
    for z in range(SIDE):
        part = jnp.dot(
            hidden, down_ref[:, column_block(z, c)], preferred_element_type=F32
        ).astype(BF16)
        for s in range(PLACES):
            out_ref[s * SIDE + z] = part[s * ROWS : (s + 1) * ROWS]


def experts_kernel(own_ref, other_ref, gate_ref, up_ref, down_ref, hidden_ref, out_ref, x_ref):
    c = lax.axis_index("c")
    local = gate_ref.shape[0] // EXPERT_COLS
    first = (lax.axis_index("x") * SIDE + lax.axis_index("y")) * local
    for s in range(PLACES):
        for z in range(SIDE):
            for half, parity in ((own_ref, c), (other_ref, 1 - c)):
                start = pl.multiple_of((z * CORES + parity) * COLS, COLS)
                for j in range(CHUNKS):
                    x_ref[s * ROWS : (s + 1) * ROWS, pl.ds(start + j * LANES, LANES)] = half[
                        s * SIDE + z, j * ROWS : (j + 1) * ROWS, :
                    ]
    squares = jnp.zeros((PLACES, 1, LANES), F32)
    for s_ref in (own_ref, other_ref):
        extras = s_ref[:, UNIT:, :].astype(F32).reshape(PLACES, SIDE, EXTRA, LANES)
        for z in range(SIDE):
            squares += jnp.sum(extras[:, z, :3, :], axis=1, keepdims=True)
    scale = lax.rsqrt(to_columns(squares, SQ) / D + 1e-06)
    routes = jnp.stack([own_ref[s * SIDE, UNIT:, :] for s in range(PLACES)]).astype(F32)
    weights = (
        pltpu.roll(routes, LANES - HI, 2)
        + pltpu.roll(routes, LANES - MID, 2)
        + pltpu.roll(routes, LANES - LO, 2)
    )
    x = x_ref[...]
    gate = lax.dot_general(x, gate_ref[...], NT, preferred_element_type=F32) * scale
    up = lax.dot_general(x, up_ref[...], NT, preferred_element_type=F32) * scale
    column = lax.broadcasted_iota(jnp.int32, gate.shape, 1)
    mix = None
    for e in range(local):
        mine = jnp.where(routes == (first + e).astype(F32), weights, 0.0)
        one = to_columns(jnp.sum(mine, axis=1, keepdims=True), IDS)
        mix = one if mix is None else jnp.where(column < e * EXPERT_COLS, mix, one)
    hidden = (gate / (1.0 + jnp.exp(-gate)) * up * mix).astype(BF16)
    hidden_ref[...] = hidden
    down_half(hidden, down_ref, out_ref, 1 - c)


def experts(own, other, gate, up, down):
    rows = PLACES * ROWS
    width = gate.shape[0]
    return pl.pallas_call(
        experts_kernel,
        out_shape=[
            jax.ShapeDtypeStruct((rows, width), BF16),
            jax.ShapeDtypeStruct((PLACES * SIDE, ROWS, COLS), BF16),
        ],
        in_specs=[VMEM] * 5,
        out_specs=[VMEM, VMEM],
        scratch_shapes=[pltpu.VMEM((rows, D), BF16)],
        compiler_params=params(20),
        cost_estimate=pl.CostEstimate(
            flops=5 * rows * width * D, bytes_accessed=6 * width * D, transcendentals=rows * width
        ),
        name="experts",
    )(own, other, gate, up, down)


def down_kernel(hidden_ref, down_ref, out_ref):
    down_half(hidden_ref[...], down_ref, out_ref, lax.axis_index("c"))


def down_own(hidden, down):
    rows, width = hidden.shape
    return pl.pallas_call(
        down_kernel,
        out_shape=jax.ShapeDtypeStruct((PLACES * SIDE, ROWS, COLS), BF16),
        in_specs=[VMEM, VMEM],
        out_specs=VMEM,
        compiler_params=params(20),
        cost_estimate=pl.CostEstimate(
            flops=rows * width * D, bytes_accessed=2 * width * D, transcendentals=0
        ),
        name="down_own",
    )(hidden, down)


def exchange(blocks):
    return lax.all_to_all(blocks, ("x", "y", "z"), split_axis=0, concat_axis=0, tiled=True)


def on_device(
    queries,
    key_cache,
    value_cache,
    lengths,
    residual,
    out_proj,
    norm_gain,
    expert_ids,
    route_weights,
    w_gate,
    w_up,
    w_down,
):
    gate = jnp.swapaxes(w_gate, 1, 2).reshape(-1, D)
    up = jnp.swapaxes(w_up, 1, 2).reshape(-1, D)
    down = w_down.reshape(-1, D)
    attended = attention(lengths, queries, key_cache, value_cache)
    pair = jnp.concatenate([attended, swap(attended)], axis=0)
    parts = spread_z(pair)
    out_proj, residual, gain, ids, weights, gate, up = fetch(
        pair, out_proj, residual, norm_gain[None, :], expert_ids.T, route_weights.T, gate, up
    )
    stream, units = make_stream(parts, out_proj, residual, gain, ids, weights)
    own = exchange(units)
    other = swap(own)
    (down,) = fetch(own, down)
    hidden, theirs = experts(own, other, gate, up, down)
    came = swap(theirs)
    mine = down_own(hidden, down)
    total = (mine.astype(F32) + came.astype(F32)).astype(BF16)
    combined = jnp.sum(exchange(total).astype(F32), axis=0)
    return (stream.astype(F32) + combined).astype(BF16)


def solution(mesh):
    devices = mesh.devices.reshape(SIDE, SIDE, SIDE, CORES)
    pool, grp = ("x", "y"), ("z", "c")
    every = pool + grp
    in_specs = (
        P(every, None),
        P(every, None, None),
        P(every, None, None),
        P(every),
        P(pool, grp),
        P(None, grp),
        P(grp),
        P(pool, None),
        P(pool, None),
        P(pool, None, grp),
        P(pool, None, grp),
        P(pool, grp, None),
    )
    return jax.shard_map(
        on_device,
        mesh=Mesh(devices, every),
        in_specs=in_specs,
        out_specs=P(pool, grp),
        check_vma=False,
    )
```

time: 106 us -> 81 us (0.76)
  blocking collectives: 0 us -> 52.8 us
  waiting for transfers between devices: 47.1 us -> 2.52 us
  starting transfers between devices: 28.1 us -> 6.07 us
  local copies, waits for them, and re-layouts: 17.1 us -> 0 us
  Pallas kernels: 11.3 us -> 18.1 us
    all_to_all x0 -> x2, blocking collectives: none -> 52.8 us  [exchange(): lax.all_to_all(blocks, ('x', 'y', 'z'), split_axis=0, concat_axis=0, tile...]
    ppermute x27 -> x6, waiting for transfers between devices: 47.1 us -> 2.52 us  [the longest x3 2.52 us: swap(): return lax.ppermute(block, 'c', SWAP)]
    ppermute x27 -> x6, starting transfers between devices: 28.1 us -> 6.07 us  [the longest x3 5.45 us: spread_z(): lax.ppermute(block, 'z', [(i, (i + k) % SIDE) for i in range(SIDE)])]
    unnamed x30 -> x0, local copies, waits for them, and re-layouts: 17 us -> none
    pallas_call x4, Pallas kernels: 4.86 us -> 10.7 us  [the longest x2 8.77 us: fetch(): pl.pallas_call(fetch_kernel, out_shape=[pltpu.VMEM(a.shape, a.dtype) for...]
  transfers between devices with their start and end apart: 27 -> 6, of which waited for: 21 -> 2; matrix products, arithmetic and copies ran while one was open for 0% -> 0% of each run, Pallas kernels for 2% -> 12%
where the time goes in v2:
time: 81 us; the launch traced here: 80.8 us
  blocking collectives  52.8 us (65%)
  Pallas kernels  18.1 us (22%)
  starting transfers between devices  6.07 us (7%)
  waiting for transfers between devices  2.52 us (3%)
  other arithmetic  1.22 us (2%)
    all_to_all x2, blocking collectives, exchange(): lax.all_to_all(blocks, ('x', 'y', 'z'), split_axis=0, concat_axis=0, tile...  52.8 us
    pallas_call x2, Pallas kernels, fetch(): pl.pallas_call(fetch_kernel, out_shape=[pltpu.VMEM(a.shape, a.dtype) for...  8.77 us
    ppermute x3, starting transfers between devices, spread_z(): lax.ppermute(block, 'z', [(i, (i + k) % SIDE) for i in range(SIDE)])  5.45 us
    pallas_call x1, Pallas kernels, experts(): pl.pallas_call(experts_kernel, out_shape=[jax.ShapeDtypeStruct((rows, wid...  4.7 us
    pallas_call x1, Pallas kernels, attention(): pl.pallas_call(attention_kernel, out_shape=jax.ShapeDtypeStruct((rows, wi...  2.7 us
    ppermute x3, waiting for transfers between devices, swap(): return lax.ppermute(block, 'c', SWAP)  2.52 us
  transfers between devices with their start and end apart: 6, of which 2 were waited for; matrix products, arithmetic and copies ran while one was open for 0% of the time, Pallas kernels for 12%

profile of v2, /device:TPU:0, one launch (start us, length us, event | category | flops | bytes accessed | tf_op | source)
XLA Modules:
  0.0 80.8 jit_solution(308559526235153579)
XLA Ops:
  0.0 2.7 %attention.1 = bf16[2,4096]{1,0:T(2,128)(2,1)S(1)} custom-call(s32[2]{0:T(128)} %len_hbm.1, bf16[2,4096]{1,0:T(2,128)(2,1)} %q_hbm.1, bf16[2,1024,256]{2,1,0:T(8,128)(2,1)} %k_hbm.1, bf16[2,1024,256]{2,1,0:T(8,128)(2,1)} %v_hbm.1), custom_call_target="tpu_custom_call" | custom-call | tf_op jit(solution)/shard_map/attention/pallas_call | solution.py:111
  2.7 0.1 collective-permute-start
  2.8 1.2 %collective-permute-done = bf16[2,4096]{1,0:T(2,128)(2,1)S(1)} collective-permute-done((bf16[2,4096]{1,0:T(2,128)(2,1)S(1)}, bf16[2,4096]{1,0:T(2,128)(2,1)S(1)}, u32[]{:S(2)}, u32[]{:S(2)}) %collective-permute-start) | collective-permute-done | bytes 16416 | tf_op jit(solution)/shard_map/ppermute | solution.py:47
  4.0 4.2 %collective-permute-start.3 = (bf16[4,4096]{1,0:T(4,128)(2,1)S(1)}, bf16[4,4096]{1,0:T(4,128)(2,1)S(1)}, u32[]{:S(2)}, u32[]{:S(2)}) collective-permute-start(bf16[4,4096]{1,0:T(4,128)(2,1)S(1)} %pad_maximum_fusion.refs_0_.a0), channel_id=1, source_target_pairs={{0,6},{2,0},{4,2},{6,4},{1,7},{3,1},{5,3},{7,5},{8,14},{10,8},{12,... | collective-permute-start | bytes 98312 | tf_op jit(solution)/shard_map/ppermute | solution.py:52
  8.2 0.0 collective-permute-start.2
  8.2 1.3 %collective-permute-start.1 = (bf16[4,4096]{1,0:T(4,128)(2,1)S(1)}, bf16[4,4096]{1,0:T(4,128)(2,1)S(1)}, u32[]{:S(2)}, u32[]{:S(2)}) collective-permute-start(bf16[4,4096]{1,0:T(4,128)(2,1)S(1)} %pad_maximum_fusion.refs_0_.a0), channel_id=1, source_target_pairs={{0,2},{2,4},{4,6},{6,0},{1,3},{3,5},{5,7},{7,1},{8,10},{10,12},{12... | collective-permute-start | bytes 98312 | tf_op jit(solution)/shard_map/ppermute | solution.py:52
  9.5 6.0 %fetch.2 = (bf16[4096,512]{1,0:T(8,128)(2,1)S(1)}, bf16[16,512]{1,0:T(8,128)(2,1)S(1)}, f32[1,512]{1,0:T(1,128)S(1)}, s32[8,16]{1,0:T(8,128)S(1)}, f32[8,16]{1,0...) custom-call(bf16[4,4096]{1,0:T(4,128)(2,1)S(1)} %pad_maximum_fusion.refs_0_.a0, ...), custom_call_target="tpu_custom_call" | custom-call | bytes 16796672 | tf_op jit(solution)/shard_map/fetch/pallas_call | solution.py:148
  15.5 0.0 collective-permute-done.3.a3
  15.5 0.0 collective-permute-done.2.a2
  15.5 0.0 collective-permute-done.1.a1
  15.5 1.0 %stream.1 = (bf16[16,512]{1,0:T(8,128)(2,1)S(1)}, bf16[64,72,128]{2,1,0:T(8,128)(2,1)S(1)}) custom-call(bf16[4,4096]{1,0:T(4,128)(2,1)S(1)} %pad_maximum_fusion.refs_0_.a0, bf16[4,4096]{1,0:T(4,128)(2,1)S(1)} %collective-permute-done.1.a1, bf16[4,4096]{1,0:T(4,128)(2,1)S(1)} %collective-permute-done.2.a2, bf16[4,4096]{1,0:T(4,128)(2,1)S(1)} %collective-permute-done.3.a3, ...), custom_call_target="tpu_custom_call" | custom-call | tf_op jit(solution)/shard_map/stream/pallas_call | solution.py:209
  16.5 29.3 %all_to_all.10.refs_0_.own_ref = bf16[64,72,128]{2,1,0:T(8,128)(2,1)S(1)} all-to-all(bf16[64,72,128]{2,1,0:T(8,128)(2,1)S(1)} %get-tuple-element.22), channel_id=1, replica_groups=mesh['x'=4,'y'=4,'z'=4,'c'=2] {'x','y','z'}, dimensions={0} | all-to-all | bytes 2359296 | tf_op jit(solution)/shard_map/all_to_all | solution.py:322
  45.8 0.0 collective-permute-start.4
  45.8 2.8 %fetch.3.down_ref = bf16[768,4096]{1,0:T(8,128)(2,1)S(1)} custom-call(bf16[64,72,128]{2,1,0:T(8,128)(2,1)S(1)} %all_to_all.10.refs_0_.own_ref, bf16[768,4096]{1,0:T(8,128)(2,1)} %bitcast.12), custom_call_target="tpu_custom_call" | custom-call | bytes 6291456 | tf_op jit(solution)/shard_map/fetch/pallas_call | solution.py:148
  48.6 0.0 collective-permute-done.4.other_ref
  48.6 4.7 %experts.1 = (bf16[256,768]{1,0:T(8,128)(2,1)S(1)}, bf16[64,16,512]{2,1,0:T(8,128)(2,1)S(1)}) custom-call(bf16[64,72,128]{2,1,0:T(8,128)(2,1)S(1)} %all_to_all.10.refs_0_.own_ref, bf16[64,72,128]{2,1,0:T(8,128)(2,1)S(1)} %collective-permute-done.4.other_ref, bf16[768,4096]{1,0:T(8,128)(2,1)S(1)} %get-tuple-element.23.gate_ref, ...), custom_call_target="tpu_custom_call" | custom-call | flops 4026531840 | bytes 18874368 | tf_op jit(solution)/shard_map/experts/pallas_call | solution.py:285
  53.3 0.5 collective-permute-start.5
  53.8 1.0 %down_own.1 = bf16[64,16,512]{2,1,0:T(8,128)(2,1)S(1)} custom-call(bf16[256,768]{1,0:T(8,128)(2,1)S(1)} %get-tuple-element.25.hidden_ref, bf16[768,4096]{1,0:T(8,128)(2,1)S(1)} %fetch.3.down_ref), custom_call_target="tpu_custom_call" | custom-call | flops 805306368 | bytes 6291456 | tf_op jit(solution)/shard_map/down_own/pallas_call | solution.py:308
  54.8 1.3 %collective-permute-done.5 = bf16[64,16,512]{2,1,0:T(8,128)(2,1)S(1)} collective-permute-done((bf16[64,16,512]{2,1,0:T(8,128)(2,1)S(1)}, bf16[64,16,512]{2,1,0:T(8,128)(2,1)S(1)}, u32[]{:S(2)}, u32[]{:S(2)}) %collective-permute-start.5) | collective-permute-done | bytes 1048608 | tf_op jit(solution)/shard_map/ppermute | solution.py:47
  56.1 0.4 add_convert_fusion
  56.5 23.5 %all_to_all.11 = bf16[64,16,512]{2,1,0:T(8,128)(2,1)S(1)} all-to-all(bf16[64,16,512]{2,1,0:T(8,128)(2,1)S(1)} %add_convert_fusion), channel_id=1, replica_groups=mesh['x'=4,'y'=4,'z'=4,'c'=2] {'x','y','z'}, dimensions={0} | all-to-all | bytes 2097152 | tf_op jit(solution)/shard_map/all_to_all | solution.py:322
  80.0 0.2 convert_reduce_fusion
  80.2 0.6 add_convert_fusion.1
  (1 shorter events, 0.0 us)
Async XLA Ops:
  2.7 1.3 %collective-permute-start = (bf16[2,4096]{1,0:T(2,128)(2,1)S(1)}, bf16[2,4096]{1,0:T(2,128)(2,1)S(1)}, u32[]{:S(2)}, u32[]{:S(2)}) collective-permute-start(bf16[2,4096]{1,0:T(2,128)(2,1)S(1)} %attention.1), channel_id=1, source_target_pairs={{0,1},{1,0},{2,3},{3,2},{4,5},{5,4},{6,7},{7,6},{8,9},{9,8},{10,11... | collective-permute-start | bytes 49160 | tf_op jit(solution)/shard_map/ppermute | solution.py:47
  4.0 11.4 %collective-permute-start.3 = (bf16[4,4096]{1,0:T(4,128)(2,1)S(1)}, bf16[4,4096]{1,0:T(4,128)(2,1)S(1)}, u32[]{:S(2)}, u32[]{:S(2)}) collective-permute-start(bf16[4,4096]{1,0:T(4,128)(2,1)S(1)} %pad_maximum_fusion.refs_0_.a0), channel_id=1, source_target_pairs={{0,6},{2,0},{4,2},{6,4},{1,7},{3,1},{5,3},{7,5},{8,14},{10,8},{12,... | collective-permute-start | bytes 98312 | tf_op jit(solution)/shard_map/ppermute | solution.py:52
  8.2 7.3 %collective-permute-start.2 = (bf16[4,4096]{1,0:T(4,128)(2,1)S(1)}, bf16[4,4096]{1,0:T(4,128)(2,1)S(1)}, u32[]{:S(2)}, u32[]{:S(2)}) collective-permute-start(bf16[4,4096]{1,0:T(4,128)(2,1)S(1)} %pad_maximum_fusion.refs_0_.a0), channel_id=1, source_target_pairs={{0,4},{2,6},{4,0},{6,2},{1,5},{3,7},{5,1},{7,3},{8,12},{10,14},{12... | collective-permute-start | bytes 98312 | tf_op jit(solution)/shard_map/ppermute | solution.py:52
  8.2 7.3 %collective-permute-start.1 = (bf16[4,4096]{1,0:T(4,128)(2,1)S(1)}, bf16[4,4096]{1,0:T(4,128)(2,1)S(1)}, u32[]{:S(2)}, u32[]{:S(2)}) collective-permute-start(bf16[4,4096]{1,0:T(4,128)(2,1)S(1)} %pad_maximum_fusion.refs_0_.a0), channel_id=1, source_target_pairs={{0,2},{2,4},{4,6},{6,0},{1,3},{3,5},{5,7},{7,1},{8,10},{10,12},{12... | collective-permute-start | bytes 98312 | tf_op jit(solution)/shard_map/ppermute | solution.py:52
  45.8 2.8 %collective-permute-start.4 = (bf16[64,72,128]{2,1,0:T(8,128)(2,1)S(1)}, bf16[64,72,128]{2,1,0:T(8,128)(2,1)S(1)}, u32[]{:S(2)}, u32[]{:S(2)}) collective-permute-start(bf16[64,72,128]{2,1,0:T(8,128)(2,1)S(1)} %all_to_all.10.refs_0_.own_ref), channel_id=1, source_target_pairs={{0,1},{1,0},{2,3},{3,2},{4,5},{5,4},{6,7},{7,6},{8,9},{9,8},{10,11... | collective-permute-start | bytes 3538952 | tf_op jit(solution)/shard_map/ppermute | solution.py:47
  53.3 2.8 %collective-permute-start.5 = (bf16[64,16,512]{2,1,0:T(8,128)(2,1)S(1)}, bf16[64,16,512]{2,1,0:T(8,128)(2,1)S(1)}, u32[]{:S(2)}, u32[]{:S(2)}) collective-permute-start(bf16[64,16,512]{2,1,0:T(8,128)(2,1)S(1)} %get-tuple-element.26), channel_id=1, source_target_pairs={{0,1},{1,0},{2,3},{3,2},{4,5},{5,4},{6,7},{7,6},{8,9},{9,8},{10,11... | collective-permute-start | bytes 3145736 | tf_op jit(solution)/shard_map/ppermute | solution.py:47

commit v3 on v2

--- a/solution.py
+++ b/solution.py
@@ -1,3 +1,4 @@
+import functools
 import math
 
 import jax
@@ -55,7 +56,7 @@
 
 
 def attention_kernel(
-    len_hbm, q_hbm, k_hbm, v_hbm, out_ref, lens, q_ref, k_ref, v_ref, q_rows, out_rows, sems
+    len_hbm, q_hbm, k_hbm, v_hbm, w_hbm, out_ref, w_ref, lens, q_ref, k_ref, v_ref, q_rows, out_rows, sems
 ):
     rows, width = q_ref.shape
     positions = k_ref.shape[1]
@@ -75,6 +76,8 @@
     for r in range(rows):
         k_copies[r].start()
         v_copies[r].start()
+    w_copy = pltpu.make_async_copy(w_hbm, w_ref, sems.at[2 + 2 * rows])
+    w_copy.start()
     q_copy.wait()
     queries = q_ref[...].astype(F32)
     for r in range(rows):
@@ -104,15 +107,16 @@
                 h = g * per_group + j
                 out_rows[r : r + 1, h * HEAD : (h + 1) * HEAD] = summed[j : j + 1, :]
     out_ref[...] = out_rows[...].astype(BF16)
-
-
-def attention(lengths, queries, keys, values):
+    w_copy.wait()
+
+
+def attention(lengths, queries, keys, values, out_proj):
     rows, width = queries.shape
     return pl.pallas_call(
         attention_kernel,
-        out_shape=jax.ShapeDtypeStruct((rows, width), BF16),
-        in_specs=[ANY] * 4,
-        out_specs=VMEM,
+        out_shape=[jax.ShapeDtypeStruct((rows, width), BF16), pltpu.VMEM(out_proj.shape, BF16)],
+        in_specs=[ANY] * 5,
+        out_specs=[VMEM] * 2,
         scratch_shapes=[
             pltpu.SMEM(lengths.shape, jnp.int32),
             pltpu.VMEM((rows, width), BF16),
@@ -120,11 +124,28 @@
             pltpu.VMEM(values.shape, BF16),
             pltpu.VMEM((rows * width // HEAD, HEAD), F32),
             pltpu.VMEM((rows, width), F32),
-            pltpu.SemaphoreType.DMA((2 + 2 * rows,)),
+            pltpu.SemaphoreType.DMA((3 + 2 * rows,)),
         ],
         compiler_params=params(16),
         name="attention",
-    )(*map(in_hbm, (lengths, queries, keys, values)))
+    )(*map(in_hbm, (lengths, queries, keys, values, out_proj)))
+
+
+def join_kernel(a_ref, b_ref, out_ref):
+    rows = a_ref.shape[0]
+    out_ref[:rows] = a_ref[...]
+    out_ref[rows:] = b_ref[...]
+
+
+def join(a, b):
+    return pl.pallas_call(
+        join_kernel,
+        out_shape=jax.ShapeDtypeStruct((a.shape[0] + b.shape[0],) + a.shape[1:], a.dtype),
+        in_specs=[VMEM] * 2,
+        out_specs=VMEM,
+        compiler_params=params(1),
+        name="join",
+    )(a, b)
 
 
 def in_hbm(value):
@@ -220,10 +241,6 @@
     )(*parts, out_proj, residual, gain, ids, weights)
 
 
-def column_block(z, c):
-    return pl.ds(pl.multiple_of((z * CORES + c) * COLS, COLS), COLS)
-
-
 def to_columns(lines, start):
     shape = (PLACES, ROWS, LANES)
     lane = lax.broadcasted_iota(jnp.int32, shape, 2)
@@ -232,90 +249,188 @@
     return jnp.sum(kept, axis=2, keepdims=True).reshape(PLACES * ROWS, 1)
 
 
-def down_half(hidden, down_ref, out_ref, c):
-    for z in range(SIDE):
-        part = jnp.dot(
-            hidden, down_ref[:, column_block(z, c)], preferred_element_type=F32
-        ).astype(BF16)
-        for s in range(PLACES):
-            out_ref[s * SIDE + z] = part[s * ROWS : (s + 1) * ROWS]
-
-
-def experts_kernel(own_ref, other_ref, gate_ref, up_ref, down_ref, hidden_ref, out_ref, x_ref):
-    c = lax.axis_index("c")
-    local = gate_ref.shape[0] // EXPERT_COLS
-    first = (lax.axis_index("x") * SIDE + lax.axis_index("y")) * local
+def gather_rows(units_ref, x_ref):
     for s in range(PLACES):
         for z in range(SIDE):
-            for half, parity in ((own_ref, c), (other_ref, 1 - c)):
-                start = pl.multiple_of((z * CORES + parity) * COLS, COLS)
-                for j in range(CHUNKS):
-                    x_ref[s * ROWS : (s + 1) * ROWS, pl.ds(start + j * LANES, LANES)] = half[
-                        s * SIDE + z, j * ROWS : (j + 1) * ROWS, :
-                    ]
-    squares = jnp.zeros((PLACES, 1, LANES), F32)
-    for s_ref in (own_ref, other_ref):
-        extras = s_ref[:, UNIT:, :].astype(F32).reshape(PLACES, SIDE, EXTRA, LANES)
-        for z in range(SIDE):
-            squares += jnp.sum(extras[:, z, :3, :], axis=1, keepdims=True)
-    scale = lax.rsqrt(to_columns(squares, SQ) / D + 1e-06)
+            for j in range(CHUNKS):
+                start = z * COLS + j * LANES
+                x_ref[s * ROWS : (s + 1) * ROWS, start : start + LANES] = units_ref[
+                    s * SIDE + z, j * ROWS : (j + 1) * ROWS, :
+                ]
+
+
+def columns_of(z, parity):
+    return pl.ds(pl.multiple_of((z * CORES + parity) * COLS, COLS), COLS)
+
+
+def products(x_ref, w_ref, parity, first=0, count=None):
+    count = count or w_ref.shape[0]
+    total = None
+    for z in range(SIDE):
+        part = lax.dot_general(
+            x_ref[:, z * COLS : (z + 1) * COLS],
+            w_ref[first : first + count, columns_of(z, parity)],
+            NT,
+            preferred_element_type=F32,
+        )
+        total = part if total is None else total + part
+    return total
+
+
+def squares_of(units):
+    extras = units[:, UNIT : UNIT + 3, :].astype(F32)
+    extras = jnp.sum(extras, axis=1, keepdims=True).reshape(PLACES, SIDE, 1, LANES)
+    return sum(extras[:, z] for z in range(SIDE))
+
+
+def own_kernel(own_ref, gate_ref, up_ref, down_ref, gate_sum, up_sum, mix_ref, squares_ref, x_ref):
+    c = lax.axis_index("c")
+    gather_rows(own_ref, x_ref)
+    squares_ref[...] = squares_of(own_ref)
     routes = jnp.stack([own_ref[s * SIDE, UNIT:, :] for s in range(PLACES)]).astype(F32)
     weights = (
         pltpu.roll(routes, LANES - HI, 2)
         + pltpu.roll(routes, LANES - MID, 2)
         + pltpu.roll(routes, LANES - LO, 2)
     )
-    x = x_ref[...]
-    gate = lax.dot_general(x, gate_ref[...], NT, preferred_element_type=F32) * scale
-    up = lax.dot_general(x, up_ref[...], NT, preferred_element_type=F32) * scale
-    column = lax.broadcasted_iota(jnp.int32, gate.shape, 1)
+    local = gate_ref.shape[0] // EXPERT_COLS
+    first = (lax.axis_index("x") * SIDE + lax.axis_index("y")) * local
+    column = lax.broadcasted_iota(jnp.int32, mix_ref.shape, 1)
     mix = None
     for e in range(local):
         mine = jnp.where(routes == (first + e).astype(F32), weights, 0.0)
         one = to_columns(jnp.sum(mine, axis=1, keepdims=True), IDS)
         mix = one if mix is None else jnp.where(column < e * EXPERT_COLS, mix, one)
-    hidden = (gate / (1.0 + jnp.exp(-gate)) * up * mix).astype(BF16)
-    hidden_ref[...] = hidden
-    down_half(hidden, down_ref, out_ref, 1 - c)
-
-
-def experts(own, other, gate, up, down):
+    mix_ref[...] = mix
+    gate_sum[...] = products(x_ref, gate_ref, c)
+    up_sum[...] = products(x_ref, up_ref, c)
+
+
+def own_part(own, gate, up, down):
     rows = PLACES * ROWS
     width = gate.shape[0]
     return pl.pallas_call(
-        experts_kernel,
-        out_shape=[
-            jax.ShapeDtypeStruct((rows, width), BF16),
-            jax.ShapeDtypeStruct((PLACES * SIDE, ROWS, COLS), BF16),
-        ],
-        in_specs=[VMEM] * 5,
-        out_specs=[VMEM, VMEM],
-        scratch_shapes=[pltpu.VMEM((rows, D), BF16)],
-        compiler_params=params(20),
-        cost_estimate=pl.CostEstimate(
-            flops=5 * rows * width * D, bytes_accessed=6 * width * D, transcendentals=rows * width
-        ),
-        name="experts",
-    )(own, other, gate, up, down)
-
-
-def down_kernel(hidden_ref, down_ref, out_ref):
-    down_half(hidden_ref[...], down_ref, out_ref, lax.axis_index("c"))
-
-
-def down_own(hidden, down):
-    rows, width = hidden.shape
-    return pl.pallas_call(
-        down_kernel,
-        out_shape=jax.ShapeDtypeStruct((PLACES * SIDE, ROWS, COLS), BF16),
+        own_kernel,
+        out_shape=[jax.ShapeDtypeStruct((rows, width), F32)] * 3
+        + [jax.ShapeDtypeStruct((PLACES, 1, LANES), F32)],
+        in_specs=[VMEM] * 4,
+        out_specs=[VMEM] * 4,
+        scratch_shapes=[pltpu.VMEM((rows, D // CORES), BF16)],
+        compiler_params=params(8),
+        name="own_part",
+    )(own, gate, up, down)
+
+
+PARTS = 3
+
+
+def hidden_kernel(
+    other_ref, gate_ref, up_ref, gate_in, up_in, mix_ref, squares_ref, down_ref, hidden_ref, out_ref, x_ref
+):
+    other = 1 - lax.axis_index("c")
+    gather_rows(other_ref, x_ref)
+    scale = lax.rsqrt(to_columns(squares_ref[...] + squares_of(other_ref), SQ) / D + 1e-06)
+    width = hidden_ref.shape[1] // PARTS
+    for i in range(PARTS):
+        first = i * width
+        part = slice(first, first + width)
+        half = (gate_in[:, part] + products(x_ref, gate_ref, other, first, width)) * (0.5 * scale)
+        up = (up_in[:, part] + products(x_ref, up_ref, other, first, width)) * scale
+        hidden_ref[:, part] = ((half + half * jnp.tanh(half)) * up * mix_ref[:, part]).astype(BF16)
+    down_part(hidden_ref, down_ref, other, out_ref, 0)
+
+
+def down_part(hidden_ref, down_ref, parity, out_ref, first):
+    for z in range(out_ref.shape[1]):
+        part = jnp.dot(
+            hidden_ref[...],
+            down_ref[:, columns_of(first + z, parity)],
+            preferred_element_type=F32,
+        ).astype(BF16)
+        for s in range(PLACES):
+            out_ref[s, z] = part[s * ROWS : (s + 1) * ROWS]
+
+
+HALF = SIDE // 2
+
+
+def blocks(count):
+    return jax.ShapeDtypeStruct((PLACES, count, ROWS, COLS), BF16)
+
+
+def make_hidden(other, gate, up, sums, down):
+    rows = PLACES * ROWS
+    width = gate.shape[0]
+    return pl.pallas_call(
+        hidden_kernel,
+        out_shape=[jax.ShapeDtypeStruct((rows, width), BF16), blocks(HALF)],
+        in_specs=[VMEM] * 8,
+        out_specs=[VMEM] * 2,
+        scratch_shapes=[pltpu.VMEM((rows, D // CORES), BF16)],
+        compiler_params=params(12),
+        name="hidden",
+    )(other, gate, up, *sums, down)
+
+
+def down_kernel(mine, hidden_ref, down_ref, out_ref):
+    c = lax.axis_index("c")
+    if mine:
+        down_part(hidden_ref, down_ref, c, out_ref, 0)
+    else:
+        down_part(hidden_ref, down_ref, 1 - c, out_ref, HALF)
+
+
+def down_blocks(mine, hidden, down):
+    count = SIDE if mine else HALF
+    return pl.pallas_call(
+        functools.partial(down_kernel, mine),
+        out_shape=blocks(count),
         in_specs=[VMEM, VMEM],
         out_specs=VMEM,
-        compiler_params=params(20),
-        cost_estimate=pl.CostEstimate(
-            flops=rows * width * D, bytes_accessed=2 * width * D, transcendentals=0
-        ),
-        name="down_own",
+        compiler_params=params(4),
+        cost_estimate=pl.CostEstimate(flops=1, bytes_accessed=1, transcendentals=0),
+        name="down_mine" if mine else "down_theirs",
     )(hidden, down)
+
+
+def add_kernel(mine_ref, first_ref, second_ref, out_ref):
+    for i, came_ref in enumerate((first_ref, second_ref)):
+        zs = slice(i * HALF, (i + 1) * HALF)
+        total = mine_ref[:, zs].astype(F32) + came_ref[...].astype(F32)
+        out_ref[:, zs] = total.astype(BF16)
+
+
+def add(mine, first, second):
+    return pl.pallas_call(
+        add_kernel,
+        out_shape=blocks(SIDE),
+        in_specs=[VMEM] * 3,
+        out_specs=VMEM,
+        compiler_params=params(4),
+        name="add",
+    )(mine, first, second)
+
+
+def finish_kernel(parts_ref, stream_ref, out_hbm, out_ref, sem):
+    total = stream_ref[...].astype(F32)
+    for i in range(parts_ref.shape[0]):
+        total += parts_ref[i].astype(F32)
+    out_ref[...] = total.astype(BF16)
+    copy = pltpu.make_async_copy(out_ref, out_hbm, sem)
+    copy.start()
+    copy.wait()
+
+
+def finish(parts, stream):
+    return pl.pallas_call(
+        finish_kernel,
+        out_shape=jax.ShapeDtypeStruct(stream.shape, BF16),
+        in_specs=[VMEM] * 2,
+        out_specs=ANY,
+        scratch_shapes=[pltpu.VMEM(stream.shape, BF16), pltpu.SemaphoreType.DMA],
+        compiler_params=params(4),
+        name="finish",
+    )(parts, stream)
 
 
 def exchange(blocks):
@@ -339,22 +454,22 @@
     gate = jnp.swapaxes(w_gate, 1, 2).reshape(-1, D)
     up = jnp.swapaxes(w_up, 1, 2).reshape(-1, D)
     down = w_down.reshape(-1, D)
-    attended = attention(lengths, queries, key_cache, value_cache)
-    pair = jnp.concatenate([attended, swap(attended)], axis=0)
+    attended, out_proj = attention(lengths, queries, key_cache, value_cache, out_proj)
+    pair = join(attended, swap(attended))
     parts = spread_z(pair)
-    out_proj, residual, gain, ids, weights, gate, up = fetch(
-        pair, out_proj, residual, norm_gain[None, :], expert_ids.T, route_weights.T, gate, up
+    residual, gain, ids, weights, gate = fetch(
+        pair, residual, norm_gain[None, :], expert_ids.T, route_weights.T, gate
     )
     stream, units = make_stream(parts, out_proj, residual, gain, ids, weights)
     own = exchange(units)
     other = swap(own)
-    (down,) = fetch(own, down)
-    hidden, theirs = experts(own, other, gate, up, down)
-    came = swap(theirs)
-    mine = down_own(hidden, down)
-    total = (mine.astype(F32) + came.astype(F32)).astype(BF16)
-    combined = jnp.sum(exchange(total).astype(F32), axis=0)
-    return (stream.astype(F32) + combined).astype(BF16)
+    sums = own_part(own, gate, up, down)
+    hidden, theirs = make_hidden(other, gate, up, sums, down)
+    first = swap(theirs)
+    second = swap(down_blocks(False, hidden, down))
+    mine = down_blocks(True, hidden, down)
+    total = add(mine, first, second).reshape(PLACES * SIDE, ROWS, COLS)
+    return finish(exchange(total), stream)
 
 
 def solution(mesh):

time: 81 us -> 76.1 us (0.940)
  Pallas kernels: 18.1 us -> 14 us
  waiting for transfers between devices: 2.52 us -> 4.38 us
  blocking collectives: 52.8 us -> 51.3 us
  other arithmetic: 1.22 us -> 0.01 us
    pallas_call x2 -> x1, Pallas kernels: 8.77 us -> 3.04 us  [fetch(): pl.pallas_call(fetch_kernel, out_shape=[pltpu.VMEM(a.shape, a.dtype) for...]
    pallas_call x3 -> x8, Pallas kernels: 8.38 us -> 10 us  [the longest x1 3.05 us: attention(): pl.pallas_call(attention_kernel, out_shape=[jax.ShapeDtypeStruct((rows, w...]
    all_to_all x2, blocking collectives: 52.8 us -> 51.3 us  [exchange(): lax.all_to_all(blocks, ('x', 'y', 'z'), split_axis=0, concat_axis=0, tile...]
    ppermute x3, waiting for transfers between devices: 0.01 us -> 1.15 us  [spread_z(): lax.ppermute(block, 'z', [(i, (i + k) % SIDE) for i in range(SIDE)])]
    convert_element_type x2 -> x0, other arithmetic: 1.01 us -> none  [the longest x1 0.61 us: on_device(): return (stream.astype(F32) + combined).astype(BF16)]
    ppermute x3 -> x4, waiting for transfers between devices: 2.52 us -> 3.23 us  [swap(): return lax.ppermute(block, 'c', SWAP)]
  transfers between devices with their start and end apart: 6 -> 7, of which waited for: 2 -> 5; matrix products, arithmetic and copies ran while one was open for 0% -> 0% of each run, Pallas kernels for 12% -> 8%
where the time goes in v3:
time: 76.1 us; the launch traced here: 76 us
  blocking collectives  51.3 us (67%)
  Pallas kernels  14 us (18%)
  starting transfers between devices  6.13 us (8%)
  waiting for transfers between devices  4.38 us (6%)
    all_to_all x2, blocking collectives, exchange(): lax.all_to_all(blocks, ('x', 'y', 'z'), split_axis=0, concat_axis=0, tile...  51.3 us
    ppermute x3, starting transfers between devices, spread_z(): lax.ppermute(block, 'z', [(i, (i + k) % SIDE) for i in range(SIDE)])  5.45 us
    ppermute x4, waiting for transfers between devices, swap(): return lax.ppermute(block, 'c', SWAP)  3.23 us
    pallas_call x1, Pallas kernels, attention(): pl.pallas_call(attention_kernel, out_shape=[jax.ShapeDtypeStruct((rows, w...  3.05 us
    pallas_call x1, Pallas kernels, fetch(): pl.pallas_call(fetch_kernel, out_shape=[pltpu.VMEM(a.shape, a.dtype) for...  3.04 us
    pallas_call x1, Pallas kernels, make_hidden(): pl.pallas_call(hidden_kernel, out_shape=[jax.ShapeDtypeStruct((rows, widt...  2.45 us
    pallas_call x1, Pallas kernels, own_part(): pl.pallas_call(own_kernel, out_shape=[jax.ShapeDtypeStruct((rows, width),...  1.9 us
    pallas_call x2, Pallas kernels, down_blocks(): pl.pallas_call(functools.partial(down_kernel, mine), out_shape=blocks(cou...  1.58 us
  transfers between devices with their start and end apart: 7, of which 5 were waited for; matrix products, arithmetic and copies ran while one was open for 0% of the time, Pallas kernels for 8%

profile of v3, /device:TPU:0, one launch (start us, length us, event | category | flops | bytes accessed | tf_op | source)
XLA Modules:
  0.0 76.0 jit_solution(2320030853728859380)
XLA Ops:
  0.0 0.0 slice-start
  0.0 0.0 slice-start.2
  0.0 3.0 %attention.1 = (bf16[2,4096]{1,0:T(2,128)(2,1)S(1)}, bf16[4096,512]{1,0:T(8,128)(2,1)S(1)}) custom-call(s32[2]{0:T(128)} %len_hbm.1, bf16[2,4096]{1,0:T(2,128)(2,1)} %q_hbm.1, bf16[2,1024,256]{2,1,0:T(8,128)(2,1)} %k_hbm.1, bf16[2,1024,256]{2,1,0:T(8,128)(2,1)} %v_hbm.1, bf16[4096,512]{1,0:T(8,128)(2,1)} %w_hbm.1), custom_call_target="tpu_custom_call" | custom-call | tf_op jit(solution)/shard_map/attention/pallas_call | solution.py:115
  3.1 0.1 collective-permute-start
  3.2 1.2 %collective-permute-done.b_ref = bf16[2,4096]{1,0:T(2,128)(2,1)S(1)} collective-permute-done((bf16[2,4096]{1,0:T(2,128)(2,1)S(1)}, bf16[2,4096]{1,0:T(2,128)(2,1)S(1)}, u32[]{:S(2)}, u32[]{:S(2)}) %collective-permute-start) | collective-permute-done | bytes 16416 | tf_op jit(solution)/shard_map/ppermute | solution.py:48
  4.3 4.2 %collective-permute-start.3 = (bf16[4,4096]{1,0:T(4,128)(2,1)S(1)}, bf16[4,4096]{1,0:T(4,128)(2,1)S(1)}, u32[]{:S(2)}, u32[]{:S(2)}) collective-permute-start(bf16[4,4096]{1,0:T(4,128)(2,1)S(1)} %join.1.refs_0_.a0), channel_id=1, source_target_pairs={{0,6},{2,0},{4,2},{6,4},{1,7},{3,1},{5,3},{7,5},{8,14},{10,8},{12,... | collective-permute-start | bytes 98312 | tf_op jit(solution)/shard_map/ppermute | solution.py:53
  8.5 0.0 collective-permute-start.2
  8.5 1.3 %collective-permute-start.1 = (bf16[4,4096]{1,0:T(4,128)(2,1)S(1)}, bf16[4,4096]{1,0:T(4,128)(2,1)S(1)}, u32[]{:S(2)}, u32[]{:S(2)}) collective-permute-start(bf16[4,4096]{1,0:T(4,128)(2,1)S(1)} %join.1.refs_0_.a0), channel_id=1, source_target_pairs={{0,2},{2,4},{4,6},{6,0},{1,3},{3,5},{5,7},{7,1},{8,10},{10,12},{12... | collective-permute-start | bytes 98312 | tf_op jit(solution)/shard_map/ppermute | solution.py:53
  9.8 0.0 slice-start.1
  9.8 0.0 slice-start.3
  9.8 3.0 %fetch.1 = (bf16[16,512]{1,0:T(8,128)(2,1)S(1)}, f32[1,512]{1,0:T(1,128)S(1)}, s32[8,16]{1,0:T(8,128)S(1)}, f32[8,16]{1,0:T(8,128)S(1)}, bf16[768,4096]{1,0:T(8,128)(2,1)S(1)}) custom-call(bf16[4,4096]{1,0:T(4,128)(2,1)S(1)} %join.1.refs_0_.a0, bf16[16,512]{1,0:T(8,128)(2,1)} %refs_1_.1, f32[1,512]{1,0:T(1,128)} %bitcast.25, s32[8,16]{1,0:T(8,128)} %bitcast.23, ...), custom_call_target="tpu_custom_call" | custom-call | bytes 6310912 | tf_op jit(solution)/shard_map/fetch/pallas_call | solution.py:169
  12.8 0.0 collective-permute-done.3.a3
  12.9 1.1 %collective-permute-done.2.a2 = bf16[4,4096]{1,0:T(4,128)(2,1)S(1)} collective-permute-done((bf16[4,4096]{1,0:T(4,128)(2,1)S(1)}, bf16[4,4096]{1,0:T(4,128)(2,1)S(1)}, u32[]{:S(2)}, u32[]{:S(2)}) %collective-permute-start.2) | collective-permute-done | bytes 32800 | tf_op jit(solution)/shard_map/ppermute | solution.py:53
  14.0 0.0 collective-permute-done.1.a1
  14.0 0.9 %stream.1 = (bf16[16,512]{1,0:T(8,128)(2,1)S(1)}, bf16[64,72,128]{2,1,0:T(8,128)(2,1)S(1)}) custom-call(bf16[4,4096]{1,0:T(4,128)(2,1)S(1)} %join.1.refs_0_.a0, bf16[4,4096]{1,0:T(4,128)(2,1)S(1)} %collective-permute-done.1.a1, bf16[4,4096]{1,0:T(4,128)(2,1)S(1)} %collective-permute-done.2.a2, bf16[4,4096]{1,0:T(4,128)(2,1)S(1)} %collective-permute-done.3.a3, ...), custom_call_target="tpu_custom_call" | custom-call | tf_op jit(solution)/shard_map/stream/pallas_call | solution.py:230
  15.0 28.2 %all_to_all.10.own_ref = bf16[64,72,128]{2,1,0:T(8,128)(2,1)S(1)} all-to-all(bf16[64,72,128]{2,1,0:T(8,128)(2,1)S(1)} %get-tuple-element.26), channel_id=1, replica_groups=mesh['x'=4,'y'=4,'z'=4,'c'=2] {'x','y','z'}, dimensions={0} | all-to-all | bytes 2359296 | tf_op jit(solution)/shard_map/all_to_all | solution.py:437
  43.1 0.0 collective-permute-start.4
  43.1 0.0 slice-done
  43.1 0.0 slice-done.2
  43.1 0.0 slice-done.1
  43.2 0.0 slice-done.3
  43.2 1.9 %own_part.1 = (f32[256,768]{1,0:T(8,128)S(1)}, f32[256,768]{1,0:T(8,128)S(1)}, f32[256,768]{1,0:T(8,128)S(1)}, f32[16,1,128]{2,1,0:T(1,128)S(1)}) custom-call(bf16[64,72,128]{2,1,0:T(8,128)(2,1)S(1)} %all_to_all.10.own_ref, bf16[768,4096]{1,0:T(8,128)(2,1)S(1)} %get-tuple-element.27.gate_ref, bf16[768,4096]{1,0:T(8,128)(2,1)S(1)} %bitcast.19, ...), custom_call_target="tpu_custom_call" | custom-call | tf_op jit(solution)/shard_map/own_part/pallas_call | solution.py:312
  45.1 0.9 %collective-permute-done.4.other_ref = bf16[64,72,128]{2,1,0:T(8,128)(2,1)S(1)} collective-permute-done((bf16[64,72,128]{2,1,0:T(8,128)(2,1)S(1)}, bf16[64,72,128]{2,1,0:T(8,128)(2,1)S(1)}, u32[]{:S(2)}, u32[]{:S(2)}) %collective-permute-start.4) | collective-permute-done | bytes 1179680 | tf_op jit(solution)/shard_map/ppermute | solution.py:48
  46.0 2.4 %hidden.1 = (bf16[256,768]{1,0:T(8,128)(2,1)S(1)}, bf16[16,2,16,512]{3,2,1,0:T(8,128)(2,1)S(1)}) custom-call(bf16[64,72,128]{2,1,0:T(8,128)(2,1)S(1)} %collective-permute-done.4.other_ref, bf16[768,4096]{1,0:T(8,128)(2,1)S(1)} %get-tuple-element.27.gate_ref, bf16[768,4096]{1,0:T(8,128)(2,1)S(1)} %bitcast.20, f32[256,768]{1,0:T(8,128)S(1)} %get-tuple-element.28.gate_in, ...), custom_call_target="tpu_custom_call" | custom-call | tf_op jit(solution)/shard_map/hidden/pallas_call | solution.py:364
  48.4 0.6 down_theirs.1
  49.0 0.2 collective-permute-start.6
  49.2 0.4 collective-permute-start.5
  49.6 1.0 %down_mine.1.mine_ref = bf16[16,4,16,512]{3,2,1,0:T(8,128)(2,1)S(1)} custom-call(bf16[256,768]{1,0:T(8,128)(2,1)S(1)} %get-tuple-element.32.hidden_ref, bf16[768,4096]{1,0:T(8,128)(2,1)S(1)} %bitcast.16), custom_call_target="tpu_custom_call" | custom-call | flops 1 | bytes 1 | tf_op jit(solution)/shard_map/down_mine/pallas_call | solution.py:385
  50.6 0.4 collective-permute-done.6.second_ref
  51.0 0.7 collective-permute-done.5.first_ref
  51.8 0.2 add.1
  52.0 23.2 %all_to_all.11.parts_ref = bf16[64,16,512]{2,1,0:T(8,128)(2,1)S(1)} all-to-all(bf16[64,16,512]{2,1,0:T(8,128)(2,1)S(1)} %bitcast.21), channel_id=1, replica_groups=mesh['x'=4,'y'=4,'z'=4,'c'=2] {'x','y','z'}, dimensions={0} | all-to-all | bytes 2097152 | tf_op jit(solution)/shard_map/all_to_all | solution.py:437
  75.2 0.8 %finish.1 = bf16[16,512]{1,0:T(8,128)(2,1)} custom-call(bf16[64,16,512]{2,1,0:T(8,128)(2,1)S(1)} %all_to_all.11.parts_ref, bf16[16,512]{1,0:T(8,128)(2,1)S(1)} %get-tuple-element.34.stream_ref), custom_call_target="tpu_custom_call" | custom-call | tf_op jit(solution)/shard_map/finish/pallas_call | solution.py:425
  (3 shorter events, 0.0 us)
Async XLA Ops:
  0.0 43.1 %slice-start = ((s8[6291456]{0:T(1024)(128)(4,1)}), s8[4194304]{0:T(1024)(128)(4,1)S(1)}, s32[]{:S(2)}) async-start(s8[6291456]{0:T(1024)(128)(4,1)} %bitcast.11), calls=%async_computation.2 | async-start | bytes 8388608
  0.0 43.1 %slice-start.2 = ((s8[6291456]{0:T(1024)(128)(4,1)}), s8[4194304]{0:T(1024)(128)(4,1)S(1)}, s32[]{:S(2)}) async-start(s8[6291456]{0:T(1024)(128)(4,1)} %bitcast.17), calls=%async_computation.4 | async-start | bytes 8388608
  3.1 1.3 %collective-permute-start = (bf16[2,4096]{1,0:T(2,128)(2,1)S(1)}, bf16[2,4096]{1,0:T(2,128)(2,1)S(1)}, u32[]{:S(2)}, u32[]{:S(2)}) collective-permute-start(bf16[2,4096]{1,0:T(2,128)(2,1)S(1)} %get-tuple-element.20.a_ref), channel_id=1, source_target_pairs={{0,1},{1,0},{2,3},{3,2},{4,5},{5,4},{6,7},{7,6},{8,9},{9,8},{10,11... | collective-permute-start | bytes 49160 | tf_op jit(solution)/shard_map/ppermute | solution.py:48
  4.3 8.5 %collective-permute-start.3 = (bf16[4,4096]{1,0:T(4,128)(2,1)S(1)}, bf16[4,4096]{1,0:T(4,128)(2,1)S(1)}, u32[]{:S(2)}, u32[]{:S(2)}) collective-permute-start(bf16[4,4096]{1,0:T(4,128)(2,1)S(1)} %join.1.refs_0_.a0), channel_id=1, source_target_pairs={{0,6},{2,0},{4,2},{6,4},{1,7},{3,1},{5,3},{7,5},{8,14},{10,8},{12,... | collective-permute-start | bytes 98312 | tf_op jit(solution)/shard_map/ppermute | solution.py:53
  8.5 5.5 %collective-permute-start.2 = (bf16[4,4096]{1,0:T(4,128)(2,1)S(1)}, bf16[4,4096]{1,0:T(4,128)(2,1)S(1)}, u32[]{:S(2)}, u32[]{:S(2)}) collective-permute-start(bf16[4,4096]{1,0:T(4,128)(2,1)S(1)} %join.1.refs_0_.a0), channel_id=1, source_target_pairs={{0,4},{2,6},{4,0},{6,2},{1,5},{3,7},{5,1},{7,3},{8,12},{10,14},{12... | collective-permute-start | bytes 98312 | tf_op jit(solution)/shard_map/ppermute | solution.py:53
  8.5 5.5 %collective-permute-start.1 = (bf16[4,4096]{1,0:T(4,128)(2,1)S(1)}, bf16[4,4096]{1,0:T(4,128)(2,1)S(1)}, u32[]{:S(2)}, u32[]{:S(2)}) collective-permute-start(bf16[4,4096]{1,0:T(4,128)(2,1)S(1)} %join.1.refs_0_.a0), channel_id=1, source_target_pairs={{0,2},{2,4},{4,6},{6,0},{1,3},{3,5},{5,7},{7,1},{8,10},{10,12},{12... | collective-permute-start | bytes 98312 | tf_op jit(solution)/shard_map/ppermute | solution.py:53
  9.8 33.4 %slice-start.1 = ((s8[6291456]{0:T(1024)(128)(4,1)}), s8[2097152]{0:T(1024)(128)(4,1)S(1)}, s32[]{:S(2)}) async-start(s8[6291456]{0:T(1024)(128)(4,1)} %bitcast.11), calls=%async_computation.3 | async-start | bytes 4194304
  9.8 33.4 %slice-start.3 = ((s8[6291456]{0:T(1024)(128)(4,1)}), s8[2097152]{0:T(1024)(128)(4,1)S(1)}, s32[]{:S(2)}) async-start(s8[6291456]{0:T(1024)(128)(4,1)} %bitcast.17), calls=%async_computation.5 | async-start | bytes 4194304
  43.1 2.8 %collective-permute-start.4 = (bf16[64,72,128]{2,1,0:T(8,128)(2,1)S(1)}, bf16[64,72,128]{2,1,0:T(8,128)(2,1)S(1)}, u32[]{:S(2)}, u32[]{:S(2)}) collective-permute-start(bf16[64,72,128]{2,1,0:T(8,128)(2,1)S(1)} %all_to_all.10.own_ref), channel_id=1, source_target_pairs={{0,1},{1,0},{2,3},{3,2},{4,5},{5,4},{6,7},{7,6},{8,9},{9,8},{10,11... | collective-permute-start | bytes 3538952 | tf_op jit(solution)/shard_map/ppermute | solution.py:48
  49.0 2.0 %collective-permute-start.6 = (bf16[16,2,16,512]{3,2,1,0:T(8,128)(2,1)S(1)}, bf16[16,2,16,512]{3,2,1,0:T(8,128)(2,1)S(1)}, u32[]{:S(2)}, u32[]{:S(2)}) collective-permute-start(bf16[16,2,16,512]{3,2,1,0:T(8,128)(2,1)S(1)} %down_theirs.1), channel_id=1, source_target_pairs={{0,1},{1,0},{2,3},{3,2},{4,5},{5,4},{6,7},{7,6},{8,9},{9,8},{10,11... | collective-permute-start | bytes 1572872 | tf_op jit(solution)/shard_map/ppermute | solution.py:48
  49.2 2.6 %collective-permute-start.5 = (bf16[16,2,16,512]{3,2,1,0:T(8,128)(2,1)S(1)}, bf16[16,2,16,512]{3,2,1,0:T(8,128)(2,1)S(1)}, u32[]{:S(2)}, u32[]{:S(2)}) collective-permute-start(bf16[16,2,16,512]{3,2,1,0:T(8,128)(2,1)S(1)} %get-tuple-element.33), channel_id=1, source_target_pairs={{0,1},{1,0},{2,3},{3,2},{4,5},{5,4},{6,7},{7,6},{8,9},{9,8},{10,11... | collective-permute-start | bytes 1572872 | tf_op jit(solution)/shard_map/ppermute | solution.py:48

commit v4 on v3

--- a/solution.py
+++ b/solution.py
@@ -1,5 +1,6 @@
 import functools
 import math
+import random
 
 import jax
 import jax.numpy as jnp
@@ -23,6 +24,10 @@
 EXTRA = 8
 IDS, HI, MID, LO, SQ = 0, ROWS, 2 * ROWS, 3 * ROWS, 4 * ROWS
 EXPERT_COLS = 192
+ORDER = list(range(PLACES * SIDE))
+random.Random(1).shuffle(ORDER)
+RANK = [ORDER.index(place) for place in range(PLACES * SIDE)]
+GROUPS = [[place * CORES + c for place in ORDER] for c in range(CORES)]
 F32 = jnp.float32
 BF16 = jnp.bfloat16
 NT = (((1,), (1,)), ((), ()))
@@ -255,7 +260,7 @@
             for j in range(CHUNKS):
                 start = z * COLS + j * LANES
                 x_ref[s * ROWS : (s + 1) * ROWS, start : start + LANES] = units_ref[
-                    s * SIDE + z, j * ROWS : (j + 1) * ROWS, :
+                    RANK[s * SIDE + z], j * ROWS : (j + 1) * ROWS, :
                 ]
 
 
@@ -278,16 +283,17 @@
 
 
 def squares_of(units):
-    extras = units[:, UNIT : UNIT + 3, :].astype(F32)
-    extras = jnp.sum(extras, axis=1, keepdims=True).reshape(PLACES, SIDE, 1, LANES)
-    return sum(extras[:, z] for z in range(SIDE))
+    extras = jnp.sum(units[:, UNIT : UNIT + 3, :].astype(F32), axis=1, keepdims=True)
+    return sum(
+        jnp.stack([extras[RANK[s * SIDE + z]] for s in range(PLACES)]) for z in range(SIDE)
+    )
 
 
 def own_kernel(own_ref, gate_ref, up_ref, down_ref, gate_sum, up_sum, mix_ref, squares_ref, x_ref):
     c = lax.axis_index("c")
     gather_rows(own_ref, x_ref)
     squares_ref[...] = squares_of(own_ref)
-    routes = jnp.stack([own_ref[s * SIDE, UNIT:, :] for s in range(PLACES)]).astype(F32)
+    routes = jnp.stack([own_ref[RANK[s * SIDE], UNIT:, :] for s in range(PLACES)]).astype(F32)
     weights = (
         pltpu.roll(routes, LANES - HI, 2)
         + pltpu.roll(routes, LANES - MID, 2)
@@ -395,15 +401,16 @@
 
 def add_kernel(mine_ref, first_ref, second_ref, out_ref):
     for i, came_ref in enumerate((first_ref, second_ref)):
-        zs = slice(i * HALF, (i + 1) * HALF)
-        total = mine_ref[:, zs].astype(F32) + came_ref[...].astype(F32)
-        out_ref[:, zs] = total.astype(BF16)
+        for z in range(HALF):
+            total = mine_ref[:, i * HALF + z].astype(F32) + came_ref[:, z].astype(F32)
+            for s in range(PLACES):
+                out_ref[RANK[s * SIDE + i * HALF + z]] = total[s].astype(BF16)
 
 
 def add(mine, first, second):
     return pl.pallas_call(
         add_kernel,
-        out_shape=blocks(SIDE),
+        out_shape=jax.ShapeDtypeStruct((PLACES * SIDE, ROWS, COLS), BF16),
         in_specs=[VMEM] * 3,
         out_specs=VMEM,
         compiler_params=params(4),
@@ -434,7 +441,10 @@
 
 
 def exchange(blocks):
-    return lax.all_to_all(blocks, ("x", "y", "z"), split_axis=0, concat_axis=0, tiled=True)
+    axes = ("x", "y", "z", "c")
+    return lax.all_to_all(
+        blocks, axes, split_axis=0, concat_axis=0, axis_index_groups=GROUPS, tiled=True
+    )
 
 
 def on_device(
@@ -468,8 +478,7 @@
     first = swap(theirs)
     second = swap(down_blocks(False, hidden, down))
     mine = down_blocks(True, hidden, down)
-    total = add(mine, first, second).reshape(PLACES * SIDE, ROWS, COLS)
-    return finish(exchange(total), stream)
+    return finish(exchange(add(mine, first, second)), stream)
 
 
 def solution(mesh):

time: 76.1 us -> 73.7 us (0.968)
  blocking collectives: 51.3 us -> 48.9 us
    all_to_all x2, blocking collectives: 51.3 us -> 48.9 us  [exchange(): lax.all_to_all(blocks, axes, split_axis=0, concat_axis=0, axis_index_grou...]
where the time goes in v4:
time: 73.7 us; the launch traced here: 73.6 us
  blocking collectives  48.9 us (66%)
  Pallas kernels  14 us (19%)
  starting transfers between devices  6.13 us (8%)
  waiting for transfers between devices  4.39 us (6%)
    all_to_all x2, blocking collectives, exchange(): lax.all_to_all(blocks, axes, split_axis=0, concat_axis=0, axis_index_grou...  48.9 us
    ppermute x3, starting transfers between devices, spread_z(): lax.ppermute(block, 'z', [(i, (i + k) % SIDE) for i in range(SIDE)])  5.45 us
    ppermute x4, waiting for transfers between devices, swap(): return lax.ppermute(block, 'c', SWAP)  3.23 us
    pallas_call x1, Pallas kernels, attention(): pl.pallas_call(attention_kernel, out_shape=[jax.ShapeDtypeStruct((rows, w...  3.05 us
    pallas_call x1, Pallas kernels, fetch(): pl.pallas_call(fetch_kernel, out_shape=[pltpu.VMEM(a.shape, a.dtype) for...  3.04 us
    pallas_call x1, Pallas kernels, make_hidden(): pl.pallas_call(hidden_kernel, out_shape=[jax.ShapeDtypeStruct((rows, widt...  2.44 us
    pallas_call x1, Pallas kernels, own_part(): pl.pallas_call(own_kernel, out_shape=[jax.ShapeDtypeStruct((rows, width),...  1.89 us
    pallas_call x2, Pallas kernels, down_blocks(): pl.pallas_call(functools.partial(down_kernel, mine), out_shape=blocks(cou...  1.59 us
  transfers between devices with their start and end apart: 7, of which 5 were waited for; matrix products, arithmetic and copies ran while one was open for 0% of the time, Pallas kernels for 8%

profile of v4, /device:TPU:0, one launch (start us, length us, event | category | flops | bytes accessed | tf_op | source)
XLA Modules:
  0.0 73.6 jit_solution(11881409829723352006)
XLA Ops:
  0.0 0.0 slice-start
  0.0 0.0 slice-start.2
  0.0 3.0 %attention.1 = (bf16[2,4096]{1,0:T(2,128)(2,1)S(1)}, bf16[4096,512]{1,0:T(8,128)(2,1)S(1)}) custom-call(s32[2]{0:T(128)} %len_hbm.1, bf16[2,4096]{1,0:T(2,128)(2,1)} %q_hbm.1, bf16[2,1024,256]{2,1,0:T(8,128)(2,1)} %k_hbm.1, bf16[2,1024,256]{2,1,0:T(8,128)(2,1)} %v_hbm.1, bf16[4096,512]{1,0:T(8,128)(2,1)} %w_hbm.1), custom_call_target="tpu_custom_call" | custom-call | tf_op jit(solution)/shard_map/attention/pallas_call | solution.py:120
  3.1 0.1 collective-permute-start
  3.2 1.2 %collective-permute-done.b_ref = bf16[2,4096]{1,0:T(2,128)(2,1)S(1)} collective-permute-done((bf16[2,4096]{1,0:T(2,128)(2,1)S(1)}, bf16[2,4096]{1,0:T(2,128)(2,1)S(1)}, u32[]{:S(2)}, u32[]{:S(2)}) %collective-permute-start) | collective-permute-done | bytes 16416 | tf_op jit(solution)/shard_map/ppermute | solution.py:53
  4.3 4.2 %collective-permute-start.3 = (bf16[4,4096]{1,0:T(4,128)(2,1)S(1)}, bf16[4,4096]{1,0:T(4,128)(2,1)S(1)}, u32[]{:S(2)}, u32[]{:S(2)}) collective-permute-start(bf16[4,4096]{1,0:T(4,128)(2,1)S(1)} %join.1.refs_0_.a0), channel_id=1, source_target_pairs={{0,6},{2,0},{4,2},{6,4},{1,7},{3,1},{5,3},{7,5},{8,14},{10,8},{12,... | collective-permute-start | bytes 98312 | tf_op jit(solution)/shard_map/ppermute | solution.py:58
  8.5 0.0 collective-permute-start.2
  8.5 1.3 %collective-permute-start.1 = (bf16[4,4096]{1,0:T(4,128)(2,1)S(1)}, bf16[4,4096]{1,0:T(4,128)(2,1)S(1)}, u32[]{:S(2)}, u32[]{:S(2)}) collective-permute-start(bf16[4,4096]{1,0:T(4,128)(2,1)S(1)} %join.1.refs_0_.a0), channel_id=1, source_target_pairs={{0,2},{2,4},{4,6},{6,0},{1,3},{3,5},{5,7},{7,1},{8,10},{10,12},{12... | collective-permute-start | bytes 98312 | tf_op jit(solution)/shard_map/ppermute | solution.py:58
  9.8 0.0 slice-start.1
  9.8 0.0 slice-start.3
  9.8 3.0 %fetch.1 = (bf16[16,512]{1,0:T(8,128)(2,1)S(1)}, f32[1,512]{1,0:T(1,128)S(1)}, s32[8,16]{1,0:T(8,128)S(1)}, f32[8,16]{1,0:T(8,128)S(1)}, bf16[768,4096]{1,0:T(8,128)(2,1)S(1)}) custom-call(bf16[4,4096]{1,0:T(4,128)(2,1)S(1)} %join.1.refs_0_.a0, bf16[16,512]{1,0:T(8,128)(2,1)} %refs_1_.1, f32[1,512]{1,0:T(1,128)} %bitcast.23, s32[8,16]{1,0:T(8,128)} %bitcast.21, ...), custom_call_target="tpu_custom_call" | custom-call | bytes 6310912 | tf_op jit(solution)/shard_map/fetch/pallas_call | solution.py:174
  12.8 0.0 collective-permute-done.3.a3
  12.9 1.1 %collective-permute-done.2.a2 = bf16[4,4096]{1,0:T(4,128)(2,1)S(1)} collective-permute-done((bf16[4,4096]{1,0:T(4,128)(2,1)S(1)}, bf16[4,4096]{1,0:T(4,128)(2,1)S(1)}, u32[]{:S(2)}, u32[]{:S(2)}) %collective-permute-start.2) | collective-permute-done | bytes 32800 | tf_op jit(solution)/shard_map/ppermute | solution.py:58
  14.0 0.0 collective-permute-done.1.a1
  14.0 0.9 %stream.1 = (bf16[16,512]{1,0:T(8,128)(2,1)S(1)}, bf16[64,72,128]{2,1,0:T(8,128)(2,1)S(1)}) custom-call(bf16[4,4096]{1,0:T(4,128)(2,1)S(1)} %join.1.refs_0_.a0, bf16[4,4096]{1,0:T(4,128)(2,1)S(1)} %collective-permute-done.1.a1, bf16[4,4096]{1,0:T(4,128)(2,1)S(1)} %collective-permute-done.2.a2, bf16[4,4096]{1,0:T(4,128)(2,1)S(1)} %collective-permute-done.3.a3, ...), custom_call_target="tpu_custom_call" | custom-call | tf_op jit(solution)/shard_map/stream/pallas_call | solution.py:235
  15.0 26.1 %all_to_all.10.own_ref = bf16[64,72,128]{2,1,0:T(8,128)(2,1)S(1)} all-to-all(bf16[64,72,128]{2,1,0:T(8,128)(2,1)S(1)} %get-tuple-element.26), channel_id=1, replica_groups={{44,24,104,6,38,10,120,116,4,66,20,16,58,52,50,18,88,36,124,22,94,80,30..., dimensions={0} | all-to-all | bytes 2359296 | tf_op jit(solution)/shard_map/all_to_all | solution.py:445
  41.1 0.0 collective-permute-start.4
  41.1 0.0 slice-done
  41.1 0.0 slice-done.2
  41.1 0.0 slice-done.1
  41.1 0.0 slice-done.3
  41.1 1.9 %own_part.1 = (f32[256,768]{1,0:T(8,128)S(1)}, f32[256,768]{1,0:T(8,128)S(1)}, f32[256,768]{1,0:T(8,128)S(1)}, f32[16,1,128]{2,1,0:T(1,128)S(1)}) custom-call(bf16[64,72,128]{2,1,0:T(8,128)(2,1)S(1)} %all_to_all.10.own_ref, bf16[768,4096]{1,0:T(8,128)(2,1)S(1)} %get-tuple-element.27.gate_ref, bf16[768,4096]{1,0:T(8,128)(2,1)S(1)} %bitcast.18, ...), custom_call_target="tpu_custom_call" | custom-call | tf_op jit(solution)/shard_map/own_part/pallas_call | solution.py:318
  43.0 0.9 %collective-permute-done.4.other_ref = bf16[64,72,128]{2,1,0:T(8,128)(2,1)S(1)} collective-permute-done((bf16[64,72,128]{2,1,0:T(8,128)(2,1)S(1)}, bf16[64,72,128]{2,1,0:T(8,128)(2,1)S(1)}, u32[]{:S(2)}, u32[]{:S(2)}) %collective-permute-start.4) | collective-permute-done | bytes 1179680 | tf_op jit(solution)/shard_map/ppermute | solution.py:53
  43.9 2.4 %hidden.1 = (bf16[256,768]{1,0:T(8,128)(2,1)S(1)}, bf16[16,2,16,512]{3,2,1,0:T(8,128)(2,1)S(1)}) custom-call(bf16[64,72,128]{2,1,0:T(8,128)(2,1)S(1)} %collective-permute-done.4.other_ref, bf16[768,4096]{1,0:T(8,128)(2,1)S(1)} %get-tuple-element.27.gate_ref, bf16[768,4096]{1,0:T(8,128)(2,1)S(1)} %bitcast.19, f32[256,768]{1,0:T(8,128)S(1)} %get-tuple-element.28.gate_in, ...), custom_call_target="tpu_custom_call" | custom-call | tf_op jit(solution)/shard_map/hidden/pallas_call | solution.py:370
  46.4 0.6 down_theirs.1
  47.0 0.2 collective-permute-start.6
  47.2 0.4 collective-permute-start.5
  47.6 1.0 %down_mine.1.mine_ref = bf16[16,4,16,512]{3,2,1,0:T(8,128)(2,1)S(1)} custom-call(bf16[256,768]{1,0:T(8,128)(2,1)S(1)} %get-tuple-element.32.hidden_ref, bf16[768,4096]{1,0:T(8,128)(2,1)S(1)} %bitcast.15), custom_call_target="tpu_custom_call" | custom-call | flops 1 | bytes 1 | tf_op jit(solution)/shard_map/down_mine/pallas_call | solution.py:391
  48.6 0.4 collective-permute-done.6.second_ref
  49.0 0.7 %collective-permute-done.5.first_ref = bf16[16,2,16,512]{3,2,1,0:T(8,128)(2,1)S(1)} collective-permute-done((bf16[16,2,16,512]{3,2,1,0:T(8,128)(2,1)S(1)}, bf16[16,2,16,512]{3,2,1,0:T(8,128)(2,1)S(1)}, u32[]{:S(2)}, u32[]{:S(2)}) %collective-permute-start.5) | collective-permute-done | bytes 524320 | tf_op jit(solution)/shard_map/ppermute | solution.py:53
  49.7 0.2 add.1
  50.0 22.8 %all_to_all.11.parts_ref = bf16[64,16,512]{2,1,0:T(8,128)(2,1)S(1)} all-to-all(bf16[64,16,512]{2,1,0:T(8,128)(2,1)S(1)} %add.1), channel_id=1, replica_groups={{44,24,104,6,38,10,120,116,4,66,20,16,58,52,50,18,88,36,124,22,94,80,30..., dimensions={0} | all-to-all | bytes 2097152 | tf_op jit(solution)/shard_map/all_to_all | solution.py:445
  72.8 0.8 %finish.1 = bf16[16,512]{1,0:T(8,128)(2,1)} custom-call(bf16[64,16,512]{2,1,0:T(8,128)(2,1)S(1)} %all_to_all.11.parts_ref, bf16[16,512]{1,0:T(8,128)(2,1)S(1)} %get-tuple-element.34.stream_ref), custom_call_target="tpu_custom_call" | custom-call | tf_op jit(solution)/shard_map/finish/pallas_call | solution.py:432
  (3 shorter events, 0.0 us)
Async XLA Ops:
  0.0 41.1 %slice-start = ((s8[6291456]{0:T(1024)(128)(4,1)}), s8[4194304]{0:T(1024)(128)(4,1)S(1)}, s32[]{:S(2)}) async-start(s8[6291456]{0:T(1024)(128)(4,1)} %bitcast.10), calls=%async_computation.2 | async-start | bytes 8388608
  0.0 41.1 %slice-start.2 = ((s8[6291456]{0:T(1024)(128)(4,1)}), s8[4194304]{0:T(1024)(128)(4,1)S(1)}, s32[]{:S(2)}) async-start(s8[6291456]{0:T(1024)(128)(4,1)} %bitcast.16), calls=%async_computation.4 | async-start | bytes 8388608
  3.1 1.3 %collective-permute-start = (bf16[2,4096]{1,0:T(2,128)(2,1)S(1)}, bf16[2,4096]{1,0:T(2,128)(2,1)S(1)}, u32[]{:S(2)}, u32[]{:S(2)}) collective-permute-start(bf16[2,4096]{1,0:T(2,128)(2,1)S(1)} %get-tuple-element.20.a_ref), channel_id=1, source_target_pairs={{0,1},{1,0},{2,3},{3,2},{4,5},{5,4},{6,7},{7,6},{8,9},{9,8},{10,11... | collective-permute-start | bytes 49160 | tf_op jit(solution)/shard_map/ppermute | solution.py:53
  4.3 8.5 %collective-permute-start.3 = (bf16[4,4096]{1,0:T(4,128)(2,1)S(1)}, bf16[4,4096]{1,0:T(4,128)(2,1)S(1)}, u32[]{:S(2)}, u32[]{:S(2)}) collective-permute-start(bf16[4,4096]{1,0:T(4,128)(2,1)S(1)} %join.1.refs_0_.a0), channel_id=1, source_target_pairs={{0,6},{2,0},{4,2},{6,4},{1,7},{3,1},{5,3},{7,5},{8,14},{10,8},{12,... | collective-permute-start | bytes 98312 | tf_op jit(solution)/shard_map/ppermute | solution.py:58
  8.5 5.5 %collective-permute-start.2 = (bf16[4,4096]{1,0:T(4,128)(2,1)S(1)}, bf16[4,4096]{1,0:T(4,128)(2,1)S(1)}, u32[]{:S(2)}, u32[]{:S(2)}) collective-permute-start(bf16[4,4096]{1,0:T(4,128)(2,1)S(1)} %join.1.refs_0_.a0), channel_id=1, source_target_pairs={{0,4},{2,6},{4,0},{6,2},{1,5},{3,7},{5,1},{7,3},{8,12},{10,14},{12... | collective-permute-start | bytes 98312 | tf_op jit(solution)/shard_map/ppermute | solution.py:58
  8.5 5.5 %collective-permute-start.1 = (bf16[4,4096]{1,0:T(4,128)(2,1)S(1)}, bf16[4,4096]{1,0:T(4,128)(2,1)S(1)}, u32[]{:S(2)}, u32[]{:S(2)}) collective-permute-start(bf16[4,4096]{1,0:T(4,128)(2,1)S(1)} %join.1.refs_0_.a0), channel_id=1, source_target_pairs={{0,2},{2,4},{4,6},{6,0},{1,3},{3,5},{5,7},{7,1},{8,10},{10,12},{12... | collective-permute-start | bytes 98312 | tf_op jit(solution)/shard_map/ppermute | solution.py:58
  9.8 31.3 %slice-start.1 = ((s8[6291456]{0:T(1024)(128)(4,1)}), s8[2097152]{0:T(1024)(128)(4,1)S(1)}, s32[]{:S(2)}) async-start(s8[6291456]{0:T(1024)(128)(4,1)} %bitcast.10), calls=%async_computation.3 | async-start | bytes 4194304
  9.8 31.3 %slice-start.3 = ((s8[6291456]{0:T(1024)(128)(4,1)}), s8[2097152]{0:T(1024)(128)(4,1)S(1)}, s32[]{:S(2)}) async-start(s8[6291456]{0:T(1024)(128)(4,1)} %bitcast.16), calls=%async_computation.5 | async-start | bytes 4194304
  41.1 2.8 %collective-permute-start.4 = (bf16[64,72,128]{2,1,0:T(8,128)(2,1)S(1)}, bf16[64,72,128]{2,1,0:T(8,128)(2,1)S(1)}, u32[]{:S(2)}, u32[]{:S(2)}) collective-permute-start(bf16[64,72,128]{2,1,0:T(8,128)(2,1)S(1)} %all_to_all.10.own_ref), channel_id=1, source_target_pairs={{0,1},{1,0},{2,3},{3,2},{4,5},{5,4},{6,7},{7,6},{8,9},{9,8},{10,11... | collective-permute-start | bytes 3538952 | tf_op jit(solution)/shard_map/ppermute | solution.py:53
  47.0 2.0 %collective-permute-start.6 = (bf16[16,2,16,512]{3,2,1,0:T(8,128)(2,1)S(1)}, bf16[16,2,16,512]{3,2,1,0:T(8,128)(2,1)S(1)}, u32[]{:S(2)}, u32[]{:S(2)}) collective-permute-start(bf16[16,2,16,512]{3,2,1,0:T(8,128)(2,1)S(1)} %down_theirs.1), channel_id=1, source_target_pairs={{0,1},{1,0},{2,3},{3,2},{4,5},{5,4},{6,7},{7,6},{8,9},{9,8},{10,11... | collective-permute-start | bytes 1572872 | tf_op jit(solution)/shard_map/ppermute | solution.py:53
  47.2 2.6 %collective-permute-start.5 = (bf16[16,2,16,512]{3,2,1,0:T(8,128)(2,1)S(1)}, bf16[16,2,16,512]{3,2,1,0:T(8,128)(2,1)S(1)}, u32[]{:S(2)}, u32[]{:S(2)}) collective-permute-start(bf16[16,2,16,512]{3,2,1,0:T(8,128)(2,1)S(1)} %get-tuple-element.33), channel_id=1, source_target_pairs={{0,1},{1,0},{2,3},{3,2},{4,5},{5,4},{6,7},{7,6},{8,9},{9,8},{10,11... | collective-permute-start | bytes 1572872 | tf_op jit(solution)/shard_map/ppermute | solution.py:53

commit v5 on v4

--- a/solution.py
+++ b/solution.py
@@ -61,7 +61,7 @@
 
 
 def attention_kernel(
-    len_hbm, q_hbm, k_hbm, v_hbm, w_hbm, out_ref, w_ref, lens, q_ref, k_ref, v_ref, q_rows, out_rows, sems
+    len_hbm, q_hbm, k_hbm, v_hbm, out_ref, lens, q_ref, k_ref, v_ref, q_rows, out_rows, sems
 ):
     rows, width = q_ref.shape
     positions = k_ref.shape[1]
@@ -78,11 +78,8 @@
     ]
     q_copy.start()
     len_copy.start()
-    for r in range(rows):
-        k_copies[r].start()
-        v_copies[r].start()
-    w_copy = pltpu.make_async_copy(w_hbm, w_ref, sems.at[2 + 2 * rows])
-    w_copy.start()
+    for copy in k_copies + v_copies:
+        copy.start()
     q_copy.wait()
     queries = q_ref[...].astype(F32)
     for r in range(rows):
@@ -92,36 +89,40 @@
             ]
     len_copy.wait()
     spots = lax.broadcasted_iota(jnp.int32, (per_group, positions), 1)
-    for r in range(rows):
-        live = spots < lens[r]
-        k_copies[r].wait()
-        v_copies[r].wait()
-        for g in range(KV_HEADS):
-            first = r * heads + g * per_group
-            q = q_rows[first : first + per_group, :].astype(BF16)
-            keys = k_ref[r, :, g * HEAD : (g + 1) * HEAD]
-            scores = lax.dot_general(q, keys, NT, preferred_element_type=F32) / math.sqrt(HEAD)
-            scores = jnp.where(live, scores, -1e30)
-            peak = jnp.max(scores, axis=1, keepdims=True)
-            probs = jnp.where(live, jnp.exp(scores - peak), 0.0)
-            weight_sum = jnp.sum(probs, axis=1, keepdims=True)
-            values = v_ref[r, :, g * HEAD : (g + 1) * HEAD]
-            summed = jnp.dot(probs.astype(BF16), values, preferred_element_type=F32)
-            summed = summed / weight_sum
-            for j in range(per_group):
-                h = g * per_group + j
-                out_rows[r : r + 1, h * HEAD : (h + 1) * HEAD] = summed[j : j + 1, :]
+    cases = [(r, g) for r in range(rows) for g in range(KV_HEADS)]
+    for copy in k_copies:
+        copy.wait()
+    scores = []
+    for r, g in cases:
+        first = r * heads + g * per_group
+        q = q_rows[first : first + per_group, :].astype(BF16)
+        keys = k_ref[r, :, g * HEAD : (g + 1) * HEAD]
+        product = lax.dot_general(q, keys, NT, preferred_element_type=F32) / math.sqrt(HEAD)
+        scores.append(jnp.where(spots < lens[r], product, -1e30))
+    peaks = [jnp.max(x, axis=1, keepdims=True) for x in scores]
+    probs = [
+        jnp.where(spots < lens[r], jnp.exp(x - peak), 0.0)
+        for (r, g), x, peak in zip(cases, scores, peaks)
+    ]
+    sums = [jnp.sum(x, axis=1, keepdims=True) for x in probs]
+    for copy in v_copies:
+        copy.wait()
+    for (r, g), x, weight_sum in zip(cases, probs, sums):
+        values = v_ref[r, :, g * HEAD : (g + 1) * HEAD]
+        summed = jnp.dot(x.astype(BF16), values, preferred_element_type=F32) / weight_sum
+        for j in range(per_group):
+            h = g * per_group + j
+            out_rows[r : r + 1, h * HEAD : (h + 1) * HEAD] = summed[j : j + 1, :]
     out_ref[...] = out_rows[...].astype(BF16)
-    w_copy.wait()
-
-
-def attention(lengths, queries, keys, values, out_proj):
+
+
+def attention(lengths, queries, keys, values):
     rows, width = queries.shape
     return pl.pallas_call(
         attention_kernel,
-        out_shape=[jax.ShapeDtypeStruct((rows, width), BF16), pltpu.VMEM(out_proj.shape, BF16)],
-        in_specs=[ANY] * 5,
-        out_specs=[VMEM] * 2,
+        out_shape=jax.ShapeDtypeStruct((rows, width), BF16),
+        in_specs=[ANY] * 4,
+        out_specs=VMEM,
         scratch_shapes=[
             pltpu.SMEM(lengths.shape, jnp.int32),
             pltpu.VMEM((rows, width), BF16),
@@ -129,11 +130,11 @@
             pltpu.VMEM(values.shape, BF16),
             pltpu.VMEM((rows * width // HEAD, HEAD), F32),
             pltpu.VMEM((rows, width), F32),
-            pltpu.SemaphoreType.DMA((3 + 2 * rows,)),
+            pltpu.SemaphoreType.DMA((2 + 2 * rows,)),
         ],
         compiler_params=params(16),
         name="attention",
-    )(*map(in_hbm, (lengths, queries, keys, values, out_proj)))
+    )(*map(in_hbm, (lengths, queries, keys, values)))
 
 
 def join_kernel(a_ref, b_ref, out_ref):
@@ -242,6 +243,9 @@
         out_specs=[VMEM, VMEM],
         scratch_shapes=[pltpu.VMEM((ROWS, D), F32)],
         compiler_params=params(4),
+        cost_estimate=pl.CostEstimate(
+            flops=10000000000, bytes_accessed=60000000, transcendentals=0
+        ),
         name="stream",
     )(*parts, out_proj, residual, gain, ids, weights)
 
@@ -343,23 +347,20 @@
         half = (gate_in[:, part] + products(x_ref, gate_ref, other, first, width)) * (0.5 * scale)
         up = (up_in[:, part] + products(x_ref, up_ref, other, first, width)) * scale
         hidden_ref[:, part] = ((half + half * jnp.tanh(half)) * up * mix_ref[:, part]).astype(BF16)
-    down_part(hidden_ref, down_ref, other, out_ref, 0)
-
-
-def down_part(hidden_ref, down_ref, parity, out_ref, first):
-    for z in range(out_ref.shape[1]):
+    down_part(hidden_ref, down_ref, other, out_ref)
+
+
+def down_part(hidden_ref, down_ref, parity, out_ref):
+    for z in range(SIDE):
         part = jnp.dot(
             hidden_ref[...],
-            down_ref[:, columns_of(first + z, parity)],
+            down_ref[:, columns_of(z, parity)],
             preferred_element_type=F32,
         ).astype(BF16)
         for s in range(PLACES):
             out_ref[s, z] = part[s * ROWS : (s + 1) * ROWS]
 
 
-HALF = SIDE // 2
-
-
 def blocks(count):
     return jax.ShapeDtypeStruct((PLACES, count, ROWS, COLS), BF16)
 
@@ -369,7 +370,7 @@
     width = gate.shape[0]
     return pl.pallas_call(
         hidden_kernel,
-        out_shape=[jax.ShapeDtypeStruct((rows, width), BF16), blocks(HALF)],
+        out_shape=[jax.ShapeDtypeStruct((rows, width), BF16), blocks(SIDE)],
         in_specs=[VMEM] * 8,
         out_specs=[VMEM] * 2,
         scratch_shapes=[pltpu.VMEM((rows, D // CORES), BF16)],
@@ -378,44 +379,37 @@
     )(other, gate, up, *sums, down)
 
 
-def down_kernel(mine, hidden_ref, down_ref, out_ref):
-    c = lax.axis_index("c")
-    if mine:
-        down_part(hidden_ref, down_ref, c, out_ref, 0)
-    else:
-        down_part(hidden_ref, down_ref, 1 - c, out_ref, HALF)
-
-
-def down_blocks(mine, hidden, down):
-    count = SIDE if mine else HALF
-    return pl.pallas_call(
-        functools.partial(down_kernel, mine),
-        out_shape=blocks(count),
+def down_kernel(hidden_ref, down_ref, out_ref):
+    down_part(hidden_ref, down_ref, lax.axis_index("c"), out_ref)
+
+
+def down_blocks(hidden, down):
+    return pl.pallas_call(
+        down_kernel,
+        out_shape=blocks(SIDE),
         in_specs=[VMEM, VMEM],
         out_specs=VMEM,
         compiler_params=params(4),
-        cost_estimate=pl.CostEstimate(flops=1, bytes_accessed=1, transcendentals=0),
-        name="down_mine" if mine else "down_theirs",
+        name="down_mine",
     )(hidden, down)
 
 
-def add_kernel(mine_ref, first_ref, second_ref, out_ref):
-    for i, came_ref in enumerate((first_ref, second_ref)):
-        for z in range(HALF):
-            total = mine_ref[:, i * HALF + z].astype(F32) + came_ref[:, z].astype(F32)
-            for s in range(PLACES):
-                out_ref[RANK[s * SIDE + i * HALF + z]] = total[s].astype(BF16)
-
-
-def add(mine, first, second):
+def add_kernel(mine_ref, came_ref, out_ref):
+    for z in range(SIDE):
+        total = mine_ref[:, z].astype(F32) + came_ref[:, z].astype(F32)
+        for s in range(PLACES):
+            out_ref[RANK[s * SIDE + z]] = total[s].astype(BF16)
+
+
+def add(mine, came):
     return pl.pallas_call(
         add_kernel,
         out_shape=jax.ShapeDtypeStruct((PLACES * SIDE, ROWS, COLS), BF16),
-        in_specs=[VMEM] * 3,
+        in_specs=[VMEM] * 2,
         out_specs=VMEM,
         compiler_params=params(4),
         name="add",
-    )(mine, first, second)
+    )(mine, came)
 
 
 def finish_kernel(parts_ref, stream_ref, out_hbm, out_ref, sem):
@@ -464,21 +458,20 @@
     gate = jnp.swapaxes(w_gate, 1, 2).reshape(-1, D)
     up = jnp.swapaxes(w_up, 1, 2).reshape(-1, D)
     down = w_down.reshape(-1, D)
-    attended, out_proj = attention(lengths, queries, key_cache, value_cache, out_proj)
+    attended = attention(lengths, queries, key_cache, value_cache)
     pair = join(attended, swap(attended))
     parts = spread_z(pair)
-    residual, gain, ids, weights, gate = fetch(
-        pair, residual, norm_gain[None, :], expert_ids.T, route_weights.T, gate
+    residual, gain, ids, weights, out_proj = fetch(
+        pair, residual, norm_gain[None, :], expert_ids.T, route_weights.T, out_proj
     )
     stream, units = make_stream(parts, out_proj, residual, gain, ids, weights)
     own = exchange(units)
     other = swap(own)
     sums = own_part(own, gate, up, down)
     hidden, theirs = make_hidden(other, gate, up, sums, down)
-    first = swap(theirs)
-    second = swap(down_blocks(False, hidden, down))
-    mine = down_blocks(True, hidden, down)
-    return finish(exchange(add(mine, first, second)), stream)
+    came = swap(theirs)
+    mine = down_blocks(hidden, down)
+    return finish(exchange(add(mine, came)), stream)
 
 
 def solution(mesh):

time: 73.7 us -> 72.9 us (0.989)
  Pallas kernels: 14 us -> 12.1 us
  waiting for transfers between devices: 4.39 us -> 5.53 us
    pallas_call x3 -> x2, Pallas kernels: 4.63 us -> 3.08 us  [the longest x1 2.11 us: attention(): pl.pallas_call(attention_kernel, out_shape=jax.ShapeDtypeStruct((rows, wi...]
    ppermute x3, waiting for transfers between devices: 1.15 us -> 1.91 us  [spread_z(): lax.ppermute(block, 'z', [(i, (i + k) % SIDE) for i in range(SIDE)])]
    pallas_call x1, Pallas kernels: 3.04 us -> 2.3 us  [fetch(): pl.pallas_call(fetch_kernel, out_shape=[pltpu.VMEM(a.shape, a.dtype) for...]
    ppermute x4 -> x3, waiting for transfers between devices: 3.23 us -> 3.62 us  [swap(): return lax.ppermute(block, 'c', SWAP)]
  transfers between devices with their start and end apart: 7 -> 6, of which waited for: 5 -> 4; matrix products, arithmetic and copies ran while one was open for 0% -> 0% of each run, Pallas kernels for 8% -> 7%
where the time goes in v5:
time: 72.9 us; the launch traced here: 72.5 us
  blocking collectives  49 us (67%)
  Pallas kernels  12.1 us (17%)
  starting transfers between devices  5.72 us (8%)
  waiting for transfers between devices  5.53 us (8%)
    all_to_all x2, blocking collectives, exchange(): lax.all_to_all(blocks, axes, split_axis=0, concat_axis=0, axis_index_grou...  49 us
    ppermute x3, starting transfers between devices, spread_z(): lax.ppermute(block, 'z', [(i, (i + k) % SIDE) for i in range(SIDE)])  5.45 us
    ppermute x3, waiting for transfers between devices, swap(): return lax.ppermute(block, 'c', SWAP)  3.62 us
    pallas_call x1, Pallas kernels, make_hidden(): pl.pallas_call(hidden_kernel, out_shape=[jax.ShapeDtypeStruct((rows, widt...  2.86 us
    pallas_call x1, Pallas kernels, fetch(): pl.pallas_call(fetch_kernel, out_shape=[pltpu.VMEM(a.shape, a.dtype) for...  2.3 us
    pallas_call x1, Pallas kernels, attention(): pl.pallas_call(attention_kernel, out_shape=jax.ShapeDtypeStruct((rows, wi...  2.11 us
    ppermute x3, waiting for transfers between devices, spread_z(): lax.ppermute(block, 'z', [(i, (i + k) % SIDE) for i in range(SIDE)])  1.91 us
    pallas_call x1, Pallas kernels, own_part(): pl.pallas_call(own_kernel, out_shape=[jax.ShapeDtypeStruct((rows, width),...  1.89 us
  transfers between devices with their start and end apart: 6, of which 4 were waited for; matrix products, arithmetic and copies ran while one was open for 0% of the time, Pallas kernels for 7%

profile of v5, /device:TPU:0, one launch (start us, length us, event | category | flops | bytes accessed | tf_op | source)
XLA Modules:
  0.0 72.5 jit_solution(16952399773038073588)
XLA Ops:
  0.0 2.1 %attention.1.a_ref = bf16[2,4096]{1,0:T(2,128)(2,1)S(1)} custom-call(s32[2]{0:T(128)} %len_hbm.1, bf16[2,4096]{1,0:T(2,128)(2,1)} %q_hbm.1, bf16[2,1024,256]{2,1,0:T(8,128)(2,1)} %k_hbm.1, bf16[2,1024,256]{2,1,0:T(8,128)(2,1)} %v_hbm.1), custom_call_target="tpu_custom_call" | custom-call | tf_op jit(solution)/shard_map/attention/pallas_call | solution.py:121
  2.1 0.1 collective-permute-start
  2.2 1.2 %collective-permute-done.b_ref = bf16[2,4096]{1,0:T(2,128)(2,1)S(1)} collective-permute-done((bf16[2,4096]{1,0:T(2,128)(2,1)S(1)}, bf16[2,4096]{1,0:T(2,128)(2,1)S(1)}, u32[]{:S(2)}, u32[]{:S(2)}) %collective-permute-start) | collective-permute-done | bytes 16416 | tf_op jit(solution)/shard_map/ppermute | solution.py:53
  3.4 4.2 %collective-permute-start.3 = (bf16[4,4096]{1,0:T(4,128)(2,1)S(1)}, bf16[4,4096]{1,0:T(4,128)(2,1)S(1)}, u32[]{:S(2)}, u32[]{:S(2)}) collective-permute-start(bf16[4,4096]{1,0:T(4,128)(2,1)S(1)} %join.1.refs_0_.a0), channel_id=1, source_target_pairs={{0,6},{2,0},{4,2},{6,4},{1,7},{3,1},{5,3},{7,5},{8,14},{10,8},{12,... | collective-permute-start | bytes 98312 | tf_op jit(solution)/shard_map/ppermute | solution.py:58
  7.6 0.0 collective-permute-start.2
  7.6 1.3 %collective-permute-start.1 = (bf16[4,4096]{1,0:T(4,128)(2,1)S(1)}, bf16[4,4096]{1,0:T(4,128)(2,1)S(1)}, u32[]{:S(2)}, u32[]{:S(2)}) collective-permute-start(bf16[4,4096]{1,0:T(4,128)(2,1)S(1)} %join.1.refs_0_.a0), channel_id=1, source_target_pairs={{0,2},{2,4},{4,6},{6,0},{1,3},{3,5},{5,7},{7,1},{8,10},{10,12},{12... | collective-permute-start | bytes 98312 | tf_op jit(solution)/shard_map/ppermute | solution.py:58
  8.8 2.3 %fetch.1 = (bf16[16,512]{1,0:T(8,128)(2,1)S(1)}, f32[1,512]{1,0:T(1,128)S(1)}, s32[8,16]{1,0:T(8,128)S(1)}, f32[8,16]{1,0:T(8,128)S(1)}, bf16[4096,512]{1,0:T(8,128)(2,1)S(1)}) custom-call(bf16[4,4096]{1,0:T(4,128)(2,1)S(1)} %join.1.refs_0_.a0, bf16[16,512]{1,0:T(8,128)(2,1)} %refs_1_.1, f32[1,512]{1,0:T(1,128)} %bitcast.25, s32[8,16]{1,0:T(8,128)} %bitcast.23, ...), custom_call_target="tpu_custom_call" | custom-call | bytes 4213760 | tf_op jit(solution)/shard_map/fetch/pallas_call | solution.py:175
  11.1 0.0 collective-permute-done.3.a3
  11.2 1.9 %collective-permute-done.2.a2 = bf16[4,4096]{1,0:T(4,128)(2,1)S(1)} collective-permute-done((bf16[4,4096]{1,0:T(4,128)(2,1)S(1)}, bf16[4,4096]{1,0:T(4,128)(2,1)S(1)}, u32[]{:S(2)}, u32[]{:S(2)}) %collective-permute-start.2) | collective-permute-done | bytes 32800 | tf_op jit(solution)/shard_map/ppermute | solution.py:58
  13.0 0.0 collective-permute-done.1.a1
  13.1 0.0 slice-start
  13.1 0.0 slice-start.2
  13.1 0.0 slice-start.4
  13.1 0.0 slice-start.1
  13.1 0.0 slice-start.3
  13.1 0.0 slice-start.5
  13.1 1.0 %stream.1 = (bf16[16,512]{1,0:T(8,128)(2,1)S(1)}, bf16[64,72,128]{2,1,0:T(8,128)(2,1)S(1)}) custom-call(bf16[4,4096]{1,0:T(4,128)(2,1)S(1)} %join.1.refs_0_.a0, bf16[4,4096]{1,0:T(4,128)(2,1)S(1)} %collective-permute-done.1.a1, bf16[4,4096]{1,0:T(4,128)(2,1)S(1)} %collective-permute-done.2.a2, bf16[4,4096]{1,0:T(4,128)(2,1)S(1)} %collective-permute-done.3.a3, ...), custom_call_target="tpu_custom_call" | custom-call | flops 10000000000 | bytes 60000000 | tf_op jit(solution)/shard_map/stream/pallas_call | solution.py:236
  14.1 26.2 %all_to_all.10.own_ref = bf16[64,72,128]{2,1,0:T(8,128)(2,1)S(1)} all-to-all(bf16[64,72,128]{2,1,0:T(8,128)(2,1)S(1)} %get-tuple-element.23), channel_id=1, replica_groups={{44,24,104,6,38,10,120,116,4,66,20,16,58,52,50,18,88,36,124,22,94,80,30..., dimensions={0} | all-to-all | bytes 2359296 | tf_op jit(solution)/shard_map/all_to_all | solution.py:439
  40.2 0.0 collective-permute-start.4
  40.2 0.0 slice-done
  40.2 0.0 slice-done.2
  40.2 0.0 slice-done.4
  40.3 0.0 slice-done.1
  40.3 0.0 slice-done.3
  40.3 0.0 slice-done.5
  40.3 1.9 %own_part.1 = (f32[256,768]{1,0:T(8,128)S(1)}, f32[256,768]{1,0:T(8,128)S(1)}, f32[256,768]{1,0:T(8,128)S(1)}, f32[16,1,128]{2,1,0:T(1,128)S(1)}) custom-call(bf16[64,72,128]{2,1,0:T(8,128)(2,1)S(1)} %all_to_all.10.own_ref, bf16[768,4096]{1,0:T(8,128)(2,1)S(1)} %bitcast.17, bf16[768,4096]{1,0:T(8,128)(2,1)S(1)} %bitcast.21, bf16[768,4096]{1,0:T(8,128)(2,1)S(1)} %bitcast.12), custom_call_target="tpu_custom_call" | custom-call | tf_op jit(solution)/shard_map/own_part/pallas_call | solution.py:322
  42.2 0.9 %collective-permute-done.4.other_ref = bf16[64,72,128]{2,1,0:T(8,128)(2,1)S(1)} collective-permute-done((bf16[64,72,128]{2,1,0:T(8,128)(2,1)S(1)}, bf16[64,72,128]{2,1,0:T(8,128)(2,1)S(1)}, u32[]{:S(2)}, u32[]{:S(2)}) %collective-permute-start.4) | collective-permute-done | bytes 1179680 | tf_op jit(solution)/shard_map/ppermute | solution.py:53
  43.1 2.9 %hidden.1 = (bf16[256,768]{1,0:T(8,128)(2,1)S(1)}, bf16[16,4,16,512]{3,2,1,0:T(8,128)(2,1)S(1)}) custom-call(bf16[64,72,128]{2,1,0:T(8,128)(2,1)S(1)} %collective-permute-done.4.other_ref, bf16[768,4096]{1,0:T(8,128)(2,1)S(1)} %bitcast.18, bf16[768,4096]{1,0:T(8,128)(2,1)S(1)} %bitcast.22, f32[256,768]{1,0:T(8,128)S(1)} %get-tuple-element.24.gate_in, ...), custom_call_target="tpu_custom_call" | custom-call | tf_op jit(solution)/shard_map/hidden/pallas_call | solution.py:371
  45.9 0.2 collective-permute-start.5
  46.1 1.0 %down_mine.1.mine_ref = bf16[16,4,16,512]{3,2,1,0:T(8,128)(2,1)S(1)} custom-call(bf16[256,768]{1,0:T(8,128)(2,1)S(1)} %get-tuple-element.28.hidden_ref, bf16[768,4096]{1,0:T(8,128)(2,1)S(1)} %bitcast.14), custom_call_target="tpu_custom_call" | custom-call | tf_op jit(solution)/shard_map/down_mine/pallas_call | solution.py:387
  47.1 1.6 %collective-permute-done.5.came_ref = bf16[16,4,16,512]{3,2,1,0:T(8,128)(2,1)S(1)} collective-permute-done((bf16[16,4,16,512]{3,2,1,0:T(8,128)(2,1)S(1)}, bf16[16,4,16,512]{3,2,1,0:T(8,128)(2,1)S(1)}, u32[]{:S(2)}, u32[]{:S(2)}) %collective-permute-start.5) | collective-permute-done | bytes 1048608 | tf_op jit(solution)/shard_map/ppermute | solution.py:53
  48.7 0.2 add.1
  48.9 22.8 %all_to_all.11.parts_ref = bf16[64,16,512]{2,1,0:T(8,128)(2,1)S(1)} all-to-all(bf16[64,16,512]{2,1,0:T(8,128)(2,1)S(1)} %add.1), channel_id=1, replica_groups={{44,24,104,6,38,10,120,116,4,66,20,16,58,52,50,18,88,36,124,22,94,80,30..., dimensions={0} | all-to-all | bytes 2097152 | tf_op jit(solution)/shard_map/all_to_all | solution.py:439
  71.7 0.8 %finish.1 = bf16[16,512]{1,0:T(8,128)(2,1)} custom-call(bf16[64,16,512]{2,1,0:T(8,128)(2,1)S(1)} %all_to_all.11.parts_ref, bf16[16,512]{1,0:T(8,128)(2,1)S(1)} %get-tuple-element.30.stream_ref), custom_call_target="tpu_custom_call" | custom-call | tf_op jit(solution)/shard_map/finish/pallas_call | solution.py:426
  (4 shorter events, 0.0 us)
Async XLA Ops:
  2.1 1.3 %collective-permute-start = (bf16[2,4096]{1,0:T(2,128)(2,1)S(1)}, bf16[2,4096]{1,0:T(2,128)(2,1)S(1)}, u32[]{:S(2)}, u32[]{:S(2)}) collective-permute-start(bf16[2,4096]{1,0:T(2,128)(2,1)S(1)} %attention.1.a_ref), channel_id=1, source_target_pairs={{0,1},{1,0},{2,3},{3,2},{4,5},{5,4},{6,7},{7,6},{8,9},{9,8},{10,11... | collective-permute-start | bytes 49160 | tf_op jit(solution)/shard_map/ppermute | solution.py:53
  3.4 7.8 %collective-permute-start.3 = (bf16[4,4096]{1,0:T(4,128)(2,1)S(1)}, bf16[4,4096]{1,0:T(4,128)(2,1)S(1)}, u32[]{:S(2)}, u32[]{:S(2)}) collective-permute-start(bf16[4,4096]{1,0:T(4,128)(2,1)S(1)} %join.1.refs_0_.a0), channel_id=1, source_target_pairs={{0,6},{2,0},{4,2},{6,4},{1,7},{3,1},{5,3},{7,5},{8,14},{10,8},{12,... | collective-permute-start | bytes 98312 | tf_op jit(solution)/shard_map/ppermute | solution.py:58
  7.6 5.5 %collective-permute-start.2 = (bf16[4,4096]{1,0:T(4,128)(2,1)S(1)}, bf16[4,4096]{1,0:T(4,128)(2,1)S(1)}, u32[]{:S(2)}, u32[]{:S(2)}) collective-permute-start(bf16[4,4096]{1,0:T(4,128)(2,1)S(1)} %join.1.refs_0_.a0), channel_id=1, source_target_pairs={{0,4},{2,6},{4,0},{6,2},{1,5},{3,7},{5,1},{7,3},{8,12},{10,14},{12... | collective-permute-start | bytes 98312 | tf_op jit(solution)/shard_map/ppermute | solution.py:58
  7.6 5.5 %collective-permute-start.1 = (bf16[4,4096]{1,0:T(4,128)(2,1)S(1)}, bf16[4,4096]{1,0:T(4,128)(2,1)S(1)}, u32[]{:S(2)}, u32[]{:S(2)}) collective-permute-start(bf16[4,4096]{1,0:T(4,128)(2,1)S(1)} %join.1.refs_0_.a0), channel_id=1, source_target_pairs={{0,2},{2,4},{4,6},{6,0},{1,3},{3,5},{5,7},{7,1},{8,10},{10,12},{12... | collective-permute-start | bytes 98312 | tf_op jit(solution)/shard_map/ppermute | solution.py:58
  13.1 27.2 %slice-start = ((s8[6291456]{0:T(1024)(128)(4,1)}), s8[4194304]{0:T(1024)(128)(4,1)S(1)}, s32[]{:S(2)}) async-start(s8[6291456]{0:T(1024)(128)(4,1)} %bitcast.10), calls=%async_computation.2 | async-start | bytes 8388608
  13.1 27.2 %slice-start.2 = ((s8[6291456]{0:T(1024)(128)(4,1)}), s8[4194304]{0:T(1024)(128)(4,1)S(1)}, s32[]{:S(2)}) async-start(s8[6291456]{0:T(1024)(128)(4,1)} %bitcast.15), calls=%async_computation.4 | async-start | bytes 8388608
  13.1 27.2 %slice-start.4 = ((s8[6291456]{0:T(1024)(128)(4,1)}), s8[4194304]{0:T(1024)(128)(4,1)S(1)}, s32[]{:S(2)}) async-start(s8[6291456]{0:T(1024)(128)(4,1)} %bitcast.19), calls=%async_computation.6 | async-start | bytes 8388608
  13.1 27.2 %slice-start.1 = ((s8[6291456]{0:T(1024)(128)(4,1)}), s8[2097152]{0:T(1024)(128)(4,1)S(1)}, s32[]{:S(2)}) async-start(s8[6291456]{0:T(1024)(128)(4,1)} %bitcast.10), calls=%async_computation.3 | async-start | bytes 4194304
  13.1 27.2 %slice-start.3 = ((s8[6291456]{0:T(1024)(128)(4,1)}), s8[2097152]{0:T(1024)(128)(4,1)S(1)}, s32[]{:S(2)}) async-start(s8[6291456]{0:T(1024)(128)(4,1)} %bitcast.15), calls=%async_computation.5 | async-start | bytes 4194304
  13.1 27.2 %slice-start.5 = ((s8[6291456]{0:T(1024)(128)(4,1)}), s8[2097152]{0:T(1024)(128)(4,1)S(1)}, s32[]{:S(2)}) async-start(s8[6291456]{0:T(1024)(128)(4,1)} %bitcast.19), calls=%async_computation.7 | async-start | bytes 4194304
  40.2 2.8 %collective-permute-start.4 = (bf16[64,72,128]{2,1,0:T(8,128)(2,1)S(1)}, bf16[64,72,128]{2,1,0:T(8,128)(2,1)S(1)}, u32[]{:S(2)}, u32[]{:S(2)}) collective-permute-start(bf16[64,72,128]{2,1,0:T(8,128)(2,1)S(1)} %all_to_all.10.own_ref), channel_id=1, source_target_pairs={{0,1},{1,0},{2,3},{3,2},{4,5},{5,4},{6,7},{7,6},{8,9},{9,8},{10,11... | collective-permute-start | bytes 3538952 | tf_op jit(solution)/shard_map/ppermute | solution.py:53
  45.9 2.7 %collective-permute-start.5 = (bf16[16,4,16,512]{3,2,1,0:T(8,128)(2,1)S(1)}, bf16[16,4,16,512]{3,2,1,0:T(8,128)(2,1)S(1)}, u32[]{:S(2)}, u32[]{:S(2)}) collective-permute-start(bf16[16,4,16,512]{3,2,1,0:T(8,128)(2,1)S(1)} %get-tuple-element.29), channel_id=1, source_target_pairs={{0,1},{1,0},{2,3},{3,2},{4,5},{5,4},{6,7},{7,6},{8,9},{9,8},{10,11... | collective-permute-start | bytes 3145736 | tf_op jit(solution)/shard_map/ppermute | solution.py:53

commit v6 on v5

--- a/solution.py
+++ b/solution.py
@@ -25,7 +25,7 @@
 IDS, HI, MID, LO, SQ = 0, ROWS, 2 * ROWS, 3 * ROWS, 4 * ROWS
 EXPERT_COLS = 192
 ORDER = list(range(PLACES * SIDE))
-random.Random(1).shuffle(ORDER)
+random.Random(13).shuffle(ORDER)
 RANK = [ORDER.index(place) for place in range(PLACES * SIDE)]
 GROUPS = [[place * CORES + c for place in ORDER] for c in range(CORES)]
 F32 = jnp.float32

time: 72.9 us -> 72.5 us (level)
  no operation moved by 1% of the time
where the time goes in v6:
time: 72.5 us; the launch traced here: 71.8 us
  blocking collectives  48.3 us (67%)
  Pallas kernels  12.1 us (17%)
  starting transfers between devices  5.73 us (8%)
  waiting for transfers between devices  5.52 us (8%)
    all_to_all x2, blocking collectives, exchange(): lax.all_to_all(blocks, axes, split_axis=0, concat_axis=0, axis_index_grou...  48.3 us
    ppermute x3, starting transfers between devices, spread_z(): lax.ppermute(block, 'z', [(i, (i + k) % SIDE) for i in range(SIDE)])  5.45 us
    ppermute x3, waiting for transfers between devices, swap(): return lax.ppermute(block, 'c', SWAP)  3.61 us
    pallas_call x1, Pallas kernels, make_hidden(): pl.pallas_call(hidden_kernel, out_shape=[jax.ShapeDtypeStruct((rows, widt...  2.85 us
    pallas_call x1, Pallas kernels, fetch(): pl.pallas_call(fetch_kernel, out_shape=[pltpu.VMEM(a.shape, a.dtype) for...  2.3 us
    pallas_call x1, Pallas kernels, attention(): pl.pallas_call(attention_kernel, out_shape=jax.ShapeDtypeStruct((rows, wi...  2.11 us
    ppermute x3, waiting for transfers between devices, spread_z(): lax.ppermute(block, 'z', [(i, (i + k) % SIDE) for i in range(SIDE)])  1.91 us
    pallas_call x1, Pallas kernels, own_part(): pl.pallas_call(own_kernel, out_shape=[jax.ShapeDtypeStruct((rows, width),...  1.89 us
  transfers between devices with their start and end apart: 6, of which 4 were waited for; matrix products, arithmetic and copies ran while one was open for 0% of the time, Pallas kernels for 7%

profile of v6, /device:TPU:0, one launch (start us, length us, event | category | flops | bytes accessed | tf_op | source)
XLA Modules:
  0.0 71.8 jit_solution(10141822202308193586)
XLA Ops:
  0.0 2.1 %attention.1.a_ref = bf16[2,4096]{1,0:T(2,128)(2,1)S(1)} custom-call(s32[2]{0:T(128)} %len_hbm.1, bf16[2,4096]{1,0:T(2,128)(2,1)} %q_hbm.1, bf16[2,1024,256]{2,1,0:T(8,128)(2,1)} %k_hbm.1, bf16[2,1024,256]{2,1,0:T(8,128)(2,1)} %v_hbm.1), custom_call_target="tpu_custom_call" | custom-call | tf_op jit(solution)/shard_map/attention/pallas_call | solution.py:121
  2.1 0.1 collective-permute-start
  2.2 1.2 %collective-permute-done.b_ref = bf16[2,4096]{1,0:T(2,128)(2,1)S(1)} collective-permute-done((bf16[2,4096]{1,0:T(2,128)(2,1)S(1)}, bf16[2,4096]{1,0:T(2,128)(2,1)S(1)}, u32[]{:S(2)}, u32[]{:S(2)}) %collective-permute-start) | collective-permute-done | bytes 16416 | tf_op jit(solution)/shard_map/ppermute | solution.py:53
  3.4 4.2 %collective-permute-start.3 = (bf16[4,4096]{1,0:T(4,128)(2,1)S(1)}, bf16[4,4096]{1,0:T(4,128)(2,1)S(1)}, u32[]{:S(2)}, u32[]{:S(2)}) collective-permute-start(bf16[4,4096]{1,0:T(4,128)(2,1)S(1)} %join.1.refs_0_.a0), channel_id=1, source_target_pairs={{0,6},{2,0},{4,2},{6,4},{1,7},{3,1},{5,3},{7,5},{8,14},{10,8},{12,... | collective-permute-start | bytes 98312 | tf_op jit(solution)/shard_map/ppermute | solution.py:58
  7.6 0.0 collective-permute-start.2
  7.6 1.3 %collective-permute-start.1 = (bf16[4,4096]{1,0:T(4,128)(2,1)S(1)}, bf16[4,4096]{1,0:T(4,128)(2,1)S(1)}, u32[]{:S(2)}, u32[]{:S(2)}) collective-permute-start(bf16[4,4096]{1,0:T(4,128)(2,1)S(1)} %join.1.refs_0_.a0), channel_id=1, source_target_pairs={{0,2},{2,4},{4,6},{6,0},{1,3},{3,5},{5,7},{7,1},{8,10},{10,12},{12... | collective-permute-start | bytes 98312 | tf_op jit(solution)/shard_map/ppermute | solution.py:58
  8.8 2.3 %fetch.1 = (bf16[16,512]{1,0:T(8,128)(2,1)S(1)}, f32[1,512]{1,0:T(1,128)S(1)}, s32[8,16]{1,0:T(8,128)S(1)}, f32[8,16]{1,0:T(8,128)S(1)}, bf16[4096,512]{1,0:T(8,128)(2,1)S(1)}) custom-call(bf16[4,4096]{1,0:T(4,128)(2,1)S(1)} %join.1.refs_0_.a0, bf16[16,512]{1,0:T(8,128)(2,1)} %refs_1_.1, f32[1,512]{1,0:T(1,128)} %bitcast.25, s32[8,16]{1,0:T(8,128)} %bitcast.23, ...), custom_call_target="tpu_custom_call" | custom-call | bytes 4213760 | tf_op jit(solution)/shard_map/fetch/pallas_call | solution.py:175
  11.1 0.0 collective-permute-done.3.a3
  11.2 1.9 %collective-permute-done.2.a2 = bf16[4,4096]{1,0:T(4,128)(2,1)S(1)} collective-permute-done((bf16[4,4096]{1,0:T(4,128)(2,1)S(1)}, bf16[4,4096]{1,0:T(4,128)(2,1)S(1)}, u32[]{:S(2)}, u32[]{:S(2)}) %collective-permute-start.2) | collective-permute-done | bytes 32800 | tf_op jit(solution)/shard_map/ppermute | solution.py:58
  13.0 0.0 collective-permute-done.1.a1
  13.1 0.0 slice-start
  13.1 0.0 slice-start.2
  13.1 0.0 slice-start.4
  13.1 0.0 slice-start.1
  13.1 0.0 slice-start.3
  13.1 0.0 slice-start.5
  13.1 1.0 %stream.1 = (bf16[16,512]{1,0:T(8,128)(2,1)S(1)}, bf16[64,72,128]{2,1,0:T(8,128)(2,1)S(1)}) custom-call(bf16[4,4096]{1,0:T(4,128)(2,1)S(1)} %join.1.refs_0_.a0, bf16[4,4096]{1,0:T(4,128)(2,1)S(1)} %collective-permute-done.1.a1, bf16[4,4096]{1,0:T(4,128)(2,1)S(1)} %collective-permute-done.2.a2, bf16[4,4096]{1,0:T(4,128)(2,1)S(1)} %collective-permute-done.3.a3, ...), custom_call_target="tpu_custom_call" | custom-call | flops 10000000000 | bytes 60000000 | tf_op jit(solution)/shard_map/stream/pallas_call | solution.py:236
  14.1 25.3 %all_to_all.10.own_ref = bf16[64,72,128]{2,1,0:T(8,128)(2,1)S(1)} all-to-all(bf16[64,72,128]{2,1,0:T(8,128)(2,1)S(1)} %get-tuple-element.23), channel_id=1, replica_groups={{74,46,58,12,88,98,24,44,100,38,4,70,48,64,126,62,40,6,20,42,52,118,104..., dimensions={0} | all-to-all | bytes 2359296 | tf_op jit(solution)/shard_map/all_to_all | solution.py:439
  39.3 0.0 collective-permute-start.4
  39.3 0.0 slice-done
  39.3 0.0 slice-done.2
  39.4 0.0 slice-done.4
  39.4 0.0 slice-done.1
  39.4 0.0 slice-done.3
  39.4 0.0 slice-done.5
  39.4 1.9 %own_part.1 = (f32[256,768]{1,0:T(8,128)S(1)}, f32[256,768]{1,0:T(8,128)S(1)}, f32[256,768]{1,0:T(8,128)S(1)}, f32[16,1,128]{2,1,0:T(1,128)S(1)}) custom-call(bf16[64,72,128]{2,1,0:T(8,128)(2,1)S(1)} %all_to_all.10.own_ref, bf16[768,4096]{1,0:T(8,128)(2,1)S(1)} %bitcast.17, bf16[768,4096]{1,0:T(8,128)(2,1)S(1)} %bitcast.21, bf16[768,4096]{1,0:T(8,128)(2,1)S(1)} %bitcast.12), custom_call_target="tpu_custom_call" | custom-call | tf_op jit(solution)/shard_map/own_part/pallas_call | solution.py:322
  41.3 0.9 %collective-permute-done.4.other_ref = bf16[64,72,128]{2,1,0:T(8,128)(2,1)S(1)} collective-permute-done((bf16[64,72,128]{2,1,0:T(8,128)(2,1)S(1)}, bf16[64,72,128]{2,1,0:T(8,128)(2,1)S(1)}, u32[]{:S(2)}, u32[]{:S(2)}) %collective-permute-start.4) | collective-permute-done | bytes 1179680 | tf_op jit(solution)/shard_map/ppermute | solution.py:53
  42.2 2.8 %hidden.1 = (bf16[256,768]{1,0:T(8,128)(2,1)S(1)}, bf16[16,4,16,512]{3,2,1,0:T(8,128)(2,1)S(1)}) custom-call(bf16[64,72,128]{2,1,0:T(8,128)(2,1)S(1)} %collective-permute-done.4.other_ref, bf16[768,4096]{1,0:T(8,128)(2,1)S(1)} %bitcast.18, bf16[768,4096]{1,0:T(8,128)(2,1)S(1)} %bitcast.22, f32[256,768]{1,0:T(8,128)S(1)} %get-tuple-element.24.gate_in, ...), custom_call_target="tpu_custom_call" | custom-call | tf_op jit(solution)/shard_map/hidden/pallas_call | solution.py:371
  45.0 0.2 collective-permute-start.5
  45.2 1.0 %down_mine.1.mine_ref = bf16[16,4,16,512]{3,2,1,0:T(8,128)(2,1)S(1)} custom-call(bf16[256,768]{1,0:T(8,128)(2,1)S(1)} %get-tuple-element.28.hidden_ref, bf16[768,4096]{1,0:T(8,128)(2,1)S(1)} %bitcast.14), custom_call_target="tpu_custom_call" | custom-call | tf_op jit(solution)/shard_map/down_mine/pallas_call | solution.py:387
  46.2 1.6 %collective-permute-done.5.came_ref = bf16[16,4,16,512]{3,2,1,0:T(8,128)(2,1)S(1)} collective-permute-done((bf16[16,4,16,512]{3,2,1,0:T(8,128)(2,1)S(1)}, bf16[16,4,16,512]{3,2,1,0:T(8,128)(2,1)S(1)}, u32[]{:S(2)}, u32[]{:S(2)}) %collective-permute-start.5) | collective-permute-done | bytes 1048608 | tf_op jit(solution)/shard_map/ppermute | solution.py:53
  47.8 0.2 add.1
  48.0 23.0 %all_to_all.11.parts_ref = bf16[64,16,512]{2,1,0:T(8,128)(2,1)S(1)} all-to-all(bf16[64,16,512]{2,1,0:T(8,128)(2,1)S(1)} %add.1), channel_id=1, replica_groups={{74,46,58,12,88,98,24,44,100,38,4,70,48,64,126,62,40,6,20,42,52,118,104..., dimensions={0} | all-to-all | bytes 2097152 | tf_op jit(solution)/shard_map/all_to_all | solution.py:439
  71.1 0.8 %finish.1 = bf16[16,512]{1,0:T(8,128)(2,1)} custom-call(bf16[64,16,512]{2,1,0:T(8,128)(2,1)S(1)} %all_to_all.11.parts_ref, bf16[16,512]{1,0:T(8,128)(2,1)S(1)} %get-tuple-element.30.stream_ref), custom_call_target="tpu_custom_call" | custom-call | tf_op jit(solution)/shard_map/finish/pallas_call | solution.py:426
  (4 shorter events, 0.0 us)
Async XLA Ops:
  2.1 1.3 %collective-permute-start = (bf16[2,4096]{1,0:T(2,128)(2,1)S(1)}, bf16[2,4096]{1,0:T(2,128)(2,1)S(1)}, u32[]{:S(2)}, u32[]{:S(2)}) collective-permute-start(bf16[2,4096]{1,0:T(2,128)(2,1)S(1)} %attention.1.a_ref), channel_id=1, source_target_pairs={{0,1},{1,0},{2,3},{3,2},{4,5},{5,4},{6,7},{7,6},{8,9},{9,8},{10,11... | collective-permute-start | bytes 49160 | tf_op jit(solution)/shard_map/ppermute | solution.py:53
  3.4 7.8 %collective-permute-start.3 = (bf16[4,4096]{1,0:T(4,128)(2,1)S(1)}, bf16[4,4096]{1,0:T(4,128)(2,1)S(1)}, u32[]{:S(2)}, u32[]{:S(2)}) collective-permute-start(bf16[4,4096]{1,0:T(4,128)(2,1)S(1)} %join.1.refs_0_.a0), channel_id=1, source_target_pairs={{0,6},{2,0},{4,2},{6,4},{1,7},{3,1},{5,3},{7,5},{8,14},{10,8},{12,... | collective-permute-start | bytes 98312 | tf_op jit(solution)/shard_map/ppermute | solution.py:58
  7.6 5.5 %collective-permute-start.2 = (bf16[4,4096]{1,0:T(4,128)(2,1)S(1)}, bf16[4,4096]{1,0:T(4,128)(2,1)S(1)}, u32[]{:S(2)}, u32[]{:S(2)}) collective-permute-start(bf16[4,4096]{1,0:T(4,128)(2,1)S(1)} %join.1.refs_0_.a0), channel_id=1, source_target_pairs={{0,4},{2,6},{4,0},{6,2},{1,5},{3,7},{5,1},{7,3},{8,12},{10,14},{12... | collective-permute-start | bytes 98312 | tf_op jit(solution)/shard_map/ppermute | solution.py:58
  7.6 5.5 %collective-permute-start.1 = (bf16[4,4096]{1,0:T(4,128)(2,1)S(1)}, bf16[4,4096]{1,0:T(4,128)(2,1)S(1)}, u32[]{:S(2)}, u32[]{:S(2)}) collective-permute-start(bf16[4,4096]{1,0:T(4,128)(2,1)S(1)} %join.1.refs_0_.a0), channel_id=1, source_target_pairs={{0,2},{2,4},{4,6},{6,0},{1,3},{3,5},{5,7},{7,1},{8,10},{10,12},{12... | collective-permute-start | bytes 98312 | tf_op jit(solution)/shard_map/ppermute | solution.py:58
  13.1 26.3 %slice-start = ((s8[6291456]{0:T(1024)(128)(4,1)}), s8[4194304]{0:T(1024)(128)(4,1)S(1)}, s32[]{:S(2)}) async-start(s8[6291456]{0:T(1024)(128)(4,1)} %bitcast.10), calls=%async_computation.2 | async-start | bytes 8388608
  13.1 26.3 %slice-start.2 = ((s8[6291456]{0:T(1024)(128)(4,1)}), s8[4194304]{0:T(1024)(128)(4,1)S(1)}, s32[]{:S(2)}) async-start(s8[6291456]{0:T(1024)(128)(4,1)} %bitcast.15), calls=%async_computation.4 | async-start | bytes 8388608
  13.1 26.3 %slice-start.4 = ((s8[6291456]{0:T(1024)(128)(4,1)}), s8[4194304]{0:T(1024)(128)(4,1)S(1)}, s32[]{:S(2)}) async-start(s8[6291456]{0:T(1024)(128)(4,1)} %bitcast.19), calls=%async_computation.6 | async-start | bytes 8388608
  13.1 26.3 %slice-start.1 = ((s8[6291456]{0:T(1024)(128)(4,1)}), s8[2097152]{0:T(1024)(128)(4,1)S(1)}, s32[]{:S(2)}) async-start(s8[6291456]{0:T(1024)(128)(4,1)} %bitcast.10), calls=%async_computation.3 | async-start | bytes 4194304
  13.1 26.3 %slice-start.3 = ((s8[6291456]{0:T(1024)(128)(4,1)}), s8[2097152]{0:T(1024)(128)(4,1)S(1)}, s32[]{:S(2)}) async-start(s8[6291456]{0:T(1024)(128)(4,1)} %bitcast.15), calls=%async_computation.5 | async-start | bytes 4194304
  13.1 26.3 %slice-start.5 = ((s8[6291456]{0:T(1024)(128)(4,1)}), s8[2097152]{0:T(1024)(128)(4,1)S(1)}, s32[]{:S(2)}) async-start(s8[6291456]{0:T(1024)(128)(4,1)} %bitcast.19), calls=%async_computation.7 | async-start | bytes 4194304
  39.3 2.8 %collective-permute-start.4 = (bf16[64,72,128]{2,1,0:T(8,128)(2,1)S(1)}, bf16[64,72,128]{2,1,0:T(8,128)(2,1)S(1)}, u32[]{:S(2)}, u32[]{:S(2)}) collective-permute-start(bf16[64,72,128]{2,1,0:T(8,128)(2,1)S(1)} %all_to_all.10.own_ref), channel_id=1, source_target_pairs={{0,1},{1,0},{2,3},{3,2},{4,5},{5,4},{6,7},{7,6},{8,9},{9,8},{10,11... | collective-permute-start | bytes 3538952 | tf_op jit(solution)/shard_map/ppermute | solution.py:53
  45.0 2.7 %collective-permute-start.5 = (bf16[16,4,16,512]{3,2,1,0:T(8,128)(2,1)S(1)}, bf16[16,4,16,512]{3,2,1,0:T(8,128)(2,1)S(1)}, u32[]{:S(2)}, u32[]{:S(2)}) collective-permute-start(bf16[16,4,16,512]{3,2,1,0:T(8,128)(2,1)S(1)} %get-tuple-element.29), channel_id=1, source_target_pairs={{0,1},{1,0},{2,3},{3,2},{4,5},{5,4},{6,7},{7,6},{8,9},{9,8},{10,11... | collective-permute-start | bytes 3145736 | tf_op jit(solution)/shard_map/ppermute | solution.py:53
